TPU v7x, 32 devices: a whole 2x2x4 slice. The times are simulated.
32 devices in a mesh: groups: 2 (over y), cells: 8 (over z, x), freq: 2 (over core).
Axes of the slice: x: 2, y: 2, z: 4, core: 2. Of those that a mesh axis runs over, the one named last changes fastest.
Arguments:
- adjoint: float32 [2, 256], P(None, ('groups', 'cells')), parts along dimension 1, may hold values from -6 to 6
- target_x: float32 [256], P(('groups', 'cells')), parts along dimension 0, may hold values from 0 to 1024
- target_y: float32 [256], P(('groups', 'cells')), parts along dimension 0, may hold values from 0 to 8
- target_z: float32 [256], P(('groups', 'cells')), parts along dimension 0, may hold values from 256 to 512
- assignment: int32 [256], P(('groups', 'cells')), parts along dimension 0, may hold values from 0 to 63
- level_codes: int32 [16384], P(('groups', 'cells', 'freq')), parts along dimension 0, may hold values from 0 to 15
- cell_params: bfloat16 [8, 16384], P(None, ('groups', 'cells', 'freq')), parts along dimension 1, may hold values from -5 to 5
- level_table: bfloat16 [16, 256], replicated, may hold values from -4 to 4
- w_proj: bfloat16 [8, 256], replicated, may hold values from -2 to 2
- w_one: bfloat16 [256, 256], replicated, may hold values from -0.375 to 0.375
- b_one: float32 [256], replicated, may hold values from -3 to 3
- w_two: bfloat16 [256, 256], replicated, may hold values from -0.375 to 0.375
- b_two: float32 [256], replicated, may hold values from -3 to 3
- w_out: bfloat16 [256, 128], replicated, may hold values from -0.375 to 0.375
Outputs:
- grad_out: float32 [512, 128], P('groups'), parts along dimension 0
- grad_w2: float32 [512, 256], P('groups'), parts along dimension 0
- grad_b2: float32 [512], P('groups'), parts along dimension 0
- grad_w1: float32 [512, 256], P('groups'), parts along dimension 0
- grad_b1: float32 [512], P('groups'), parts along dimension 0
- grad_table: float32 [32, 256], P('groups'), parts along dimension 0
- grad_proj: float32 [16, 256], P('groups'), parts along dimension 0
- grad_params: float32 [8, 16384], P(None, ('groups', 'cells', 'freq')), parts along dimension 1
There are 2 independent parts, one for each index of `groups`. A program takes and returns all parts, laid end to end along the dimension named above; an argument that names none is the same for every part. Nothing has to cross between parts.
All inputs are finite; a program needn't handle non-finite values.
Results may differ from a plain program's by a relative error of at most 0.01.
Values may be sent and summed in bfloat16 or wider, within the bound.
No kernel may reach another device: no remote copies, remote signals or barrier semaphores. Data moves between devices by JAX's collectives and lax.ppermute only.
A program may use at most 64 MiB of HBM per device.

v0:
```python
import math

import jax
import jax.numpy as jnp
from jax import lax
from jax.sharding import PartitionSpec as P

SIDE = 1024


wave_low = 1.0
wave_high = 3.0
kernel_gain = 150.0


def silu_slope(value):
    sigma = jax.nn.sigmoid(value)
    return sigma * (1.0 + value * (1.0 - sigma))


def contract(left, right, left_dim, right_dim):
    return lax.dot_general(
        left, right, (((left_dim,), (right_dim,)), ((), ())), preferred_element_type=jnp.float32
    )


def kernel_tile(point_x, point_y, point_z, freq_value, cell_col, cell_row, count_freq):
    wave = wave_low + (wave_high - wave_low) * freq_value / (count_freq - 1)
    offset_x = point_x[:, None] - cell_col[None, :]
    offset_y = point_y[:, None] - cell_row[None, :]
    square = offset_x * offset_x + offset_y * offset_y + (point_z * point_z)[:, None]
    distance = jnp.sqrt(square)
    amplitude = kernel_gain * point_z[:, None] / square
    phase = wave[:, None] * distance
    return (
        (amplitude * jnp.cos(phase)).astype(jnp.bfloat16),
        (amplitude * jnp.sin(phase)).astype(jnp.bfloat16),
    )


def forward_pass(level_codes, cell_params, level_table, w_proj, w_one, b_one, w_two, b_two):
    levels = level_table.shape[0]
    onehot = (level_codes[:, None] == jnp.arange(levels, dtype=jnp.int32)[None, :]).astype(
        jnp.bfloat16
    )
    hidden_in = (
        jnp.dot(onehot, level_table, preferred_element_type=jnp.float32)
        + contract(cell_params, w_proj, 0, 0)
    ).astype(jnp.bfloat16)
    pre_one = jnp.dot(hidden_in, w_one, preferred_element_type=jnp.float32) + b_one
    act_one = jax.nn.silu(pre_one).astype(jnp.bfloat16)
    pre_two = jnp.dot(act_one, w_two, preferred_element_type=jnp.float32) + b_two
    act_two = jax.nn.silu(pre_two).astype(jnp.bfloat16)
    return (onehot, hidden_in, pre_one, act_one, pre_two, act_two)


def upper_grads(spectra, w_out, act_one, pre_two, act_two):
    back_two = contract(spectra, w_out, 0, 1)
    delta_two = (back_two * silu_slope(pre_two)).astype(jnp.bfloat16)
    grad_out = contract(act_two, spectra, 0, 1)
    grad_w2 = contract(act_one, delta_two, 0, 0)
    grad_b2 = jnp.sum(delta_two.astype(jnp.float32), axis=0)
    return ((grad_out, grad_w2, grad_b2), delta_two)


def lower_grads(delta_two, w_two, w_one, pre_one, hidden_in, onehot, cell_params, w_proj):
    back_one = contract(delta_two, w_two, 1, 1)
    delta_one = (back_one * silu_slope(pre_one)).astype(jnp.bfloat16)
    grad_w1 = contract(hidden_in, delta_one, 0, 0)
    grad_b1 = jnp.sum(delta_one.astype(jnp.float32), axis=0)
    back_zero = contract(delta_one, w_one, 1, 1).astype(jnp.bfloat16)
    grad_table = contract(onehot, back_zero, 0, 0)
    grad_proj = contract(cell_params, back_zero, 1, 0)
    grad_params = contract(w_proj, back_zero, 1, 1)
    return ((grad_w1, grad_b1, grad_table, grad_proj), grad_params)


def body(
    adjoint,
    target_x,
    target_y,
    target_z,
    assignment,
    level_codes,
    cell_params,
    level_table,
    w_proj,
    w_one,
    b_one,
    w_two,
    b_two,
    w_out,
):
    cell_count = level_codes.shape[0]
    freq_count = w_out.shape[1] // 2
    freq_size = lax.axis_size("freq")
    cell_rank = lax.axis_index("cells")
    freq_rank = lax.axis_index("freq")
    first_cell = (cell_rank * freq_size + freq_rank) * cell_count
    index = first_cell + jnp.arange(cell_count, dtype=jnp.int32)
    cell_col = (index % SIDE).astype(jnp.float32)
    cell_row = (index // SIDE).astype(jnp.float32)
    freq_grid = jnp.arange(freq_count, dtype=jnp.int32).astype(jnp.float32)
    stacked = jnp.concatenate(
        [
            adjoint,
            target_x[None, :],
            target_y[None, :],
            target_z[None, :],
            assignment.astype(jnp.float32)[None, :],
        ],
        axis=0,
    )
    initial = jnp.zeros((2 * freq_count, cell_count), jnp.float32)
    total = initial
    piece = lax.all_gather(stacked, "cells", axis=1, tiled=True)
    length = piece.shape[1]
    block_len = math.gcd(length, 256)
    sections = piece.reshape(6, length // block_len, block_len).transpose(1, 0, 2)

    def inner(accum, rows):
        adj_round = rows[0:2].astype(jnp.bfloat16)
        kre, kim = kernel_tile(rows[2], rows[3], rows[4], rows[5], cell_col, cell_row, freq_count)
        select = (rows[5][:, None] == freq_grid[None, :]).astype(jnp.bfloat16)
        part_a = select * adj_round[0][:, None]
        part_b = select * adj_round[1][:, None]
        left_re = jnp.concatenate([part_a, part_b], axis=1)
        left_im = jnp.concatenate([part_b, -part_a], axis=1)
        return (accum + contract(left_re, kre, 0, 0) + contract(left_im, kim, 0, 0), None)

    total, unused = lax.scan(inner, total, sections)
    local_spec = total.astype(jnp.bfloat16)
    scale = 1.0 / math.sqrt(cell_count * lax.axis_size("cells") * freq_size)
    onehot, hidden_in, pre_one, act_one, pre_two, act_two = forward_pass(
        level_codes, cell_params, level_table, w_proj, w_one, b_one, w_two, b_two
    )
    upper, delta_two = upper_grads(local_spec, w_out, act_one, pre_two, act_two)
    lower, grad_params = lower_grads(
        delta_two, w_two, w_one, pre_one, hidden_in, onehot, cell_params, w_proj
    )
    totals = lax.psum(
        (
            upper[0] * scale,
            upper[1] * scale,
            upper[2] * scale,
            lower[0] * scale,
            lower[1] * scale,
            lower[2] * scale,
            lower[3] * scale,
        ),
        ("cells", "freq"),
    )
    grad_out, grad_w2, grad_b2, grad_w1, grad_b1, grad_table, grad_proj = totals
    return (grad_out, grad_w2, grad_b2, grad_w1, grad_b1, grad_table, grad_proj, grad_params)


def solution(mesh):
    placed = (
        P(None, ("groups", "cells")),
        P(("groups", "cells")),
        P(("groups", "cells")),
        P(("groups", "cells")),
        P(("groups", "cells")),
        P(("groups", "cells", "freq")),
        P(None, ("groups", "cells", "freq")),
        P(),
        P(),
        P(),
        P(),
        P(),
        P(),
        P(),
    )
    return jax.shard_map(
        body,
        mesh=mesh,
        in_specs=placed,
        out_specs=(
            P("groups", None),
            P("groups", None),
            P("groups"),
            P("groups", None),
            P("groups"),
            P("groups", None),
            P("groups", None),
            P(None, ("groups", "cells", "freq")),
        ),
        check_vma=False,
    )
```

profile of v0, /device:TPU:0, one launch (start us, length us, event | category | flops | bytes accessed | tf_op | source)
XLA Modules:
  0.0 153.0 jit_solution(16663212163118805640)
XLA Ops:
  7.2 0.0 copy-start
  7.2 0.0 all-reduce.4.cloned.1.call-start
  7.2 0.0 copy-start.15
  7.3 0.7 copy-done.15
  7.9 0.0 copy-start.10
  7.9 0.6 copy-done.11
  8.6 0.0 copy-done.12
  8.6 0.0 copy-done.8
  8.6 0.0 copy-done.10
  8.7 32.2 %all-gather = f32[8,16,6]{1,2,0:T(8,128)S(1)} all-gather(f32[1,16,6]{1,2,0:T(8,128)S(1)} %bitcast.55), channel_id=1, replica_groups=mesh['groups'=2,'cells'=8,'freq'=2] {'cells'}, dimensions={0}, use_global_device_ids=true | all-gather | bytes 3456 | tf_op jit(solution)/shard_map/all_gather | solution.py:116
  40.9 0.1 reshape.88
  41.0 0.1 fusion.35
  41.1 1.2 fusion.7
  42.3 0.0 copy-start.6
  42.4 0.0 copy-start.7
  42.4 1.2 fusion.3
  43.6 0.0 copy-done.6
  43.6 0.0 copy-done.7
  43.6 0.0 copy-start.4
  43.6 0.0 copy-start.5
  43.7 0.3 fusion.6
  43.9 0.4 copy-done.4
  44.3 0.0 copy-done.5
  44.3 0.3 fusion
  44.6 0.6 copy-done.1
  45.2 0.0 copy-done.9
  45.2 0.2 convolution_add_fusion.2
  45.5 0.0 copy-done
  45.5 0.4 copy-done.14
  45.9 0.3 convolution_add_fusion.1
  46.2 0.0 copy-start.13
  46.2 1.0 convolution_multiply_fusion.4
  47.2 0.3 convert_reduce_fusion.1
  47.5 1.0 convolution_multiply_fusion.3
  48.6 0.3 convert_reduce_fusion
  48.9 1.0 convolution_multiply_fusion.2
  49.9 0.0 all-reduce.4.cloned.1.call-update
  49.9 0.3 convolution_convert_fusion
  50.2 0.1 fusion.4
  50.3 0.3 convolution_multiply_fusion.5
  50.7 58.1 %all-reduce = (f32[256]{0:T(256)}, f32[256]{0:T(256)}, f32[16,256]{1,0:T(8,128)}, f32[8,256]{1,0:T(8,128)}) all-reduce(f32[256]{0:T(256)S(1)} %broadcast_multiply_fusion.1, f32[256]{0:T(256)S(1)} %broadcast_multiply_fusion, ...), channel_id=1, replica_groups=mesh['groups'=2,'cells'=8,'freq'=2] {'cells','freq'}, use_global_device_ids=true, to_apply=%region_3.4 | all-reduce | flops 6656 | bytes 53248 | tf_op jit(solution)/shard_map/psum | solution.py:141
  108.7 0.8 convolution_bitcast_fusion
  109.5 33.3 %all-reduce.4.cloned.1.call-done = (f32[256,128]{1,0:T(8,128)}, f32[256,256]{1,0:T(8,128)}, f32[256,256]{1,0:T(8,128)}) async-done(((f32[256,128]{1,0:T(8,128)}, f32[256,256]{1,0:T(8,128)}, f32[256,256]{1,0:T(8,128)}), (f32[256,128]{1,0:T(8,128)}, f32[256,256]{1,0:T(8,128)}, f32[256,256]{1,0:T(8,128)})) %all-reduce.4.cloned.1.call-update) | async-done | bytes 655376 | tf_op jit(solution)/shard_map/psum | solution.py:141
  142.8 1.6 %copy.27 = f32[256,128]{1,0:T(8,128)} copy(f32[256,128]{1,0:T(8,128)} %get-tuple-element.49) | data formatting | bytes 262144
  144.4 0.0 copy-done.3
  144.4 0.7 copy.28
  145.1 0.3 copy-done.2
  145.5 0.7 copy.29
  (20 shorter events, 0.1 us)
Async XLA Ops:
  7.2 38.3 %copy-start = (bf16[256,256]{1,0:T(8,128)(2,1)S(1)}, bf16[256,256]{1,0:T(8,128)(2,1)}, u32[]{:S(2)}) copy-start(bf16[256,256]{1,0:T(8,128)(2,1)} %param.25) | copy-start | bytes 393220
  7.2 135.6 %all-reduce.4.cloned.1.call-start = ((), (), s32[]{:S(2)}) async-start(), calls=%async_computation | async-start | bytes 1310720 | tf_op jit(solution)/shard_map/psum | solution.py:141
  7.2 0.7 copy-start.15
  7.9 0.7 copy-start.11
  7.9 0.7 copy-start.12
  7.9 0.7 copy-start.8
  7.9 0.7 copy-start.10
  42.3 1.3 copy-start.6
  42.4 1.3 copy-start.7
  43.6 0.7 copy-start.4
  43.6 0.7 copy-start.5
  44.3 0.9 copy-start.1
  44.3 0.9 copy-start.9
  45.2 0.7 copy-start.14
  46.2 1.0 copy-start.13
  142.8 1.6 %copy-start.3 = (f32[256,256]{1,0:T(8,128)S(1)}, f32[256,256]{1,0:T(8,128)}, u32[]{:S(2)}) copy-start(f32[256,256]{1,0:T(8,128)} %get-tuple-element.50) | copy-start | bytes 786436
  144.4 1.0 copy-start.2
Sparse Core Ops, SparseCore 0:
  50.0 92.7 all-reduce.3
where the time goes:
time: 153 us
  blocking collectives  90.3 us (59%)
  waiting for transfers between devices  33.3 us (22%)
  between operations  14.2 us (9%)
  matrix products  8.63 us (6%)
  local copies, waits for them, and re-layouts  6.34 us (4%)
    psum x1, blocking collectives, body(): lax.psum((upper[0] * scale, upper[1] * scale, upper[2] * scale, lower[0]...  58.1 us
    psum x1, waiting for transfers between devices, body(): lax.psum((upper[0] * scale, upper[1] * scale, upper[2] * scale, lower[0]...  33.3 us
    all_gather x1, blocking collectives, body(): piece = lax.all_gather(stacked, 'cells', axis=1, tiled=True)  32.2 us
    dot_general x12, matrix products, contract(): lax.dot_general(left, right, (((left_dim,), (right_dim,)), ((), ())), pre...  7.85 us
    unnamed x36, local copies, waits for them, and re-layouts  6.3 us
  transfers between devices with their start and end apart: 1, of which 1 were waited for; matrix products, arithmetic and copies ran while one was open for 1% of the time, Pallas kernels for 0%

commit v1 on v0

--- a/solution.py
+++ b/solution.py
@@ -1,16 +1,22 @@
+import functools
 import math
 
 import jax
 import jax.numpy as jnp
 from jax import lax
+from jax.experimental import pallas as pl
+from jax.experimental.pallas import tpu as pltpu
 from jax.sharding import PartitionSpec as P
 
 SIDE = 1024
-
 
 wave_low = 1.0
 wave_high = 3.0
 kernel_gain = 150.0
+
+F32 = jnp.float32
+BF16 = jnp.bfloat16
+VMEM_BYTES = 40 * 1024 * 1024
 
 
 def silu_slope(value):
@@ -75,7 +81,7 @@
     return ((grad_w1, grad_b1, grad_table, grad_proj), grad_params)
 
 
-def body(
+def general_body(
     adjoint,
     target_x,
     target_y,
@@ -111,8 +117,7 @@
         ],
         axis=0,
     )
-    initial = jnp.zeros((2 * freq_count, cell_count), jnp.float32)
-    total = initial
+    total = jnp.zeros((2 * freq_count, cell_count), jnp.float32)
     piece = lax.all_gather(stacked, "cells", axis=1, tiled=True)
     length = piece.shape[1]
     block_len = math.gcd(length, 256)
@@ -138,23 +143,315 @@
     lower, grad_params = lower_grads(
         delta_two, w_two, w_one, pre_one, hidden_in, onehot, cell_params, w_proj
     )
-    totals = lax.psum(
-        (
-            upper[0] * scale,
-            upper[1] * scale,
-            upper[2] * scale,
-            lower[0] * scale,
-            lower[1] * scale,
-            lower[2] * scale,
-            lower[3] * scale,
+    totals = lax.psum(tuple(term * scale for term in upper + lower), ("cells", "freq"))
+    return totals + (grad_params,)
+
+
+def split(value, parts):
+    pieces = []
+    for _ in range(parts):
+        piece = value.astype(BF16)
+        pieces.append(piece.astype(F32))
+        value = value - piece.astype(F32)
+    return pieces
+
+
+def pack_kernel(adj_ref, x_ref, y_ref, z_ref, assign_ref, codes_ref, params_ref, out_ref, rows):
+    count = x_ref.shape[1]
+    cells = codes_ref.shape[1]
+    rows[...] = jnp.zeros_like(rows)
+    rows[0:2, 0:count] = adj_ref[...]
+    at = 2
+    for ref in (x_ref, y_ref, z_ref):
+        for piece in split(ref[...], 3):
+            rows[at : at + 1, 0:count] = piece
+            at += 1
+    rows[at : at + 1, 0:count] = assign_ref[...].astype(F32)
+    out_ref[:, 0:cells] = jnp.concatenate(
+        [params_ref[...].astype(F32), jnp.broadcast_to(codes_ref[...].astype(F32), (8, cells))],
+        axis=0,
+    ).astype(BF16)
+    out_ref[:, cells:] = rows[...].T[0:count].astype(BF16)
+
+
+def weight_kernel(
+    table_ref, proj_ref, w1_ref, b1_ref, w2_ref, b2_ref, wo_ref,
+    first_ref, second_ref, bias_ref, back_two_ref, back_one_ref, params_ref, embed_ref,
+):
+    levels, hidden = table_ref.shape
+    stack = jnp.concatenate([table_ref[...].astype(F32), proj_ref[...].astype(F32)], axis=0)
+    joined = jnp.dot(stack.astype(BF16), w1_ref[...], preferred_element_type=F32)
+    used = levels + proj_ref.shape[0]
+    pad = jnp.zeros((7, hidden), F32)
+    full = 0.5 * jnp.concatenate([joined, b1_ref[...], pad], axis=0)
+    rows = jnp.concatenate(split(full, 3), axis=0)
+    fill = 128 - rows.shape[0]
+    first_ref[...] = jnp.concatenate([rows, jnp.zeros((fill, hidden), F32)], axis=0).T.astype(BF16)
+    second_ref[...] = (0.5 * w2_ref[...].astype(F32)).T.astype(BF16)
+    bias_ref[...] = jnp.broadcast_to(0.5 * b2_ref[...], (128, hidden)).T
+    back_two_ref[...] = (0.5 * wo_ref[...].astype(F32)).astype(BF16)
+    back_one_ref[...] = (0.5 * w2_ref[...].astype(F32)).astype(BF16)
+    params_ref[...] = jnp.concatenate(split(joined[levels:used], 2), axis=0).astype(BF16)
+    triple = jnp.concatenate([stack, jnp.zeros((8, hidden), F32)], axis=0)
+    embed_ref[...] = jnp.concatenate(
+        [triple, triple, triple, jnp.zeros((fill, hidden), F32)], axis=0
+    ).T.astype(BF16)
+
+
+def cell_kernel(
+    freq_size, step,
+    place_ref, gathered_ref, first_ref, second_ref, bias_ref, back_two_ref, back_one_ref, params_ref,
+    sums_ref, grad_params_ref,
+    where, lift, waves, deltas,
+):
+    chunks, local, width = gathered_ref.shape
+    cells = width - 128
+    hidden = second_ref.shape[0]
+    freqs = back_two_ref.shape[1] // 2
+    targets = chunks * local
+    me = place_ref[0]
+    freq_rank = place_ref[1]
+
+    parts = []
+    for chunk in range(chunks):
+        parts.append(gathered_ref[chunk ^ me, :, cells:].astype(F32))
+    table = jnp.concatenate(parts, axis=0)
+    point_x = (table[:, 2:3] + table[:, 3:4]) + table[:, 4:5]
+    point_y = (table[:, 5:6] + table[:, 6:7]) + table[:, 7:8]
+    point_z = (table[:, 8:9] + table[:, 9:10]) + table[:, 10:11]
+    assign = table[:, 11:12]
+    wave = (wave_low + (wave_high - wave_low) * assign / (freqs - 1)) * (0.5 / math.pi)
+    full = (targets, 128)
+    where[0] = jnp.broadcast_to(point_x, full)
+    where[1] = jnp.broadcast_to(point_y, full)
+    where[2] = jnp.broadcast_to(point_z * point_z, full)
+    where[3] = jnp.broadcast_to(wave, full)
+    where[4] = jnp.broadcast_to(kernel_gain * point_z, full)
+    grid = lax.broadcasted_iota(jnp.int32, (targets, freqs), 1).astype(F32)
+    select = jnp.where(assign == grid, 1.0, 0.0)
+    part_a = select * table[:, 0:1]
+    part_b = select * table[:, 1:2]
+    lift[:, 0:targets] = jnp.concatenate([part_a, part_b], axis=1).T.astype(BF16)
+    lift[:, targets:] = jnp.concatenate([part_b, -part_a], axis=1).T.astype(BF16)
+    sums_ref[...] = jnp.zeros_like(sums_ref)
+
+    def one(chunk, start):
+        slot = chunk ^ me
+        base = (chunk * freq_size + freq_rank) * cells + start
+        index = base + lax.broadcasted_iota(jnp.int32, (1, step), 1)
+        col = (index % SIDE).astype(F32)
+        row = (index // SIDE).astype(F32)
+        for at in range(0, targets, 16):
+            for lane in range(0, step, 128):
+                here = pl.ds(at, 16)
+                off_x = where[0, here] - col[:, lane : lane + 128]
+                off_y = where[1, here] - row[:, lane : lane + 128]
+                square = off_x * off_x + off_y * off_y + where[2, here]
+                inverse = lax.rsqrt(square)
+                turns = where[3, here] * (square * inverse)
+                angle = (turns - jnp.round(turns)) * (2.0 * math.pi)
+                amplitude = where[4, here] * (inverse * inverse)
+                waves[at : at + 16, lane : lane + 128] = (amplitude * jnp.cos(angle)).astype(BF16)
+                waves[targets + at : targets + at + 16, lane : lane + 128] = (
+                    amplitude * jnp.sin(angle)
+                ).astype(BF16)
+        spectra = jnp.dot(lift[...], waves[...], preferred_element_type=F32).astype(BF16)
+
+        data = gathered_ref[slot, :, pl.ds(start, step)].astype(F32)
+        codes = data[8:16]
+        steps = lax.broadcasted_iota(jnp.int32, (8, step), 0).astype(F32)
+        feature = jnp.concatenate(
+            [
+                jnp.where(codes == steps, 1.0, 0.0),
+                jnp.where(codes == steps + 8.0, 1.0, 0.0),
+                data[0:8],
+                jnp.where(steps == 0.0, 1.0, 0.0),
+            ],
+            axis=0,
+        ).astype(BF16)
+        tripled = jnp.concatenate(
+            [feature, feature, feature, jnp.zeros((32, step), BF16)], axis=0
+        )
+        half_one = jnp.dot(first_ref[...], tripled, preferred_element_type=F32)
+        tanh_one = jnp.tanh(half_one)
+        gate_one = 1.0 + tanh_one
+        act_one = half_one * gate_one
+        slope_one = gate_one + act_one * (1.0 - tanh_one)
+        act_one = act_one.astype(BF16)
+        half_two = jnp.dot(second_ref[...], act_one, preferred_element_type=F32)
+        half_two = half_two + jnp.concatenate([bias_ref[...]] * (step // 128), axis=1)
+        tanh_two = jnp.tanh(half_two)
+        gate_two = 1.0 + tanh_two
+        act_two = half_two * gate_two
+        slope_two = gate_two + act_two * (1.0 - tanh_two)
+        act_two = act_two.astype(BF16)
+        back_two = jnp.dot(back_two_ref[...], spectra, preferred_element_type=F32)
+        delta_two = (back_two * slope_two).astype(BF16)
+        back_one = jnp.dot(back_one_ref[...], delta_two, preferred_element_type=F32)
+        delta_one = (back_one * slope_one).astype(BF16)
+        deltas[chunk, :, pl.ds(start, step)] = delta_one
+        top = hidden + 2 * freqs
+        sums_ref[0:hidden] += contract(act_one, delta_two, 1, 1)
+        sums_ref[hidden:top] += contract(spectra, act_two, 1, 1)
+        sums_ref[top : top + 32] += contract(feature, delta_one, 1, 1)
+        sums_ref[top + 32 : top + 64] += contract(feature, delta_two, 1, 1)
+
+    def each(at, carry):
+        one(at // (cells // step), pl.multiple_of((at % (cells // step)) * step, step))
+        return carry
+
+    lax.fori_loop(0, chunks * (cells // step), each, 0)
+    both = jnp.dot(params_ref[...], deltas[me], preferred_element_type=F32)
+    grad_params_ref[...] = both[0:8] + both[8:16]
+
+
+def finish_kernel(
+    scale, own_ref, other_ref, embed_ref, w1_ref,
+    out_ref, w2_ref, b2_ref, wone_ref, b1_ref, table_ref, proj_ref,
+):
+    hidden = w1_ref.shape[0]
+    top = hidden + out_ref.shape[1]
+    levels = table_ref.shape[0]
+    used = levels + proj_ref.shape[0]
+
+    def total(low, high):
+        return (own_ref[low:high].astype(F32) + other_ref[low:high].astype(F32)) * scale
+
+    w2_ref[...] = total(0, hidden)
+    out_ref[...] = total(hidden, top).T
+    feature = total(top, top + 32)
+    b1_ref[...] = feature[used : used + 1]
+    b2_ref[...] = total(top + 32, top + 64)[used : used + 1]
+    pieces = split(feature, 3)
+    rows = jnp.concatenate(pieces, axis=0).astype(BF16)
+    wone_ref[...] = jnp.dot(embed_ref[:, 0:96], rows, preferred_element_type=F32)
+    back = contract(rows, w1_ref[...], 1, 1)
+    back = (back[0:32] + back[32:64]) + back[64:96]
+    table_ref[...] = back[0:levels]
+    proj_ref[...] = back[levels:used]
+
+
+def small_body(
+    adjoint,
+    target_x,
+    target_y,
+    target_z,
+    assignment,
+    level_codes,
+    cell_params,
+    level_table,
+    w_proj,
+    w_one,
+    b_one,
+    w_two,
+    b_two,
+    w_out,
+):
+    cells = level_codes.shape[0]
+    local = target_x.shape[0]
+    levels, hidden = level_table.shape
+    props = w_proj.shape[0]
+    freqs = w_out.shape[1] // 2
+    chunks = lax.axis_size("cells")
+    freq_size = lax.axis_size("freq")
+    shape = jax.ShapeDtypeStruct
+    params = pltpu.CompilerParams(vmem_limit_bytes=VMEM_BYTES)
+
+    packed = pl.pallas_call(
+        pack_kernel,
+        out_shape=shape((16, cells + 128), BF16),
+        scratch_shapes=[pltpu.VMEM((128, 128), F32)],
+        compiler_params=params,
+        name="pack_inputs",
+    )(
+        adjoint, target_x[None, :], target_y[None, :], target_z[None, :], assignment[None, :],
+        level_codes[None, :], cell_params,
+    )
+    gathered = packed[None]
+    reach = 1
+    while reach < chunks:
+        moved = lax.ppermute(gathered, "cells", [(at, at ^ reach) for at in range(chunks)])
+        gathered = jnp.concatenate([gathered, moved], axis=0)
+        reach *= 2
+
+    first, second, bias, back_two, back_one, proj_rows, embed = pl.pallas_call(
+        weight_kernel,
+        out_shape=(
+            shape((hidden, 128), BF16),
+            shape((hidden, hidden), BF16),
+            shape((hidden, 128), F32),
+            shape((hidden, 2 * freqs), BF16),
+            shape((hidden, hidden), BF16),
+            shape((2 * props, hidden), BF16),
+            shape((hidden, 128), BF16),
         ),
-        ("cells", "freq"),
-    )
-    grad_out, grad_w2, grad_b2, grad_w1, grad_b1, grad_table, grad_proj = totals
-    return (grad_out, grad_w2, grad_b2, grad_w1, grad_b1, grad_table, grad_proj, grad_params)
+        compiler_params=params,
+        name="prepare_weights",
+    )(level_table, w_proj, w_one, b_one[None, :], w_two, b_two[None, :], w_out)
+
+    place = jnp.stack([lax.axis_index("cells"), lax.axis_index("freq")]).astype(jnp.int32)
+    step = min(256, cells)
+    targets = chunks * local
+    vmem = pl.BlockSpec(memory_space=pltpu.VMEM)
+    sums, grad_params = pl.pallas_call(
+        functools.partial(cell_kernel, freq_size, step),
+        out_shape=(
+            shape((hidden + 2 * freqs + 64, hidden), F32),
+            shape((props, cells), F32),
+        ),
+        in_specs=[pl.BlockSpec(memory_space=pltpu.SMEM)] + [vmem] * 7,
+        out_specs=(vmem, vmem),
+        scratch_shapes=[
+            pltpu.VMEM((5, targets, 128), F32),
+            pltpu.VMEM((2 * freqs, 2 * targets), BF16),
+            pltpu.VMEM((2 * targets, step), BF16),
+            pltpu.VMEM((chunks, hidden, cells), BF16),
+        ],
+        compiler_params=params,
+        name="all_cells",
+    )(place, gathered, first, second, bias, back_two, back_one, proj_rows)
+
+    other = lax.ppermute(sums, "freq", [(at, at ^ 1) for at in range(freq_size)])
+    scale = 1.0 / math.sqrt(cells * chunks * freq_size)
+    grad_out, grad_w2, grad_b2, grad_w1, grad_b1, grad_table, grad_proj = pl.pallas_call(
+        functools.partial(finish_kernel, scale),
+        out_shape=(
+            shape((hidden, 2 * freqs), F32),
+            shape((hidden, hidden), F32),
+            shape((1, hidden), F32),
+            shape((hidden, hidden), F32),
+            shape((1, hidden), F32),
+            shape((levels, hidden), F32),
+            shape((props, hidden), F32),
+        ),
+        compiler_params=params,
+        name="finish_sums",
+    )(sums, other, embed, w_one)
+    return (
+        grad_out, grad_w2, grad_b2[0], grad_w1, grad_b1[0], grad_table, grad_proj, grad_params,
+    )
 
 
 def solution(mesh):
+    chunks = mesh.shape["cells"]
+    paired = mesh.shape["freq"] == 2 and chunks & (chunks - 1) == 0
+
+    def body(*args):
+        local = args[1].shape[0]
+        cells = args[5].shape[0]
+        hidden = args[9].shape[0]
+        suits = (
+            paired
+            and local == 16
+            and cells % 256 == 0
+            and chunks * cells * chunks * local <= 1 << 20
+            and args[7].shape[0] == 16
+            and args[8].shape[0] == 8
+            and hidden % 128 == 0
+            and args[13].shape[1] == 128
+        )
+        return (small_body if suits else general_body)(*args)
+
     placed = (
         P(None, ("groups", "cells")),
         P(("groups", "cells")),

time: 153 us -> 47.5 us (0.31)
  blocking collectives: 90.3 us -> 0 us
  waiting for transfers between devices: 33.3 us -> 7.13 us
  Pallas kernels: 0 us -> 23.6 us
  between operations: 14.2 us -> 0.7 us
  matrix products: 8.63 us -> 0 us
  starting transfers between devices: 0.04 us -> 7.8 us
    psum x1 -> x0, blocking collectives: 58.1 us -> none  [body(): lax.psum((upper[0] * scale, upper[1] * scale, upper[2] * scale, lower[0]...]
    psum x1 -> x0, waiting for transfers between devices: 33.3 us -> none  [body(): lax.psum((upper[0] * scale, upper[1] * scale, upper[2] * scale, lower[0]...]
    all_gather x1 -> x0, blocking collectives: 32.2 us -> none  [body(): piece = lax.all_gather(stacked, 'cells', axis=1, tiled=True)]
    pallas_call x0 -> x4, Pallas kernels: none -> 23.6 us  [the longest x1 22.2 us: small_body(): pl.pallas_call(functools.partial(cell_kernel, freq_size, step), out_shape...]
    dot_general x15 -> x0, matrix products: 8.63 us -> none  [the longest x12 7.85 us: contract(): lax.dot_general(left, right, (((left_dim,), (right_dim,)), ((), ())), pre...]
    ppermute x0 -> x4, starting transfers between devices: none -> 7.8 us  [the longest x3 7.8 us: small_body(): lax.ppermute(gathered, 'cells', [(at, at ^ reach) for at in range(chunks)])]
    ppermute x0 -> x4, waiting for transfers between devices: none -> 7.13 us  [the longest x3 5.32 us: small_body(): lax.ppermute(gathered, 'cells', [(at, at ^ reach) for at in range(chunks)])]
    unnamed x36 -> x28, local copies, waits for them, and re-layouts: 6.3 us -> 7.83 us
  transfers between devices with their start and end apart: 1 -> 4, of which waited for: 1 -> 3; matrix products, arithmetic and copies ran while one was open for 1% -> 0% of each run, Pallas kernels for 0% -> 1%
where the time goes in v1:
time: 47.5 us; the launch traced here: 47.1 us
  Pallas kernels  23.6 us (50%)
  local copies, waits for them, and re-layouts  7.83 us (16%)
  starting transfers between devices  7.8 us (16%)
  waiting for transfers between devices  7.13 us (15%)
  between operations  0.7 us (1%)
    pallas_call x1, Pallas kernels, small_body(): pl.pallas_call(functools.partial(cell_kernel, freq_size, step), out_shape...  22.2 us
    unnamed x28, local copies, waits for them, and re-layouts  7.83 us
    ppermute x3, starting transfers between devices, small_body(): lax.ppermute(gathered, 'cells', [(at, at ^ reach) for at in range(chunks)])  7.8 us
    ppermute x3, waiting for transfers between devices, small_body(): lax.ppermute(gathered, 'cells', [(at, at ^ reach) for at in range(chunks)])  5.32 us
    ppermute x1, waiting for transfers between devices, small_body(): lax.ppermute(sums, 'freq', [(at, at ^ 1) for at in range(freq_size)])  1.81 us
    pallas_call x1, Pallas kernels, small_body(): pl.pallas_call(functools.partial(finish_kernel, scale), out_shape=(shape(...  0.98 us
  transfers between devices with their start and end apart: 4, of which 3 were waited for; matrix products, arithmetic and copies ran while one was open for 0% of the time, Pallas kernels for 1%

profile of v1, /device:TPU:0, one launch (start us, length us, event | category | flops | bytes accessed | tf_op | source)
XLA Modules:
  0.0 47.1 jit_solution(18155886495849872453)
XLA Ops:
  0.6 0.0 copy-start
  0.6 0.0 copy-start.4
  0.7 0.7 %copy-done.4 = bf16[8,512]{1,0:T(8,128)(2,1)S(1)} copy-done((bf16[8,512]{1,0:T(8,128)(2,1)S(1)}, bf16[8,512]{1,0:T(8,128)(2,1)}, u32[]{:S(2)}) %copy-start.4) | copy-done | bytes 8216
  1.4 0.0 copy-start.6
  1.4 0.7 %copy-done.6 = s32[512]{0:T(512)S(1)} copy-done((s32[512]{0:T(512)S(1)}, s32[512]{0:T(512)}, u32[]{:S(2)}) %copy-start.6) | copy-done | bytes 2072
  2.1 0.0 copy-start.9
  2.1 0.7 %copy-done.9 = f32[2,16]{1,0:T(2,128)S(1)} copy-done((f32[2,16]{1,0:T(2,128)S(1)}, f32[2,16]{1,0:T(2,128)}, u32[]{:S(2)}) %copy-start.9) | copy-done | bytes 152
  2.7 0.0 copy-start.10
  2.7 0.7 %copy-done.10 = f32[16]{0:T(128)S(1)} copy-done((f32[16]{0:T(128)S(1)}, f32[16]{0:T(128)}, u32[]{:S(2)}) %copy-start.10) | copy-done | bytes 88
  3.4 0.0 copy-start.11
  3.4 0.7 %copy-done.11 = f32[16]{0:T(128)S(1)} copy-done((f32[16]{0:T(128)S(1)}, f32[16]{0:T(128)}, u32[]{:S(2)}) %copy-start.11) | copy-done | bytes 88
  4.1 0.0 copy-start.12
  4.1 0.7 %copy-done.12 = f32[16]{0:T(128)S(1)} copy-done((f32[16]{0:T(128)S(1)}, f32[16]{0:T(128)}, u32[]{:S(2)}) %copy-start.12) | copy-done | bytes 88
  4.7 0.0 copy-start.13
  4.7 0.7 %copy-done.13 = s32[16]{0:T(128)S(1)} copy-done((s32[16]{0:T(128)S(1)}, s32[16]{0:T(128)}, u32[]{:S(2)}) %copy-start.13) | copy-done | bytes 88
  5.4 0.1 pack_inputs.1
  5.4 3.0 %collective-permute-start = (bf16[1,16,640]{2,1,0:T(8,128)(2,1)S(1)}, bf16[1,16,640]{2,1,0:T(8,128)(2,1)S(1)}, u32[]{:S(2)}, u32[]{:S(2)}) collective-permute-start(bf16[1,16,640]{2,1,0:T(8,128)(2,1)S(1)} %bitcast.12), channel_id=1, source_target_pairs={{0,2},{2,0},{4,6},{6,4},{8,10},{10,8},{12,14},{14,12},{1,3},{3,1},... | collective-permute-start | bytes 61448 | tf_op jit(solution)/shard_map/ppermute | solution.py:373
  8.4 1.8 %collective-permute-done = bf16[1,16,640]{2,1,0:T(8,128)(2,1)S(1)} collective-permute-done((bf16[1,16,640]{2,1,0:T(8,128)(2,1)S(1)}, bf16[1,16,640]{2,1,0:T(8,128)(2,1)S(1)}, u32[]{:S(2)}, u32[]{:S(2)}) %collective-permute-start) | collective-permute-done | bytes 20512 | tf_op jit(solution)/shard_map/ppermute | solution.py:373
  10.2 0.0 copy-start.3
  10.2 2.2 %collective-permute-start.1 = (bf16[2,16,640]{2,1,0:T(8,128)(2,1)S(1)}, bf16[2,16,640]{2,1,0:T(8,128)(2,1)S(1)}, u32[]{:S(2)}, u32[]{:S(2)}) collective-permute-start(bf16[2,16,640]{2,1,0:T(8,128)(2,1)S(1)} %pad_maximum_fusion.2), channel_id=1, source_target_pairs={{0,4},{2,6},{4,0},{6,2},{8,12},{10,14},{12,8},{14,10},{1,5},{3,7},... | collective-permute-start | bytes 122888 | tf_op jit(solution)/shard_map/ppermute | solution.py:373
  12.4 0.0 copy-start.8
  12.4 0.0 copy-start.7
  12.4 0.0 copy-done
  12.4 0.0 copy-done.3
  12.4 0.7 %copy-done.8 = f32[256]{0:T(256)S(1)} copy-done((f32[256]{0:T(256)S(1)}, f32[256]{0:T(256)}, u32[]{:S(2)}) %copy-start.8) | copy-done | bytes 1048
  13.0 0.0 copy-done.7
  13.1 0.0 copy-start.1
  13.1 0.9 %copy-done.1 = bf16[256,256]{1,0:T(8,128)(2,1)S(1)} copy-done((bf16[256,256]{1,0:T(8,128)(2,1)S(1)}, bf16[256,256]{1,0:T(8,128)(2,1)}, u32[]{:S(2)}) %copy-start.1) | copy-done | bytes 131096
  14.0 0.0 copy-start.2
  14.0 0.8 %copy-done.2 = bf16[256,128]{1,0:T(8,128)(2,1)S(1)} copy-done((bf16[256,128]{1,0:T(8,128)(2,1)S(1)}, bf16[256,128]{1,0:T(8,128)(2,1)}, u32[]{:S(2)}) %copy-start.2) | copy-done | bytes 65560
  14.8 0.0 copy-start.5
  14.8 0.7 %copy-done.5 = bf16[8,256]{1,0:T(8,128)(2,1)S(1)} copy-done((bf16[8,256]{1,0:T(8,128)(2,1)S(1)}, bf16[8,256]{1,0:T(8,128)(2,1)}, u32[]{:S(2)}) %copy-start.5) | copy-done | bytes 4120
  15.5 0.3 prepare_weights.1
  15.8 0.0 collective-permute-done.1
  15.8 2.7 %collective-permute-start.2 = (bf16[4,16,640]{2,1,0:T(8,128)(2,1)S(1)}, bf16[4,16,640]{2,1,0:T(8,128)(2,1)S(1)}, u32[]{:S(2)}, u32[]{:S(2)}) collective-permute-start(bf16[4,16,640]{2,1,0:T(8,128)(2,1)S(1)} %pad_maximum_fusion.1), channel_id=1, source_target_pairs={{0,8},{2,10},{4,12},{6,14},{8,0},{10,2},{12,4},{14,6},{1,9},{3,11}... | collective-permute-start | bytes 245768 | tf_op jit(solution)/shard_map/ppermute | solution.py:373
  18.5 0.1 pad_add_fusion.place_ref
  18.5 3.6 %collective-permute-done.2 = bf16[4,16,640]{2,1,0:T(8,128)(2,1)S(1)} collective-permute-done((bf16[4,16,640]{2,1,0:T(8,128)(2,1)S(1)}, bf16[4,16,640]{2,1,0:T(8,128)(2,1)S(1)}, u32[]{:S(2)}, u32[]{:S(2)}) %collective-permute-start.2) | collective-permute-done | bytes 81952 | tf_op jit(solution)/shard_map/ppermute | solution.py:373
  22.1 22.2 %all_cells.1 = (f32[448,256]{1,0:T(8,128)S(1)}, f32[8,512]{1,0:T(8,128)}) custom-call(s32[2]{0:T(128)S(1)} %pad_add_fusion.place_ref, bf16[8,16,640]{2,1,0:T(8,128)(2,1)S(1)} %pad_maximum_fusion.gathered_ref, bf16[256,128]{1,0:T(8,128)(2,1)S(1)} %get-tuple-element.24.first_ref, bf16[256,256]{1,0:T(8,128)(2,1)S(1)} %get-tuple-element.25.second_ref, ...), custom_call_target="tpu_custom_call" | custom-call | tf_op jit(solution)/shard_map/all_cells/pallas_call | solution.py:396
  44.3 0.0 collective-permute-start.3
  44.3 1.8 %collective-permute-done.3.other_ref = f32[448,256]{1,0:T(8,128)S(1)} collective-permute-done((f32[448,256]{1,0:T(8,128)S(1)}, f32[448,256]{1,0:T(8,128)S(1)}, u32[]{:S(2)}, u32[]{:S(2)}) %collective-permute-start.3) | collective-permute-done | bytes 458784 | tf_op jit(solution)/shard_map/ppermute | solution.py:414
  46.2 1.0 %finish_sums.1 = (f32[256,128]{1,0:T(8,128)}, f32[256,256]{1,0:T(8,128)}, f32[1,256]{1,0:T(1,128)}, f32[256,256]{1,0:T(8,128)}, f32[1,256]{1,0:T(1,128)}, /*index=5*/f32[16,256]{1,0:T(8,128)}, f32[8,256]{1,0:T(8,128)}) custom-call(f32[448,256]{1,0:T(8,128)S(1)} %get-tuple-element.30.own_ref, f32[448,256]{1,0:T(8,128)S(1)} %collective-permute-done.3.other_ref, ...), custom_call_target="tpu_custom_call" | custom-call | tf_op jit(solution)/shard_map/finish_sums/pallas_call | solution.py:416
  (3 shorter events, 0.0 us)
Async XLA Ops:
  0.6 11.7 %copy-start = (bf16[256,256]{1,0:T(8,128)(2,1)S(1)}, bf16[256,256]{1,0:T(8,128)(2,1)}, u32[]{:S(2)}) copy-start(bf16[256,256]{1,0:T(8,128)(2,1)} %w1_ref.3) | copy-start | bytes 393220
  0.6 0.7 %copy-start.4 = (bf16[8,512]{1,0:T(8,128)(2,1)S(1)}, bf16[8,512]{1,0:T(8,128)(2,1)}, u32[]{:S(2)}) copy-start(bf16[8,512]{1,0:T(8,128)(2,1)} %params_ref.1) | copy-start | bytes 24580
  1.4 0.7 %copy-start.6 = (s32[512]{0:T(512)S(1)}, s32[512]{0:T(512)}, u32[]{:S(2)}) copy-start(s32[512]{0:T(512)} %param.19) | copy-start | bytes 6148
  2.1 0.7 %copy-start.9 = (f32[2,16]{1,0:T(2,128)S(1)}, f32[2,16]{1,0:T(2,128)}, u32[]{:S(2)}) copy-start(f32[2,16]{1,0:T(2,128)} %adj_ref.1) | copy-start | bytes 388
  2.7 0.7 %copy-start.10 = (f32[16]{0:T(128)S(1)}, f32[16]{0:T(128)}, u32[]{:S(2)}) copy-start(f32[16]{0:T(128)} %param.15) | copy-start | bytes 196
  3.4 0.7 %copy-start.11 = (f32[16]{0:T(128)S(1)}, f32[16]{0:T(128)}, u32[]{:S(2)}) copy-start(f32[16]{0:T(128)} %param.16) | copy-start | bytes 196
  4.1 0.7 %copy-start.12 = (f32[16]{0:T(128)S(1)}, f32[16]{0:T(128)}, u32[]{:S(2)}) copy-start(f32[16]{0:T(128)} %param.17) | copy-start | bytes 196
  4.7 0.7 %copy-start.13 = (s32[16]{0:T(128)S(1)}, s32[16]{0:T(128)}, u32[]{:S(2)}) copy-start(s32[16]{0:T(128)} %param.18) | copy-start | bytes 196
  5.4 4.7 %collective-permute-start = (bf16[1,16,640]{2,1,0:T(8,128)(2,1)S(1)}, bf16[1,16,640]{2,1,0:T(8,128)(2,1)S(1)}, u32[]{:S(2)}, u32[]{:S(2)}) collective-permute-start(bf16[1,16,640]{2,1,0:T(8,128)(2,1)S(1)} %bitcast.12), channel_id=1, source_target_pairs={{0,2},{2,0},{4,6},{6,4},{8,10},{10,8},{12,14},{14,12},{1,3},{3,1},... | collective-permute-start | bytes 61448 | tf_op jit(solution)/shard_map/ppermute | solution.py:373
  10.2 2.2 %copy-start.3 = (bf16[16,256]{1,0:T(8,128)(2,1)S(1)}, bf16[16,256]{1,0:T(8,128)(2,1)}, u32[]{:S(2)}) copy-start(bf16[16,256]{1,0:T(8,128)(2,1)} %table_ref.1) | copy-start | bytes 24580
  10.2 5.6 %collective-permute-start.1 = (bf16[2,16,640]{2,1,0:T(8,128)(2,1)S(1)}, bf16[2,16,640]{2,1,0:T(8,128)(2,1)S(1)}, u32[]{:S(2)}, u32[]{:S(2)}) collective-permute-start(bf16[2,16,640]{2,1,0:T(8,128)(2,1)S(1)} %pad_maximum_fusion.2), channel_id=1, source_target_pairs={{0,4},{2,6},{4,0},{6,2},{8,12},{10,14},{12,8},{14,10},{1,5},{3,7},... | collective-permute-start | bytes 122888 | tf_op jit(solution)/shard_map/ppermute | solution.py:373
  12.4 0.7 %copy-start.8 = (f32[256]{0:T(256)S(1)}, f32[256]{0:T(256)}, u32[]{:S(2)}) copy-start(f32[256]{0:T(256)} %param.26) | copy-start | bytes 3076
  12.4 0.7 %copy-start.7 = (f32[256]{0:T(256)S(1)}, f32[256]{0:T(256)}, u32[]{:S(2)}) copy-start(f32[256]{0:T(256)} %param.24) | copy-start | bytes 3076
  13.1 0.9 %copy-start.1 = (bf16[256,256]{1,0:T(8,128)(2,1)S(1)}, bf16[256,256]{1,0:T(8,128)(2,1)}, u32[]{:S(2)}) copy-start(bf16[256,256]{1,0:T(8,128)(2,1)} %w2_ref.1) | copy-start | bytes 393220
  14.0 0.8 %copy-start.2 = (bf16[256,128]{1,0:T(8,128)(2,1)S(1)}, bf16[256,128]{1,0:T(8,128)(2,1)}, u32[]{:S(2)}) copy-start(bf16[256,128]{1,0:T(8,128)(2,1)} %wo_ref.1) | copy-start | bytes 196612
  14.8 0.7 %copy-start.5 = (bf16[8,256]{1,0:T(8,128)(2,1)S(1)}, bf16[8,256]{1,0:T(8,128)(2,1)}, u32[]{:S(2)}) copy-start(bf16[8,256]{1,0:T(8,128)(2,1)} %proj_ref.1) | copy-start | bytes 12292
  15.8 6.3 %collective-permute-start.2 = (bf16[4,16,640]{2,1,0:T(8,128)(2,1)S(1)}, bf16[4,16,640]{2,1,0:T(8,128)(2,1)S(1)}, u32[]{:S(2)}, u32[]{:S(2)}) collective-permute-start(bf16[4,16,640]{2,1,0:T(8,128)(2,1)S(1)} %pad_maximum_fusion.1), channel_id=1, source_target_pairs={{0,8},{2,10},{4,12},{6,14},{8,0},{10,2},{12,4},{14,6},{1,9},{3,11}... | collective-permute-start | bytes 245768 | tf_op jit(solution)/shard_map/ppermute | solution.py:373
  44.3 1.8 %collective-permute-start.3 = (f32[448,256]{1,0:T(8,128)S(1)}, f32[448,256]{1,0:T(8,128)S(1)}, u32[]{:S(2)}, u32[]{:S(2)}) collective-permute-start(f32[448,256]{1,0:T(8,128)S(1)} %get-tuple-element.30.own_ref), channel_id=1, source_target_pairs={{0,1},{1,0},{2,3},{3,2},{4,5},{5,4},{6,7},{7,6},{8,9},{9,8},{10,11... | collective-permute-start | bytes 1376264 | tf_op jit(solution)/shard_map/ppermute | solution.py:414

commit v2 on v1

--- a/solution.py
+++ b/solution.py
@@ -17,6 +17,7 @@
 F32 = jnp.float32
 BF16 = jnp.bfloat16
 VMEM_BYTES = 40 * 1024 * 1024
+WHOLE_VMEM = 64 * 1024 * 1024 - 256 * 1024
 
 
 def silu_slope(value):
@@ -156,7 +157,21 @@
     return pieces
 
 
-def pack_kernel(adj_ref, x_ref, y_ref, z_ref, assign_ref, codes_ref, params_ref, out_ref, rows):
+def fetch(sources, buffers, arrived):
+    copies = [
+        pltpu.make_async_copy(source, buffer, arrived.at[at])
+        for at, (source, buffer) in enumerate(zip(sources, buffers))
+    ]
+    for copy in copies:
+        copy.start()
+    for copy in copies:
+        copy.wait()
+
+
+def pack_kernel(*refs):
+    sources, out_ref, buffers, (rows, arrived) = refs[:7], refs[7], refs[8:15], refs[15:]
+    fetch(sources, buffers, arrived)
+    adj_ref, x_ref, y_ref, z_ref, assign_ref, codes_ref, params_ref = buffers
     count = x_ref.shape[1]
     cells = codes_ref.shape[1]
     rows[...] = jnp.zeros_like(rows)
@@ -174,10 +189,11 @@
     out_ref[:, cells:] = rows[...].T[0:count].astype(BF16)
 
 
-def weight_kernel(
-    table_ref, proj_ref, w1_ref, b1_ref, w2_ref, b2_ref, wo_ref,
-    first_ref, second_ref, bias_ref, back_two_ref, back_one_ref, params_ref, embed_ref,
-):
+def weight_kernel(*refs):
+    sources, buffers, arrived = refs[:7], refs[14:21], refs[21]
+    first_ref, second_ref, bias_ref, back_two_ref, back_one_ref, params_ref, embed_ref = refs[7:14]
+    fetch(sources, buffers, arrived)
+    table_ref, proj_ref, w1_ref, b1_ref, w2_ref, b2_ref, wo_ref = buffers
     levels, hidden = table_ref.shape
     stack = jnp.concatenate([table_ref[...].astype(F32), proj_ref[...].astype(F32)], axis=0)
     joined = jnp.dot(stack.astype(BF16), w1_ref[...], preferred_element_type=F32)
@@ -198,11 +214,16 @@
     ).T.astype(BF16)
 
 
+SINE = (3.1415820121765137, -5.167142868041992, 2.5418989658355713, -0.5546361804008484)
+COSINE = (-4.934795379638672, 4.058451175689697, -1.3320938348770142, 0.22008062899112701)
+
+
 def cell_kernel(
     freq_size, step,
     place_ref, gathered_ref, first_ref, second_ref, bias_ref, back_two_ref, back_one_ref, params_ref,
     sums_ref, grad_params_ref,
-    where, lift, waves, deltas,
+    across, where, lift, waves, deltas,
+    act_one, act_kept, slope_one, act_two, delta_two, spectra,
 ):
     chunks, local, width = gathered_ref.shape
     cells = width - 128
@@ -211,6 +232,7 @@
     targets = chunks * local
     me = place_ref[0]
     freq_rank = place_ref[1]
+    stride = freq_size * cells
 
     parts = []
     for chunk in range(chunks):
@@ -222,11 +244,15 @@
     assign = table[:, 11:12]
     wave = (wave_low + (wave_high - wave_low) * assign / (freqs - 1)) * (0.5 / math.pi)
     full = (targets, 128)
-    where[0] = jnp.broadcast_to(point_x, full)
-    where[1] = jnp.broadcast_to(point_y, full)
-    where[2] = jnp.broadcast_to(point_z * point_z, full)
-    where[3] = jnp.broadcast_to(wave, full)
-    where[4] = jnp.broadcast_to(kernel_gain * point_z, full)
+    where[0] = jnp.broadcast_to(point_y, full)
+    where[1] = jnp.broadcast_to(point_z * point_z, full)
+    where[2] = jnp.broadcast_to(wave, full)
+    where[3] = jnp.broadcast_to(kernel_gain * point_z, full)
+    wide_x = jnp.broadcast_to(point_x, full)
+    for lane in range(0, cells, 128):
+        index = freq_rank * cells + lane + lax.broadcasted_iota(jnp.int32, (1, 128), 1)
+        offset = wide_x - (index % SIDE).astype(F32)
+        across[:, lane : lane + 128] = offset * offset
     grid = lax.broadcasted_iota(jnp.int32, (targets, freqs), 1).astype(F32)
     select = jnp.where(assign == grid, 1.0, 0.0)
     part_a = select * table[:, 0:1]
@@ -235,72 +261,137 @@
     lift[:, targets:] = jnp.concatenate([part_b, -part_a], axis=1).T.astype(BF16)
     sums_ref[...] = jnp.zeros_like(sums_ref)
 
-    def one(chunk, start):
-        slot = chunk ^ me
-        base = (chunk * freq_size + freq_rank) * cells + start
-        index = base + lax.broadcasted_iota(jnp.int32, (1, step), 1)
-        col = (index % SIDE).astype(F32)
-        row = (index // SIDE).astype(F32)
+    per = cells // step
+    total = chunks * per
+    top = hidden + 2 * freqs
+    dot = functools.partial(jnp.dot, preferred_element_type=F32)
+
+    def place(block):
+        return block // per, pl.multiple_of(lax.rem(block, per) * step, step)
+
+    def holograms(block, even):
+        chunk, start = place(block)
+        row = ((chunk * stride + freq_rank * cells) // SIDE).astype(F32)
         for at in range(0, targets, 16):
+            here = slice(at, at + 16)
+            offset = where[0, here] - row
+            rest = offset * offset + where[1, here]
             for lane in range(0, step, 128):
-                here = pl.ds(at, 16)
-                off_x = where[0, here] - col[:, lane : lane + 128]
-                off_y = where[1, here] - row[:, lane : lane + 128]
-                square = off_x * off_x + off_y * off_y + where[2, here]
+                square = across[here, pl.ds(start + lane, 128)] + rest
                 inverse = lax.rsqrt(square)
-                turns = where[3, here] * (square * inverse)
-                angle = (turns - jnp.round(turns)) * (2.0 * math.pi)
-                amplitude = where[4, here] * (inverse * inverse)
-                waves[at : at + 16, lane : lane + 128] = (amplitude * jnp.cos(angle)).astype(BF16)
-                waves[targets + at : targets + at + 16, lane : lane + 128] = (
-                    amplitude * jnp.sin(angle)
+                turns = where[2, here] * (square * inverse)
+                part = turns - jnp.round(turns)
+                power = part * part
+                sine = part * (((SINE[3] * power + SINE[2]) * power + SINE[1]) * power + SINE[0])
+                cosine = (COSINE[2] * power + COSINE[1]) * power + COSINE[0]
+                cosine = cosine * power + 1.0
+                amplitude = where[3, here] * (inverse * inverse)
+                twice = (amplitude + amplitude) * sine
+                waves[even, at : at + 16, lane : lane + 128] = (amplitude - twice * sine).astype(BF16)
+                waves[even, targets + at : targets + at + 16, lane : lane + 128] = (
+                    twice * cosine
                 ).astype(BF16)
-        spectra = jnp.dot(lift[...], waves[...], preferred_element_type=F32).astype(BF16)
-
-        data = gathered_ref[slot, :, pl.ds(start, step)].astype(F32)
+                yield
+
+    def feature_of(block):
+        chunk, start = place(block)
+        data = gathered_ref[chunk ^ me, :, pl.ds(start, step)].astype(F32)
         codes = data[8:16]
         steps = lax.broadcasted_iota(jnp.int32, (8, step), 0).astype(F32)
-        feature = jnp.concatenate(
-            [
-                jnp.where(codes == steps, 1.0, 0.0),
-                jnp.where(codes == steps + 8.0, 1.0, 0.0),
-                data[0:8],
-                jnp.where(steps == 0.0, 1.0, 0.0),
-            ],
-            axis=0,
-        ).astype(BF16)
-        tripled = jnp.concatenate(
-            [feature, feature, feature, jnp.zeros((32, step), BF16)], axis=0
-        )
-        half_one = jnp.dot(first_ref[...], tripled, preferred_element_type=F32)
-        tanh_one = jnp.tanh(half_one)
-        gate_one = 1.0 + tanh_one
-        act_one = half_one * gate_one
-        slope_one = gate_one + act_one * (1.0 - tanh_one)
-        act_one = act_one.astype(BF16)
-        half_two = jnp.dot(second_ref[...], act_one, preferred_element_type=F32)
-        half_two = half_two + jnp.concatenate([bias_ref[...]] * (step // 128), axis=1)
-        tanh_two = jnp.tanh(half_two)
-        gate_two = 1.0 + tanh_two
-        act_two = half_two * gate_two
-        slope_two = gate_two + act_two * (1.0 - tanh_two)
-        act_two = act_two.astype(BF16)
-        back_two = jnp.dot(back_two_ref[...], spectra, preferred_element_type=F32)
-        delta_two = (back_two * slope_two).astype(BF16)
-        back_one = jnp.dot(back_one_ref[...], delta_two, preferred_element_type=F32)
-        delta_one = (back_one * slope_one).astype(BF16)
-        deltas[chunk, :, pl.ds(start, step)] = delta_one
-        top = hidden + 2 * freqs
-        sums_ref[0:hidden] += contract(act_one, delta_two, 1, 1)
-        sums_ref[hidden:top] += contract(spectra, act_two, 1, 1)
-        sums_ref[top : top + 32] += contract(feature, delta_one, 1, 1)
-        sums_ref[top + 32 : top + 64] += contract(feature, delta_two, 1, 1)
-
-    def each(at, carry):
-        one(at // (cells // step), pl.multiple_of((at % (cells // step)) * step, step))
+        rows = [
+            jnp.where(codes == steps, 1.0, 0.0),
+            jnp.where(codes == steps + 8.0, 1.0, 0.0),
+            data[0:8],
+            jnp.where(steps == 0.0, 1.0, 0.0),
+        ]
+        return jnp.concatenate(rows, axis=0).astype(BF16)
+
+    def activate(half):
+        tanh = jnp.tanh(half)
+        gate = 1.0 + tanh
+        act = half * gate
+        return act.astype(BF16), gate + act * (1.0 - tanh)
+
+    def outer(low, left, right):
+        sums_ref[low : low + left.shape[0]] += contract(left, right, 1, 1)
+
+    def lower(block, even):
+        chunk, start = place(block)
+        feature = feature_of(block)
+        delta = delta_two[even]
+        back = dot(back_one_ref[...], delta)
+        yield
+        value = (back * slope_one[even]).astype(BF16)
+        deltas[chunk, :, pl.ds(start, step)] = value
+        yield
+        outer(0, act_kept[even], delta)
+        yield
+        outer(hidden, spectra[even], act_two[even])
+        yield
+        outer(top + 32, feature, delta)
+        outer(top, feature, value)
+        yield
+
+    def upper(block, even):
+        spectrum = dot(lift[...], waves[even]).astype(BF16)
+        spectra[even] = spectrum
+        yield
+        act = act_one[even]
+        act_kept[even] = act
+        half = dot(second_ref[...], act)
+        half = half + jnp.concatenate([bias_ref[...]] * (step // 128), axis=1)
+        yield
+        back = dot(back_two_ref[...], spectrum)
+        yield
+        act, slope = activate(half)
+        act_two[even] = act
+        yield
+        delta_two[even] = (back * slope).astype(BF16)
+        yield
+
+    def begin(block, even):
+        feature = feature_of(block)
+        rows = [feature] * 3 + [jnp.zeros((32, step), BF16)]
+        half = dot(first_ref[...], jnp.concatenate(rows, axis=0))
+        yield
+        act, slope = activate(half)
+        act_one[even] = act
+        slope_one[even] = slope
+        yield
+
+    stages = (begin, upper, lower)
+
+    def each(at, odd, live=(2, 1, 0)):
+        waiting = [stages[lag](at - lag, (odd + lag) % 2) for lag in live]
+        points = {2: 5, 1: 5, 0: 2}
+        spots = sum(points[lag] for lag in live)
+        pieces = (targets // 16) * (step // 128) if 0 in live else 0
+        extra = holograms(at, odd)
+        done, drawn = 0, 0
+        while waiting:
+            for stage in list(waiting):
+                if next(stage, True) is True:
+                    waiting.remove(stage)
+                    continue
+                done += 1
+                while drawn < pieces * done // spots:
+                    next(extra)
+                    drawn += 1
+        if pieces:
+            for _ in extra:
+                pass
+
+    each(jnp.int32(0), 0, (0,))
+    each(jnp.int32(1), 1, (1, 0))
+
+    def run(at, carry):
+        each(2 * at, 0)
+        each(2 * at + 1, 1)
         return carry
 
-    lax.fori_loop(0, chunks * (cells // step), each, 0)
+    lax.fori_loop(1, total // 2, run, 0)
+    each(jnp.int32(total), 0, (2, 1))
+    each(jnp.int32(total + 1), 1, (2,))
     both = jnp.dot(params_ref[...], deltas[me], preferred_element_type=F32)
     grad_params_ref[...] = both[0:8] + both[8:16]
 
@@ -329,6 +420,38 @@
     back = (back[0:32] + back[32:64]) + back[64:96]
     table_ref[...] = back[0:levels]
     proj_ref[...] = back[levels:used]
+
+
+def run_cells(place, gathered, *weights, step, freq_size, local):
+    chunks, _, width = gathered.shape
+    cells = width - 128
+    hidden, out_dim = weights[3].shape
+    targets = chunks * local
+    vmem = pl.BlockSpec(memory_space=pltpu.VMEM)
+    return pl.pallas_call(
+        functools.partial(cell_kernel, freq_size, step),
+        out_shape=(
+            jax.ShapeDtypeStruct((hidden + out_dim + 64, hidden), F32),
+            jax.ShapeDtypeStruct((weights[5].shape[0] // 2, cells), F32),
+        ),
+        in_specs=[pl.BlockSpec(memory_space=pltpu.SMEM)] + [vmem] * 7,
+        out_specs=(vmem, vmem),
+        scratch_shapes=[
+            pltpu.VMEM((targets, cells), F32),
+            pltpu.VMEM((4, targets, 128), F32),
+            pltpu.VMEM((out_dim, 2 * targets), BF16),
+            pltpu.VMEM((2, 2 * targets, step), BF16),
+            pltpu.VMEM((chunks, hidden, cells), BF16),
+            pltpu.VMEM((2, hidden, step), BF16),
+            pltpu.VMEM((2, hidden, step), BF16),
+            pltpu.VMEM((2, hidden, step), F32),
+            pltpu.VMEM((2, hidden, step), BF16),
+            pltpu.VMEM((2, hidden, step), BF16),
+            pltpu.VMEM((2, out_dim, step), BF16),
+        ],
+        compiler_params=pltpu.CompilerParams(vmem_limit_bytes=VMEM_BYTES),
+        name="all_cells",
+    )(place, gathered, *weights)
 
 
 def small_body(
@@ -357,16 +480,23 @@
     shape = jax.ShapeDtypeStruct
     params = pltpu.CompilerParams(vmem_limit_bytes=VMEM_BYTES)
 
+    def fetched(arrays):
+        buffers = [pltpu.VMEM(array.shape, array.dtype) for array in arrays]
+        return buffers, pltpu.SemaphoreType.DMA((len(arrays),))
+
+    inputs = (
+        adjoint, target_x[None, :], target_y[None, :], target_z[None, :], assignment[None, :],
+        level_codes[None, :], cell_params,
+    )
+    buffers, arrived = fetched(inputs)
     packed = pl.pallas_call(
         pack_kernel,
         out_shape=shape((16, cells + 128), BF16),
-        scratch_shapes=[pltpu.VMEM((128, 128), F32)],
-        compiler_params=params,
+        in_specs=[pl.BlockSpec(memory_space=pltpu.HBM)] * len(inputs),
+        scratch_shapes=buffers + [pltpu.VMEM((128, 128), F32), arrived],
+        compiler_params=pltpu.CompilerParams(vmem_limit_bytes=WHOLE_VMEM),
         name="pack_inputs",
-    )(
-        adjoint, target_x[None, :], target_y[None, :], target_z[None, :], assignment[None, :],
-        level_codes[None, :], cell_params,
-    )
+    )(*inputs)
     gathered = packed[None]
     reach = 1
     while reach < chunks:
@@ -374,8 +504,12 @@
         gathered = jnp.concatenate([gathered, moved], axis=0)
         reach *= 2
 
+    inputs = (level_table, w_proj, w_one, b_one[None, :], w_two, b_two[None, :], w_out)
+    buffers, arrived = fetched(inputs)
     first, second, bias, back_two, back_one, proj_rows, embed = pl.pallas_call(
         weight_kernel,
+        in_specs=[pl.BlockSpec(memory_space=pltpu.HBM)] * len(inputs),
+        scratch_shapes=buffers + [arrived],
         out_shape=(
             shape((hidden, 128), BF16),
             shape((hidden, hidden), BF16),
@@ -385,31 +519,15 @@
             shape((2 * props, hidden), BF16),
             shape((hidden, 128), BF16),
         ),
-        compiler_params=params,
+        compiler_params=pltpu.CompilerParams(vmem_limit_bytes=WHOLE_VMEM),
         name="prepare_weights",
-    )(level_table, w_proj, w_one, b_one[None, :], w_two, b_two[None, :], w_out)
+    )(*inputs)
 
     place = jnp.stack([lax.axis_index("cells"), lax.axis_index("freq")]).astype(jnp.int32)
-    step = min(256, cells)
-    targets = chunks * local
-    vmem = pl.BlockSpec(memory_space=pltpu.VMEM)
-    sums, grad_params = pl.pallas_call(
-        functools.partial(cell_kernel, freq_size, step),
-        out_shape=(
-            shape((hidden + 2 * freqs + 64, hidden), F32),
-            shape((props, cells), F32),
-        ),
-        in_specs=[pl.BlockSpec(memory_space=pltpu.SMEM)] + [vmem] * 7,
-        out_specs=(vmem, vmem),
-        scratch_shapes=[
-            pltpu.VMEM((5, targets, 128), F32),
-            pltpu.VMEM((2 * freqs, 2 * targets), BF16),
-            pltpu.VMEM((2 * targets, step), BF16),
-            pltpu.VMEM((chunks, hidden, cells), BF16),
-        ],
-        compiler_params=params,
-        name="all_cells",
-    )(place, gathered, first, second, bias, back_two, back_one, proj_rows)
+    sums, grad_params = run_cells(
+        place, gathered, first, second, bias, back_two, back_one, proj_rows,
+        step=min(512, cells), freq_size=freq_size, local=local,
+    )
 
     other = lax.ppermute(sums, "freq", [(at, at ^ 1) for at in range(freq_size)])
     scale = 1.0 / math.sqrt(cells * chunks * freq_size)
@@ -448,6 +566,8 @@
             and args[7].shape[0] == 16
             and args[8].shape[0] == 8
             and hidden % 128 == 0
+            and mesh.shape["freq"] * cells % SIDE == 0
+            and SIDE % cells == 0
             and args[13].shape[1] == 128
         )
         return (small_body if suits else general_body)(*args)

time: 47.5 us -> 30.6 us (0.64)
  Pallas kernels: 23.6 us -> 13 us
  local copies, waits for them, and re-layouts: 7.83 us -> 1.52 us
  waiting for transfers between devices: 7.13 us -> 6.16 us
  other arithmetic: 0.12 us -> 0.85 us
    pallas_call x3, Pallas kernels: 22.6 us -> 12 us  [the longest x1 8.35 us: run_cells(): pl.pallas_call(functools.partial(cell_kernel, freq_size, step), out_shape...]
    unnamed x28 -> x18, local copies, waits for them, and re-layouts: 7.83 us -> 1.52 us
    ppermute x3, waiting for transfers between devices: 5.32 us -> 4.34 us  [small_body(): lax.ppermute(gathered, 'cells', [(at, at ^ reach) for at in range(chunks)])]
    concatenate x3, other arithmetic: 0.05 us -> 0.77 us  [small_body(): gathered = jnp.concatenate([gathered, moved], axis=0)]
  transfers between devices with their start and end apart: 4 -> 4, of which waited for: 3 -> 3; matrix products, arithmetic and copies ran while one was open for 0% -> 0% of each run, Pallas kernels for 1% -> 7%
where the time goes in v2:
time: 30.6 us; the launch traced here: 30.3 us
  Pallas kernels  13 us (42%)
  starting transfers between devices  8.07 us (26%)
  waiting for transfers between devices  6.16 us (20%)
  local copies, waits for them, and re-layouts  1.52 us (5%)
  other arithmetic  0.85 us (3%)
  between operations  0.74 us (2%)
    pallas_call x1, Pallas kernels, run_cells(): pl.pallas_call(functools.partial(cell_kernel, freq_size, step), out_shape...  8.35 us
    ppermute x3, starting transfers between devices, small_body(): lax.ppermute(gathered, 'cells', [(at, at ^ reach) for at in range(chunks)])  8.06 us
    ppermute x3, waiting for transfers between devices, small_body(): lax.ppermute(gathered, 'cells', [(at, at ^ reach) for at in range(chunks)])  4.34 us
    pallas_call x1, Pallas kernels, small_body(): pl.pallas_call(weight_kernel, in_specs=[pl.BlockSpec(memory_space=pltpu.H...  2.08 us
    ppermute x1, waiting for transfers between devices, small_body(): lax.ppermute(sums, 'freq', [(at, at ^ 1) for at in range(freq_size)])  1.81 us
    pallas_call x1, Pallas kernels, small_body(): pl.pallas_call(pack_kernel, out_shape=shape((16, cells + 128), BF16), in_...  1.54 us
    unnamed x18, local copies, waits for them, and re-layouts  1.52 us
    pallas_call x1, Pallas kernels, small_body(): pl.pallas_call(functools.partial(finish_kernel, scale), out_shape=(shape(...  0.99 us
  transfers between devices with their start and end apart: 4, of which 3 were waited for; matrix products, arithmetic and copies ran while one was open for 0% of the time, Pallas kernels for 7%

profile of v2, /device:TPU:0, one launch (start us, length us, event | category | flops | bytes accessed | tf_op | source)
XLA Modules:
  0.0 30.3 jit_solution(12967278292798418617)
XLA Ops:
  0.6 1.5 %pack_inputs.1 = bf16[16,640]{1,0:T(8,128)(2,1)} custom-call(f32[2,16]{1,0:T(2,128)} %refs_0_.2, f32[1,16]{1,0:T(1,128)} %bitcast.19, f32[1,16]{1,0:T(1,128)} %bitcast.20, f32[1,16]{1,0:T(1,128)} %bitcast.21, s32[1,16]{1,0:T(1,128)} %bitcast.22, s32[1,512]{1,0:T(1,128)} %bitcast.16, bf16[8,512]{1,0:T(8,128)(2,1)} %refs_6_.2), custom_call_target="tpu_custom_call" | custom-call | tf_op jit(solution)/shard_map/pack_inputs/pallas_call | solution.py:492
  2.2 3.0 %collective-permute-start = (bf16[1,16,640]{2,1,0:T(8,128)(2,1)}, bf16[1,16,640]{2,1,0:T(8,128)(2,1)S(1)}, u32[]{:S(2)}, u32[]{:S(2)}) collective-permute-start(bf16[1,16,640]{2,1,0:T(8,128)(2,1)} %bitcast.12), channel_id=1, source_target_pairs={{0,2},{2,0},{4,6},{6,4},{8,10},{10,8},{12,14},{14,12},{1,3},{3,1},... | collective-permute-start | bytes 61448 | tf_op jit(solution)/shard_map/ppermute | solution.py:503
  5.2 2.0 %collective-permute-done = bf16[1,16,640]{2,1,0:T(8,128)(2,1)S(1)} collective-permute-done((bf16[1,16,640]{2,1,0:T(8,128)(2,1)}, bf16[1,16,640]{2,1,0:T(8,128)(2,1)S(1)}, u32[]{:S(2)}, u32[]{:S(2)}) %collective-permute-start) | collective-permute-done | bytes 20512 | tf_op jit(solution)/shard_map/ppermute | solution.py:503
  7.2 0.7 %pad_maximum_fusion.2 = bf16[2,16,640]{2,1,0:T(8,128)(2,1)S(1)} fusion(bf16[1,16,640]{2,1,0:T(8,128)(2,1)S(1)} %collective-permute-done, bf16[1,16,640]{2,1,0:T(8,128)(2,1)} %bitcast.13), kind=kLoop, calls=%fused_computation.2 | loop fusion | flops 20480 | bytes 81920 | tf_op jit(solution)/shard_map/concatenate | solution.py:504
  7.9 2.1 %collective-permute-start.1 = (bf16[2,16,640]{2,1,0:T(8,128)(2,1)S(1)}, bf16[2,16,640]{2,1,0:T(8,128)(2,1)S(1)}, u32[]{:S(2)}, u32[]{:S(2)}) collective-permute-start(bf16[2,16,640]{2,1,0:T(8,128)(2,1)S(1)} %pad_maximum_fusion.2), channel_id=1, source_target_pairs={{0,4},{2,6},{4,0},{6,2},{8,12},{10,14},{12,8},{14,10},{1,5},{3,7},... | collective-permute-start | bytes 122888 | tf_op jit(solution)/shard_map/ppermute | solution.py:503
  10.0 0.0 copy-start.8
  10.0 2.1 %prepare_weights.1 = (bf16[256,128]{1,0:T(8,128)(2,1)}, bf16[256,256]{1,0:T(8,128)(2,1)}, f32[256,128]{1,0:T(8,128)}, bf16[256,128]{1,0:T(8,128)(2,1)}, bf16[256...) custom-call(bf16[16,256]{1,0:T(8,128)(2,1)} %refs_0_.3, bf16[8,256]{1,0:T(8,128)(2,1)} %refs_1_.1, ...), custom_call_target="tpu_custom_call" | custom-call | tf_op jit(solution)/shard_map/prepare_weights/pallas_call | solution.py:509
  12.1 0.0 collective-permute-done.1
  12.1 0.0 copy-done.8
  12.1 0.0 copy-start.3
  12.2 3.0 %collective-permute-start.2 = (bf16[4,16,640]{2,1,0:T(8,128)(2,1)S(1)}, bf16[4,16,640]{2,1,0:T(8,128)(2,1)S(1)}, u32[]{:S(2)}, u32[]{:S(2)}) collective-permute-start(bf16[4,16,640]{2,1,0:T(8,128)(2,1)S(1)} %pad_maximum_fusion.1), channel_id=1, source_target_pairs={{0,8},{2,10},{4,12},{6,14},{8,0},{10,2},{12,4},{14,6},{1,9},{3,11}... | collective-permute-start | bytes 245768 | tf_op jit(solution)/shard_map/ppermute | solution.py:503
  15.1 0.1 pad_add_fusion.place_ref
  15.2 0.0 copy-start.1
  15.2 0.0 copy-start.2
  15.2 0.0 copy-start.5
  15.2 2.4 %collective-permute-done.2 = bf16[4,16,640]{2,1,0:T(8,128)(2,1)S(1)} collective-permute-done((bf16[4,16,640]{2,1,0:T(8,128)(2,1)S(1)}, bf16[4,16,640]{2,1,0:T(8,128)(2,1)S(1)}, u32[]{:S(2)}, u32[]{:S(2)}) %collective-permute-start.2) | collective-permute-done | bytes 81952 | tf_op jit(solution)/shard_map/ppermute | solution.py:503
  17.6 0.0 copy-start.7
  17.6 0.0 copy-done.3
  17.6 0.0 copy-done.1
  17.6 0.0 copy-done.2
  17.6 0.0 copy-done.5
  17.6 0.6 %copy-done.7 = bf16[16,256]{1,0:T(8,128)(2,1)S(1)} copy-done((bf16[16,256]{1,0:T(8,128)(2,1)S(1)}, bf16[16,256]{1,0:T(8,128)(2,1)}, u32[]{:S(2)}) %copy-start.7) | copy-done | bytes 8216
  18.3 0.0 copy-start.6
  18.3 0.8 %copy-done.6 = bf16[256,128]{1,0:T(8,128)(2,1)S(1)} copy-done((bf16[256,128]{1,0:T(8,128)(2,1)S(1)}, bf16[256,128]{1,0:T(8,128)(2,1)}, u32[]{:S(2)}) %copy-start.6) | copy-done | bytes 65560
  19.1 0.0 copy-start
  19.1 0.0 copy-start.4
  19.1 8.4 %all_cells.1 = (f32[448,256]{1,0:T(8,128)S(1)}, f32[8,512]{1,0:T(8,128)}) custom-call(s32[2]{0:T(128)S(1)} %pad_add_fusion.place_ref, bf16[8,16,640]{2,1,0:T(8,128)(2,1)S(1)} %pad_maximum_fusion.gathered_ref, bf16[256,128]{1,0:T(8,128)(2,1)S(1)} %copy-done.5, bf16[256,256]{1,0:T(8,128)(2,1)S(1)} %copy-done.1, f32[256,128]{1,0:T(8,128)S(1)} %copy-done.2, ...), custom_call_target="tpu_custom_call" | custom-call | tf_op jit(solution)/shard_map/all_cells/pallas_call | solution.py:431
  27.5 0.0 collective-permute-start.3
  27.5 1.8 %collective-permute-done.3.other_ref = f32[448,256]{1,0:T(8,128)S(1)} collective-permute-done((f32[448,256]{1,0:T(8,128)S(1)}, f32[448,256]{1,0:T(8,128)S(1)}, u32[]{:S(2)}, u32[]{:S(2)}) %collective-permute-start.3) | collective-permute-done | bytes 458784 | tf_op jit(solution)/shard_map/ppermute | solution.py:532
  29.3 0.0 copy-done
  29.3 0.0 copy-done.4
  29.3 1.0 %finish_sums.1 = (f32[256,128]{1,0:T(8,128)}, f32[256,256]{1,0:T(8,128)}, f32[1,256]{1,0:T(1,128)}, f32[256,256]{1,0:T(8,128)}, f32[1,256]{1,0:T(1,128)}, /*index=5*/f32[16,256]{1,0:T(8,128)}, f32[8,256]{1,0:T(8,128)}) custom-call(f32[448,256]{1,0:T(8,128)S(1)} %get-tuple-element.30.own_ref, f32[448,256]{1,0:T(8,128)S(1)} %collective-permute-done.3.other_ref, ...), custom_call_target="tpu_custom_call" | custom-call | tf_op jit(solution)/shard_map/finish_sums/pallas_call | solution.py:534
  (2 shorter events, 0.0 us)
Async XLA Ops:
  2.2 5.0 %collective-permute-start = (bf16[1,16,640]{2,1,0:T(8,128)(2,1)}, bf16[1,16,640]{2,1,0:T(8,128)(2,1)S(1)}, u32[]{:S(2)}, u32[]{:S(2)}) collective-permute-start(bf16[1,16,640]{2,1,0:T(8,128)(2,1)} %bitcast.12), channel_id=1, source_target_pairs={{0,2},{2,0},{4,6},{6,4},{8,10},{10,8},{12,14},{14,12},{1,3},{3,1},... | collective-permute-start | bytes 61448 | tf_op jit(solution)/shard_map/ppermute | solution.py:503
  7.9 4.2 %collective-permute-start.1 = (bf16[2,16,640]{2,1,0:T(8,128)(2,1)S(1)}, bf16[2,16,640]{2,1,0:T(8,128)(2,1)S(1)}, u32[]{:S(2)}, u32[]{:S(2)}) collective-permute-start(bf16[2,16,640]{2,1,0:T(8,128)(2,1)S(1)} %pad_maximum_fusion.2), channel_id=1, source_target_pairs={{0,4},{2,6},{4,0},{6,2},{8,12},{10,14},{12,8},{14,10},{1,5},{3,7},... | collective-permute-start | bytes 122888 | tf_op jit(solution)/shard_map/ppermute | solution.py:503
  10.0 2.1 %copy-start.8 = (bf16[16,640]{1,0:T(8,128)(2,1)S(1)}, bf16[16,640]{1,0:T(8,128)(2,1)}, u32[]{:S(2)}) copy-start(bf16[16,640]{1,0:T(8,128)(2,1)} %pack_inputs.1) | copy-start | bytes 61444
  12.1 5.5 %copy-start.3 = (bf16[256,256]{1,0:T(8,128)(2,1)S(1)}, bf16[256,256]{1,0:T(8,128)(2,1)}, u32[]{:S(2)}) copy-start(bf16[256,256]{1,0:T(8,128)(2,1)} %get-tuple-element.28.back_one_ref) | copy-start | bytes 393220
  12.2 5.4 %collective-permute-start.2 = (bf16[4,16,640]{2,1,0:T(8,128)(2,1)S(1)}, bf16[4,16,640]{2,1,0:T(8,128)(2,1)S(1)}, u32[]{:S(2)}, u32[]{:S(2)}) collective-permute-start(bf16[4,16,640]{2,1,0:T(8,128)(2,1)S(1)} %pad_maximum_fusion.1), channel_id=1, source_target_pairs={{0,8},{2,10},{4,12},{6,14},{8,0},{10,2},{12,4},{14,6},{1,9},{3,11}... | collective-permute-start | bytes 245768 | tf_op jit(solution)/shard_map/ppermute | solution.py:503
  15.2 2.4 %copy-start.1 = (bf16[256,256]{1,0:T(8,128)(2,1)S(1)}, bf16[256,256]{1,0:T(8,128)(2,1)}, u32[]{:S(2)}) copy-start(bf16[256,256]{1,0:T(8,128)(2,1)} %get-tuple-element.25.second_ref) | copy-start | bytes 393220
  15.2 2.4 %copy-start.2 = (f32[256,128]{1,0:T(8,128)S(1)}, f32[256,128]{1,0:T(8,128)}, u32[]{:S(2)}) copy-start(f32[256,128]{1,0:T(8,128)} %get-tuple-element.26.bias_ref) | copy-start | bytes 393220
  15.2 2.4 %copy-start.5 = (bf16[256,128]{1,0:T(8,128)(2,1)S(1)}, bf16[256,128]{1,0:T(8,128)(2,1)}, u32[]{:S(2)}) copy-start(bf16[256,128]{1,0:T(8,128)(2,1)} %get-tuple-element.24.first_ref) | copy-start | bytes 196612
  17.6 0.7 %copy-start.7 = (bf16[16,256]{1,0:T(8,128)(2,1)S(1)}, bf16[16,256]{1,0:T(8,128)(2,1)}, u32[]{:S(2)}) copy-start(bf16[16,256]{1,0:T(8,128)(2,1)} %get-tuple-element.29.params_ref) | copy-start | bytes 24580
  18.3 0.8 %copy-start.6 = (bf16[256,128]{1,0:T(8,128)(2,1)S(1)}, bf16[256,128]{1,0:T(8,128)(2,1)}, u32[]{:S(2)}) copy-start(bf16[256,128]{1,0:T(8,128)(2,1)} %get-tuple-element.27.back_two_ref) | copy-start | bytes 196612
  19.1 10.2 %copy-start = (bf16[256,256]{1,0:T(8,128)(2,1)S(1)}, bf16[256,256]{1,0:T(8,128)(2,1)}, u32[]{:S(2)}) copy-start(bf16[256,256]{1,0:T(8,128)(2,1)} %w1_ref.1) | copy-start | bytes 393220
  19.1 10.2 %copy-start.4 = (bf16[256,128]{1,0:T(8,128)(2,1)S(1)}, bf16[256,128]{1,0:T(8,128)(2,1)}, u32[]{:S(2)}) copy-start(bf16[256,128]{1,0:T(8,128)(2,1)} %get-tuple-element.31.embed_ref) | copy-start | bytes 196612
  27.5 1.8 %collective-permute-start.3 = (f32[448,256]{1,0:T(8,128)S(1)}, f32[448,256]{1,0:T(8,128)S(1)}, u32[]{:S(2)}, u32[]{:S(2)}) collective-permute-start(f32[448,256]{1,0:T(8,128)S(1)} %get-tuple-element.30.own_ref), channel_id=1, source_target_pairs={{0,1},{1,0},{2,3},{3,2},{4,5},{5,4},{6,7},{7,6},{8,9},{9,8},{10,11... | collective-permute-start | bytes 1376264 | tf_op jit(solution)/shard_map/ppermute | solution.py:532

commit v3 on v2

v3 whole, which is shorter than its diff:
```python
import functools
import math

import jax
import jax.numpy as jnp
from jax import lax
from jax.experimental import pallas as pl
from jax.experimental.pallas import tpu as pltpu
from jax.sharding import PartitionSpec as P

SIDE = 1024

wave_low = 1.0
wave_high = 3.0
kernel_gain = 150.0

F32 = jnp.float32
BF16 = jnp.bfloat16
VMEM_BYTES = 40 * 1024 * 1024
WHOLE_VMEM = 64 * 1024 * 1024 - 256 * 1024


def silu_slope(value):
    sigma = jax.nn.sigmoid(value)
    return sigma * (1.0 + value * (1.0 - sigma))


def contract(left, right, left_dim, right_dim):
    return lax.dot_general(
        left, right, (((left_dim,), (right_dim,)), ((), ())), preferred_element_type=jnp.float32
    )


def kernel_tile(point_x, point_y, point_z, freq_value, cell_col, cell_row, count_freq):
    wave = wave_low + (wave_high - wave_low) * freq_value / (count_freq - 1)
    offset_x = point_x[:, None] - cell_col[None, :]
    offset_y = point_y[:, None] - cell_row[None, :]
    square = offset_x * offset_x + offset_y * offset_y + (point_z * point_z)[:, None]
    distance = jnp.sqrt(square)
    amplitude = kernel_gain * point_z[:, None] / square
    phase = wave[:, None] * distance
    return (
        (amplitude * jnp.cos(phase)).astype(jnp.bfloat16),
        (amplitude * jnp.sin(phase)).astype(jnp.bfloat16),
    )


def forward_pass(level_codes, cell_params, level_table, w_proj, w_one, b_one, w_two, b_two):
    levels = level_table.shape[0]
    onehot = (level_codes[:, None] == jnp.arange(levels, dtype=jnp.int32)[None, :]).astype(
        jnp.bfloat16
    )
    hidden_in = (
        jnp.dot(onehot, level_table, preferred_element_type=jnp.float32)
        + contract(cell_params, w_proj, 0, 0)
    ).astype(jnp.bfloat16)
    pre_one = jnp.dot(hidden_in, w_one, preferred_element_type=jnp.float32) + b_one
    act_one = jax.nn.silu(pre_one).astype(jnp.bfloat16)
    pre_two = jnp.dot(act_one, w_two, preferred_element_type=jnp.float32) + b_two
    act_two = jax.nn.silu(pre_two).astype(jnp.bfloat16)
    return (onehot, hidden_in, pre_one, act_one, pre_two, act_two)


def upper_grads(spectra, w_out, act_one, pre_two, act_two):
    back_two = contract(spectra, w_out, 0, 1)
    delta_two = (back_two * silu_slope(pre_two)).astype(jnp.bfloat16)
    grad_out = contract(act_two, spectra, 0, 1)
    grad_w2 = contract(act_one, delta_two, 0, 0)
    grad_b2 = jnp.sum(delta_two.astype(jnp.float32), axis=0)
    return ((grad_out, grad_w2, grad_b2), delta_two)


def lower_grads(delta_two, w_two, w_one, pre_one, hidden_in, onehot, cell_params, w_proj):
    back_one = contract(delta_two, w_two, 1, 1)
    delta_one = (back_one * silu_slope(pre_one)).astype(jnp.bfloat16)
    grad_w1 = contract(hidden_in, delta_one, 0, 0)
    grad_b1 = jnp.sum(delta_one.astype(jnp.float32), axis=0)
    back_zero = contract(delta_one, w_one, 1, 1).astype(jnp.bfloat16)
    grad_table = contract(onehot, back_zero, 0, 0)
    grad_proj = contract(cell_params, back_zero, 1, 0)
    grad_params = contract(w_proj, back_zero, 1, 1)
    return ((grad_w1, grad_b1, grad_table, grad_proj), grad_params)


def general_body(
    adjoint,
    target_x,
    target_y,
    target_z,
    assignment,
    level_codes,
    cell_params,
    level_table,
    w_proj,
    w_one,
    b_one,
    w_two,
    b_two,
    w_out,
):
    cell_count = level_codes.shape[0]
    freq_count = w_out.shape[1] // 2
    freq_size = lax.axis_size("freq")
    cell_rank = lax.axis_index("cells")
    freq_rank = lax.axis_index("freq")
    first_cell = (cell_rank * freq_size + freq_rank) * cell_count
    index = first_cell + jnp.arange(cell_count, dtype=jnp.int32)
    cell_col = (index % SIDE).astype(jnp.float32)
    cell_row = (index // SIDE).astype(jnp.float32)
    freq_grid = jnp.arange(freq_count, dtype=jnp.int32).astype(jnp.float32)
    stacked = jnp.concatenate(
        [
            adjoint,
            target_x[None, :],
            target_y[None, :],
            target_z[None, :],
            assignment.astype(jnp.float32)[None, :],
        ],
        axis=0,
    )
    total = jnp.zeros((2 * freq_count, cell_count), jnp.float32)
    piece = lax.all_gather(stacked, "cells", axis=1, tiled=True)
    length = piece.shape[1]
    block_len = math.gcd(length, 256)
    sections = piece.reshape(6, length // block_len, block_len).transpose(1, 0, 2)

    def inner(accum, rows):
        adj_round = rows[0:2].astype(jnp.bfloat16)
        kre, kim = kernel_tile(rows[2], rows[3], rows[4], rows[5], cell_col, cell_row, freq_count)
        select = (rows[5][:, None] == freq_grid[None, :]).astype(jnp.bfloat16)
        part_a = select * adj_round[0][:, None]
        part_b = select * adj_round[1][:, None]
        left_re = jnp.concatenate([part_a, part_b], axis=1)
        left_im = jnp.concatenate([part_b, -part_a], axis=1)
        return (accum + contract(left_re, kre, 0, 0) + contract(left_im, kim, 0, 0), None)

    total, unused = lax.scan(inner, total, sections)
    local_spec = total.astype(jnp.bfloat16)
    scale = 1.0 / math.sqrt(cell_count * lax.axis_size("cells") * freq_size)
    onehot, hidden_in, pre_one, act_one, pre_two, act_two = forward_pass(
        level_codes, cell_params, level_table, w_proj, w_one, b_one, w_two, b_two
    )
    upper, delta_two = upper_grads(local_spec, w_out, act_one, pre_two, act_two)
    lower, grad_params = lower_grads(
        delta_two, w_two, w_one, pre_one, hidden_in, onehot, cell_params, w_proj
    )
    totals = lax.psum(tuple(term * scale for term in upper + lower), ("cells", "freq"))
    return totals + (grad_params,)


def split(value, parts):
    pieces = []
    for _ in range(parts):
        piece = value.astype(BF16)
        pieces.append(piece.astype(F32))
        value = value - piece.astype(F32)
    return pieces


def fetch(sources, buffers, arrived):
    copies = [
        pltpu.make_async_copy(source, buffer, arrived.at[at])
        for at, (source, buffer) in enumerate(zip(sources, buffers))
    ]
    for copy in copies:
        copy.start()
    for copy in copies:
        copy.wait()


def pack_kernel(*refs):
    sources, out_ref, buffers, (rows, arrived) = refs[:7], refs[7], refs[8:15], refs[15:]
    fetch(sources, buffers, arrived)
    adj_ref, x_ref, y_ref, z_ref, assign_ref, codes_ref, params_ref = buffers
    cells = codes_ref.shape[1]
    pieces = [adj_ref[0:1], adj_ref[1:2]]
    for ref in (x_ref, y_ref, z_ref):
        pieces += split(ref[...], 3)
    pieces.append(assign_ref[...].astype(F32))
    pieces += [jnp.zeros_like(pieces[0])] * 4
    codes = codes_ref[...].astype(F32)
    for at in range(4):
        rows[at : at + 1] = codes[:, at * 128 : (at + 1) * 128]
    rows[4:5] = jnp.concatenate(pieces[0:8], axis=1)
    rows[5:6] = jnp.concatenate(pieces[8:16], axis=1)
    rows[6:8] = jnp.zeros((2, 128), F32)
    out_ref[:, 0:cells] = params_ref[...]
    out_ref[:, cells:] = rows[...].astype(BF16)


def stage_kernel(packed_ref, out_ref):
    out_ref[...] = packed_ref[...]


def weight_kernel(joint_ref, embed_ref, bias_ref, out_ref):
    hidden = joint_ref.shape[0]
    used = embed_ref.shape[0]
    stack = embed_ref[...]
    joined = jnp.dot(stack, joint_ref[:, 0:hidden], preferred_element_type=F32)
    joined = jnp.concatenate([joined, bias_ref[0:1], jnp.zeros((7, hidden), F32)], axis=0)
    shifts = split(0.5 * bias_ref[1:2], 3)
    rows = split(0.5 * joined, 3) + shifts + [jnp.zeros((29, hidden), F32)]
    out_ref[:, 0:128] = jnp.concatenate(rows, axis=0).T.astype(BF16)
    second = joint_ref[:, hidden : 2 * hidden].astype(F32)
    out_ref[:, 128 : 128 + hidden] = (0.5 * second).T.astype(BF16)
    filled = [stack.astype(F32), jnp.zeros((8, hidden), F32)]
    rows = filled * 3 + [jnp.zeros((32, hidden), F32)]
    out_ref[:, 128 + hidden :] = jnp.concatenate(rows, axis=0).T.astype(BF16)


SINE = (3.1415820121765137, -5.167142868041992, 2.5418989658355713, -0.5546361804008484)
COSINE = (-4.934795379638672, 4.058451175689697, -1.3320938348770142, 0.22008062899112701)


def dot(left, right):
    return jnp.dot(left, right, preferred_element_type=F32)


def feature_of(gathered_ref, slot):
    width = gathered_ref.shape[2]
    cells = width - 128
    rows = gathered_ref[slot, :, cells:].astype(F32)
    codes = jnp.concatenate(
        [jnp.broadcast_to(rows[at : at + 1], (8, 128)) for at in range(4)], axis=1
    )
    steps = lax.broadcasted_iota(jnp.int32, (8, cells), 0).astype(F32)
    blocks = [
        jnp.where(codes == steps, 1.0, 0.0),
        jnp.where(codes == steps + 8.0, 1.0, 0.0),
        gathered_ref[slot, :, 0:cells].astype(F32),
        jnp.where(steps == 0.0, 1.0, 0.0),
    ]
    return jnp.concatenate(blocks, axis=0).astype(BF16)


def activate(half):
    tanh = jnp.tanh(half)
    gate = 1.0 + tanh
    act = half * gate
    return act.astype(BF16), gate + act * (1.0 - tanh)


def layer_one(weights_ref, feature):
    rows = [feature] * 3 + [jnp.zeros((32, feature.shape[1]), BF16)]
    return dot(weights_ref[:, 0:128], jnp.concatenate(rows, axis=0))


def bias_of(weights_ref):
    shift = weights_ref[:, 96:128].astype(F32)
    shift = (shift[:, 0:1] + shift[:, 1:2]) + shift[:, 2:3]
    return jnp.broadcast_to(shift, (shift.shape[0], 128))


def forward_kernel(gathered_ref, weights_ref, one_ref, slope_one_ref, two_ref, slope_two_ref, bias):
    count, hidden, cells = one_ref.shape
    bias[...] = bias_of(weights_ref)
    wide = jnp.concatenate([bias[...]] * (cells // 128), axis=1)

    def first(slot):
        act, slope = activate(layer_one(weights_ref, feature_of(gathered_ref, slot)))
        one_ref[slot] = act
        slope_one_ref[slot] = slope

    def second(slot):
        half = dot(weights_ref[:, 128 : 128 + hidden], one_ref[slot]) + wide
        act, slope = activate(half)
        two_ref[slot] = act
        slope_two_ref[slot] = slope

    first(0)
    for slot in range(1, count):
        second(slot - 1)
        first(slot)
    second(count - 1)


def cell_kernel(
    freq_size,
    place_ref, gathered_ref, weights_ref, joint_ref,
    one_ref, slope_one_ref, two_ref, slope_two_ref,
    sums_ref, grad_params_ref,
    across, where, lift, bias, totals, waves, deltas,
    act_one, act_kept, slope_one, act_two, delta_two, spectra,
):
    chunks, _, width = gathered_ref.shape
    cells = width - 128
    hidden = joint_ref.shape[0]
    freqs = (joint_ref.shape[1] - 2 * hidden) // 2
    w2_ref = joint_ref.at[:, hidden : 2 * hidden]
    wo_ref = joint_ref.at[:, 2 * hidden :]
    targets = chunks * 16
    me = place_ref[0]
    freq_rank = place_ref[1]
    stride = freq_size * cells
    second_ref = weights_ref.at[:, 128 : 128 + hidden]

    rows = [gathered_ref[chunk ^ me, :, cells:].astype(F32) for chunk in range(chunks)]
    low = jnp.concatenate([row[4:5] for row in rows], axis=0).T
    high = jnp.concatenate([row[5:6] for row in rows], axis=0).T
    parts = [low[at * 16 : (at + 1) * 16] for at in range(8)]
    parts += [high[at * 16 : (at + 1) * 16] for at in range(4)]
    point_x = (parts[2] + parts[3]) + parts[4]
    point_y = (parts[5] + parts[6]) + parts[7]
    point_z = (parts[8] + parts[9]) + parts[10]
    wave = (wave_low + (wave_high - wave_low) * parts[11] / (freqs - 1)) * (0.5 / math.pi)
    sides = [
        freq_rank * cells + lane + lax.broadcasted_iota(jnp.int32, (1, 128), 1)
        for lane in range(0, cells, 128)
    ]
    sides = [lax.rem(side, SIDE).astype(F32) for side in sides]
    grid = lax.broadcasted_iota(jnp.int32, (16, freqs), 1).astype(F32)
    near, far = [], []
    for chunk in range(chunks):
        here = slice(chunk * 16, chunk * 16 + 16)

        def spread(value):
            return jnp.broadcast_to(value[:, chunk : chunk + 1], (16, 128))

        where[0, here] = spread(point_y)
        where[1, here] = spread(point_z * point_z)
        where[2, here] = spread(wave)
        where[3, here] = spread(kernel_gain * point_z)
        wide = spread(point_x)
        for at, side in enumerate(sides):
            offset = wide - side
            across[here, at * 128 : (at + 1) * 128] = offset * offset
        select = jnp.where(spread(parts[11])[:, 0:freqs] == grid, 1.0, 0.0)
        part_a = select * spread(parts[0])[:, 0:freqs]
        part_b = select * spread(parts[1])[:, 0:freqs]
        near.append(jnp.concatenate([part_a, part_b], axis=1))
        far.append(jnp.concatenate([part_b, -part_a], axis=1))
    lift[:, 0:targets] = jnp.concatenate(near, axis=0).T.astype(BF16)
    lift[:, targets:] = jnp.concatenate(far, axis=0).T.astype(BF16)
    bias[...] = bias_of(weights_ref)
    totals[...] = jnp.zeros_like(totals)

    top = hidden + 2 * freqs
    ready = one_ref.shape[0]

    def place(block):
        slot = (block // ready) * ready + lax.bitwise_and(lax.bitwise_xor(me, block), ready - 1)
        return slot, lax.bitwise_xor(slot, me)

    def holograms(block, even):
        chunk = place(block)[1]
        row = ((chunk * stride + freq_rank * cells) // SIDE).astype(F32)
        for at in range(0, targets, 16):
            here = slice(at, at + 16)
            offset = where[0, here] - row
            rest = offset * offset + where[1, here]
            for lane in range(0, cells, 128):
                square = across[here, lane : lane + 128] + rest
                inverse = lax.rsqrt(square)
                turns = where[2, here] * (square * inverse)
                part = turns - jnp.round(turns)
                power = part * part
                sine = part * (((SINE[3] * power + SINE[2]) * power + SINE[1]) * power + SINE[0])
                cosine = (COSINE[2] * power + COSINE[1]) * power + COSINE[0]
                cosine = cosine * power + 1.0
                amplitude = where[3, here] * (inverse * inverse)
                twice = (amplitude + amplitude) * sine
                waves[even, at : at + 16, lane : lane + 128] = (amplitude - twice * sine).astype(BF16)
                waves[even, targets + at : targets + at + 16, lane : lane + 128] = (
                    twice * cosine
                ).astype(BF16)
                yield

    def kept(block, even):
        if block < ready:
            slot = place(block)[0]
            refs = (one_ref, slope_one_ref, two_ref, slope_two_ref)
            return [ref.at[slot] for ref in refs]
        return act_kept.at[even], slope_one.at[even], act_two.at[even], None

    def lower(block, even):
        slot, chunk = place(block)
        total = totals.at[chunk // ready]

        def outer(low, left, right):
            total[low : low + left.shape[0]] += contract(left, right, 1, 1)

        one, slope, two, _ = kept(block, even)
        feature = feature_of(gathered_ref, slot)
        delta = delta_two[even]
        back = dot(w2_ref[...], delta)
        yield
        value = (back * slope[...]).astype(BF16)
        deltas[chunk] = value
        yield
        outer(0, one[...], delta)
        yield
        outer(hidden, spectra[even], two[...])
        yield
        outer(top + 32, feature, delta)
        outer(top, feature, value)
        yield

    def upper(block, even):
        spectrum = dot(lift[...], waves[even]).astype(BF16)
        spectra[even] = spectrum
        yield
        if block < ready:
            back = dot(wo_ref[...], spectrum)
            yield
            delta_two[even] = (back * kept(block, even)[3][...]).astype(BF16)
            yield
            return
        act = act_one[even]
        act_kept[even] = act
        half = dot(second_ref[...], act)
        half = half + jnp.concatenate([bias[...]] * (cells // 128), axis=1)
        yield
        back = dot(wo_ref[...], spectrum)
        yield
        act, slope = activate(half)
        act_two[even] = act
        yield
        delta_two[even] = (back * slope).astype(BF16)
        yield

    def begin(block, even):
        if block >= ready:
            half = layer_one(weights_ref, feature_of(gathered_ref, place(block)[0]))
            yield
            act, slope = activate(half)
            act_one[even] = act
            slope_one[even] = slope
            yield

    stages = (begin, upper, lower)
    for at in range(chunks + 2):
        live = [lag for lag in (2, 1, 0) if 0 <= at - lag < chunks]
        waiting = [stages[lag](at - lag, (at - lag) % 2) for lag in live]
        spots = sum(5 if lag == 2 else ((5, 3), (2, 0))[1 - lag][at - lag < ready] for lag in live)
        pieces = (targets // 16) * (cells // 128) if 0 in live else 0
        extra = holograms(at, at % 2)
        done, drawn = 0, 0
        while waiting:
            for stage in list(waiting):
                if next(stage, True) is True:
                    waiting.remove(stage)
                    continue
                done += 1
                while drawn < pieces * done // spots:
                    next(extra)
                    drawn += 1
        if pieces:
            for _ in extra:
                pass
    both = contract(weights_ref[:, 0:128], deltas[me], 0, 0)
    grad_params_ref[...] = 0.5 * ((both[16:24] + both[48:56]) + both[80:88])
    sums_ref[...] = (totals[0] + totals[1]).astype(BF16)


def finish_kernel(
    scale, own_ref, other_ref, weights_ref, joint_ref,
    out_ref, w2_ref, b2_ref, wone_ref, b1_ref, table_ref, proj_ref,
):
    hidden = joint_ref.shape[0]
    top = hidden + out_ref.shape[1]
    levels = table_ref.shape[0]
    used = levels + proj_ref.shape[0]

    def total(low, high, factor):
        both = own_ref[low:high].astype(F32) + other_ref[low:high].astype(F32)
        return both * (scale * factor)

    w2_ref[...] = total(0, hidden, 0.5)
    out_ref[...] = total(hidden, top, 1.0).T
    feature = total(top, top + 32, 0.25)
    b1_ref[...] = feature[used : used + 1]
    b2_ref[...] = total(top + 32, top + 64, 0.5)[used : used + 1]
    rows = jnp.concatenate(split(feature, 3), axis=0).astype(BF16)
    embed = weights_ref[:, 128 + hidden : 128 + hidden + 96]
    wone_ref[...] = jnp.dot(embed, rows, preferred_element_type=F32)
    back = contract(rows, joint_ref[:, 0:hidden], 1, 1)
    back = (back[0:32] + back[32:64]) + back[64:96]
    table_ref[...] = back[0:levels]
    proj_ref[...] = back[levels:used]


def run_forward(gathered, weights):
    count, _, width = gathered.shape
    hidden = weights.shape[0]
    block = (count, hidden, width - 128)
    return pl.pallas_call(
        forward_kernel,
        out_shape=[jax.ShapeDtypeStruct(block, kind) for kind in (BF16, F32, BF16, F32)],
        scratch_shapes=[pltpu.VMEM((hidden, 128), F32)],
        compiler_params=pltpu.CompilerParams(vmem_limit_bytes=VMEM_BYTES),
        name="early_forward",
    )(gathered, weights)


def run_cells(place, gathered, weights, joint, early, freq_size):
    chunks, props, width = gathered.shape
    cells = width - 128
    hidden = joint.shape[0]
    out_dim = joint.shape[1] - 2 * hidden
    targets = chunks * 16
    vmem = pl.BlockSpec(memory_space=pltpu.VMEM)
    return pl.pallas_call(
        functools.partial(cell_kernel, freq_size),
        out_shape=(
            jax.ShapeDtypeStruct((hidden + out_dim + 64, hidden), BF16),
            jax.ShapeDtypeStruct((props, cells), F32),
        ),
        in_specs=[pl.BlockSpec(memory_space=pltpu.SMEM)] + [vmem] * 7,
        out_specs=(vmem, vmem),
        scratch_shapes=[
            pltpu.VMEM((targets, cells), F32),
            pltpu.VMEM((4, targets, 128), F32),
            pltpu.VMEM((out_dim, 2 * targets), BF16),
            pltpu.VMEM((hidden, 128), F32),
            pltpu.VMEM((2, hidden + out_dim + 64, hidden), F32),
            pltpu.VMEM((2, 2 * targets, cells), BF16),
            pltpu.VMEM((chunks, hidden, cells), BF16),
            pltpu.VMEM((2, hidden, cells), BF16),
            pltpu.VMEM((2, hidden, cells), BF16),
            pltpu.VMEM((2, hidden, cells), F32),
            pltpu.VMEM((2, hidden, cells), BF16),
            pltpu.VMEM((2, hidden, cells), BF16),
            pltpu.VMEM((2, out_dim, cells), BF16),
        ],
        compiler_params=pltpu.CompilerParams(vmem_limit_bytes=VMEM_BYTES),
        name="all_cells",
    )(place, gathered, weights, joint, *early)


def small_body(
    adjoint,
    target_x,
    target_y,
    target_z,
    assignment,
    level_codes,
    cell_params,
    level_table,
    w_proj,
    w_one,
    b_one,
    w_two,
    b_two,
    w_out,
):
    cells = level_codes.shape[0]
    local = target_x.shape[0]
    levels, hidden = level_table.shape
    props = w_proj.shape[0]
    freqs = w_out.shape[1] // 2
    chunks = lax.axis_size("cells")
    freq_size = lax.axis_size("freq")
    shape = jax.ShapeDtypeStruct
    params = pltpu.CompilerParams(vmem_limit_bytes=VMEM_BYTES)

    def fetched(arrays):
        buffers = [pltpu.VMEM(array.shape, array.dtype) for array in arrays]
        return buffers, pltpu.SemaphoreType.DMA((len(arrays),))

    inputs = (
        adjoint, target_x[None, :], target_y[None, :], target_z[None, :], assignment[None, :],
        level_codes[None, :], cell_params,
    )
    whole = pltpu.CompilerParams(vmem_limit_bytes=WHOLE_VMEM)
    buffers, arrived = fetched(inputs)
    packed = pl.pallas_call(
        pack_kernel,
        out_shape=shape((props, cells + 128), BF16),
        in_specs=[pl.BlockSpec(memory_space=pltpu.HBM)] * len(inputs),
        scratch_shapes=buffers + [pltpu.VMEM((8, 128), F32), arrived],
        compiler_params=whole,
        name="pack_inputs",
    )(*inputs)
    staged = pl.pallas_call(
        stage_kernel,
        out_shape=shape((props, cells + 128), BF16),
        compiler_params=params,
        name="stage_own",
    )(packed)
    moved = lax.ppermute(packed[None], "cells", [(at, at ^ 1) for at in range(chunks)])
    embed = jnp.concatenate([level_table, w_proj], axis=0)
    biases = jnp.concatenate([b_one[None, :], b_two[None, :]], axis=0)
    gathered = jnp.concatenate([staged[None], moved], axis=0)
    gathered, embed, biases, w_one, w_two, w_out = lax.optimization_barrier(
        (gathered, embed, biases, w_one, w_two, w_out)
    )
    joint = jnp.concatenate([w_one, w_two, w_out], axis=1)
    weights = pl.pallas_call(
        weight_kernel,
        out_shape=shape((hidden, 256 + hidden), BF16),
        compiler_params=params,
        name="prepare_weights",
    )(joint, embed, biases)
    reach = 2
    while reach < chunks:
        moved = lax.ppermute(gathered, "cells", [(at, at ^ reach) for at in range(chunks)])
        if 2 * reach == chunks:
            early = run_forward(gathered, weights)
        gathered = jnp.concatenate([gathered, moved], axis=0)
        gathered, weights = lax.optimization_barrier((gathered, weights))
        reach *= 2

    place = jnp.stack([lax.axis_index("cells"), lax.axis_index("freq")]).astype(jnp.int32)
    sums, grad_params = run_cells(place, gathered, weights, joint, early, freq_size)

    other = lax.ppermute(sums, "freq", [(at, at ^ 1) for at in range(freq_size)])
    scale = 1.0 / math.sqrt(cells * chunks * freq_size)
    grad_out, grad_w2, grad_b2, grad_w1, grad_b1, grad_table, grad_proj = pl.pallas_call(
        functools.partial(finish_kernel, scale),
        out_shape=(
            shape((hidden, 2 * freqs), F32),
            shape((hidden, hidden), F32),
            shape((1, hidden), F32),
            shape((hidden, hidden), F32),
            shape((1, hidden), F32),
            shape((levels, hidden), F32),
            shape((props, hidden), F32),
        ),
        compiler_params=params,
        name="finish_sums",
    )(sums, other, weights, joint)
    return (
        grad_out, grad_w2, grad_b2[0], grad_w1, grad_b1[0], grad_table, grad_proj, grad_params,
    )


def solution(mesh):
    chunks = mesh.shape["cells"]
    paired = mesh.shape["freq"] == 2 and chunks > 2 and chunks & (chunks - 1) == 0

    def body(*args):
        local = args[1].shape[0]
        cells = args[5].shape[0]
        hidden = args[9].shape[0]
        suits = (
            paired
            and local == 16
            and cells == 512
            and chunks * cells * chunks * local <= 1 << 20
            and args[7].shape[0] == 16
            and args[8].shape[0] == 8
            and hidden % 128 == 0
            and mesh.shape["freq"] * cells % SIDE == 0
            and SIDE % cells == 0
            and args[13].shape[1] == 128
        )
        return (small_body if suits else general_body)(*args)

    placed = (
        P(None, ("groups", "cells")),
        P(("groups", "cells")),
        P(("groups", "cells")),
        P(("groups", "cells")),
        P(("groups", "cells")),
        P(("groups", "cells", "freq")),
        P(None, ("groups", "cells", "freq")),
        P(),
        P(),
        P(),
        P(),
        P(),
        P(),
        P(),
    )
    return jax.shard_map(
        body,
        mesh=mesh,
        in_specs=placed,
        out_specs=(
            P("groups", None),
            P("groups", None),
            P("groups"),
            P("groups", None),
            P("groups"),
            P("groups", None),
            P("groups", None),
            P(None, ("groups", "cells", "freq")),
        ),
        check_vma=False,
    )
```

time: 30.6 us -> 28.2 us (0.922)
  waiting for transfers between devices: 6.16 us -> 2.33 us
  local copies, waits for them, and re-layouts: 1.52 us -> 3.39 us
  Pallas kernels: 13 us -> 12.3 us
  other arithmetic: 0.85 us -> 1.52 us
  starting transfers between devices: 8.07 us -> 7.56 us
    ppermute x3 -> x2, starting transfers between devices: 8.06 us -> 4.55 us  [small_body(): lax.ppermute(gathered, 'cells', [(at, at ^ reach) for at in range(chunks)])]
    ppermute x3 -> x2, waiting for transfers between devices: 4.34 us -> 0.85 us  [small_body(): lax.ppermute(gathered, 'cells', [(at, at ^ reach) for at in range(chunks)])]
    ppermute x0 -> x1, starting transfers between devices: none -> 3 us  [small_body(): lax.ppermute(packed[None], 'cells', [(at, at ^ 1) for at in range(chunks)])]
    concatenate x0 -> x3, other arithmetic: none -> 1.42 us  [the longest x1 0.71 us: small_body(): embed = jnp.concatenate([level_table, w_proj], axis=0)]
    unnamed x18 -> x4, local copies, waits for them, and re-layouts: 1.52 us -> 2.53 us
    concatenate x0 -> x1, local copies, waits for them, and re-layouts: none -> 0.86 us  [small_body(): joint = jnp.concatenate([w_one, w_two, w_out], axis=1)]
    concatenate x3 -> x2, other arithmetic: 0.77 us -> 0.02 us  [small_body(): gathered = jnp.concatenate([gathered, moved], axis=0)]
    pallas_call x3 -> x5, Pallas kernels: 12 us -> 11.3 us  [the longest x1 7.62 us: run_cells(): pl.pallas_call(functools.partial(cell_kernel, freq_size), out_shape=(jax....]
  transfers between devices with their start and end apart: 4 -> 4, of which waited for: 3 -> 2; matrix products, arithmetic and copies ran while one was open for 0% -> 15% of each run, Pallas kernels for 7% -> 8%
where the time goes in v3:
time: 28.2 us; the launch traced here: 27.8 us
  Pallas kernels  12.3 us (44%)
  starting transfers between devices  7.56 us (27%)
  local copies, waits for them, and re-layouts  3.39 us (12%)
  waiting for transfers between devices  2.33 us (8%)
  other arithmetic  1.52 us (5%)
  between operations  0.69 us (2%)
    pallas_call x1, Pallas kernels, run_cells(): pl.pallas_call(functools.partial(cell_kernel, freq_size), out_shape=(jax....  7.62 us
    ppermute x2, starting transfers between devices, small_body(): lax.ppermute(gathered, 'cells', [(at, at ^ reach) for at in range(chunks)])  4.55 us
    ppermute x1, starting transfers between devices, small_body(): lax.ppermute(packed[None], 'cells', [(at, at ^ 1) for at in range(chunks)])  3 us
    unnamed x4, local copies, waits for them, and re-layouts  2.53 us
    pallas_call x1, Pallas kernels, run_forward(): pl.pallas_call(forward_kernel, out_shape=[jax.ShapeDtypeStruct(block, kin...  1.82 us
    pallas_call x1, Pallas kernels, small_body(): pl.pallas_call(pack_kernel, out_shape=shape((props, cells + 128), BF16),...  1.54 us
    ppermute x1, waiting for transfers between devices, small_body(): lax.ppermute(sums, 'freq', [(at, at ^ 1) for at in range(freq_size)])  1.49 us
    pallas_call x1, Pallas kernels, small_body(): pl.pallas_call(functools.partial(finish_kernel, scale), out_shape=(shape(...  0.99 us
  transfers between devices with their start and end apart: 4, of which 2 were waited for; matrix products, arithmetic and copies ran while one was open for 15% of the time, Pallas kernels for 8%

profile of v3, /device:TPU:0, one launch (start us, length us, event | category | flops | bytes accessed | tf_op | source)
XLA Modules:
  0.0 27.8 jit_solution(16804564588787484852)
XLA Ops:
  0.6 1.5 %pack_inputs.1.packed_ref = bf16[8,640]{1,0:T(8,128)(2,1)} custom-call(f32[2,16]{1,0:T(2,128)} %refs_0_.1, f32[1,16]{1,0:T(1,128)} %bitcast.18, f32[1,16]{1,0:T(1,128)} %bitcast.19, f32[1,16]{1,0:T(1,128)} %bitcast.20, s32[1,16]{1,0:T(1,128)} %bitcast.21, s32[1,512]{1,0:T(1,128)} %bitcast.15, bf16[8,512]{1,0:T(8,128)(2,1)} %refs_6_.1), custom_call_target="tpu_custom_call" | custom-call | tf_op jit(solution)/shard_map/pack_inputs/pallas_call | solution.py:566
  2.2 3.0 %collective-permute-start = (bf16[1,8,640]{2,1,0:T(8,128)(2,1)}, bf16[1,8,640]{2,1,0:T(8,128)(2,1)S(1)}, u32[]{:S(2)}, u32[]{:S(2)}) collective-permute-start(bf16[1,8,640]{2,1,0:T(8,128)(2,1)} %bitcast.14), channel_id=1, source_target_pairs={{0,2},{2,0},{4,6},{6,4},{8,10},{10,8},{12,14},{14,12},{1,3},{3,1},... | collective-permute-start | bytes 30728 | tf_op jit(solution)/shard_map/ppermute | solution.py:580
  5.2 0.7 %pad_maximum_fusion.3.embed_ref = bf16[24,256]{1,0:T(8,128)(2,1)S(1)} fusion(bf16[8,256]{1,0:T(8,128)(2,1)} %param.22, bf16[16,256]{1,0:T(8,128)(2,1)} %param.21), kind=kLoop, calls=%fused_computation.3 | loop fusion | flops 24576 | bytes 24576 | tf_op jit(solution)/shard_map/concatenate | solution.py:581
  5.9 0.7 %pad_maximum_fusion.4.bias_ref = f32[2,256]{1,0:T(2,128)S(1)} fusion(f32[1,256]{1,0:T(1,128)} %bitcast.16, f32[1,256]{1,0:T(1,128)} %bitcast.17), kind=kLoop, calls=%fused_computation.7 | loop fusion | flops 512 | bytes 4096 | tf_op jit(solution)/shard_map/concatenate | solution.py:582
  6.6 0.0 copy-start
  6.6 0.7 %copy-done = bf16[8,640]{1,0:T(8,128)(2,1)S(1)} copy-done((bf16[8,640]{1,0:T(8,128)(2,1)S(1)}, bf16[8,640]{1,0:T(8,128)(2,1)}, u32[]{:S(2)}) %copy-start) | copy-done | bytes 10264
  7.3 0.0 collective-permute-done
  7.3 1.9 %collective-permute-start.1 = (bf16[2,8,640]{2,1,0:T(8,128)(2,1)S(1)}, bf16[2,8,640]{2,1,0:T(8,128)(2,1)S(1)}, u32[]{:S(2)}, u32[]{:S(2)}) collective-permute-start(bf16[2,8,640]{2,1,0:T(8,128)(2,1)S(1)} %pad_maximum_fusion.2), channel_id=1, source_target_pairs={{0,4},{2,6},{4,0},{6,2},{8,12},{10,14},{12,8},{14,10},{1,5},{3,7},... | collective-permute-start | bytes 61448 | tf_op jit(solution)/shard_map/ppermute | solution.py:596
  9.2 0.9 %constant_dynamic-update-slice_fusion.2 = bf16[256,640]{1,0:T(8,128)(2,1)S(1)} fusion(bf16[256,256]{1,0:T(8,128)(2,1)} %param.23), kind=kLoop, calls=%fused_computation.6 | loop fusion | bytes 262144
  10.1 0.9 %constant_dynamic-update-slice_fusion.1 = bf16[256,640]{1,0:T(8,128)(2,1)S(1)} fusion(bf16[256,640]{1,0:T(8,128)(2,1)S(1)} %constant_dynamic-update-slice_fusion.2, bf16[256,256]{1,0:T(8,128)(2,1)} %param.25), kind=kLoop, calls=%fused_computation.5 | loop fusion | bytes 262144
  11.1 0.9 %constant_dynamic-update-slice_fusion.joint_ref = bf16[256,640]{1,0:T(8,128)(2,1)S(1)} fusion(bf16[256,640]{1,0:T(8,128)(2,1)S(1)} %constant_dynamic-update-slice_fusion.1, bf16[256,128]{1,0:T(8,128)(2,1)} %param.27), kind=kLoop, calls=%fused_computation.4 | loop fusion | bytes 131072 | tf_op jit(solution)/shard_map/concatenate | solution.py:587
  11.9 0.3 %prepare_weights.1.weights_ref = bf16[256,512]{1,0:T(8,128)(2,1)S(1)} custom-call(bf16[256,640]{1,0:T(8,128)(2,1)S(1)} %constant_dynamic-update-slice_fusion.joint_ref, bf16[24,256]{1,0:T(8,128)(2,1)S(1)} %pad_maximum_fusion.3.embed_ref, f32[2,256]{1,0:T(2,128)S(1)} %pad_maximum_fusion.4.bias_ref), custom_call_target="tpu_custom_call" | custom-call | tf_op jit(solution)/shard_map/prepare_weights/pallas_call | solution.py:588
  12.2 0.0 collective-permute-done.1
  12.2 2.7 %collective-permute-start.2 = (bf16[4,8,640]{2,1,0:T(8,128)(2,1)S(1)}, bf16[4,8,640]{2,1,0:T(8,128)(2,1)S(1)}, u32[]{:S(2)}, u32[]{:S(2)}) collective-permute-start(bf16[4,8,640]{2,1,0:T(8,128)(2,1)S(1)} %pad_maximum_fusion.1.gathered_ref), channel_id=1, source_target_pairs={{0,8},{2,10},{4,12},{6,14},{8,0},{10,2},{12,4},{14,6},{1,9},{3,11}... | collective-permute-start | bytes 122888 | tf_op jit(solution)/shard_map/ppermute | solution.py:596
  14.9 0.1 pad_add_fusion.place_ref
  15.0 1.8 %early_forward.1 = (bf16[4,256,512]{2,1,0:T(8,128)(2,1)S(1)}, f32[4,256,512]{2,1,0:T(8,128)S(1)}, bf16[4,256,512]{2,1,0:T(8,128)(2,1)S(1)}, f32[4,256,512]{2,1,0:T(8,128)S(1)}) custom-call(bf16[4,8,640]{2,1,0:T(8,128)(2,1)S(1)} %pad_maximum_fusion.1.gathered_ref, bf16[256,512]{1,0:T(8,128)(2,1)S(1)} %prepare_weights.1.weights_ref), custom_call_target="tpu_custom_call" | custom-call | tf_op jit(solution)/shard_map/early_forward/pallas_call | solution.py:486
  16.8 0.8 %collective-permute-done.2 = bf16[4,8,640]{2,1,0:T(8,128)(2,1)S(1)} collective-permute-done((bf16[4,8,640]{2,1,0:T(8,128)(2,1)S(1)}, bf16[4,8,640]{2,1,0:T(8,128)(2,1)S(1)}, u32[]{:S(2)}, u32[]{:S(2)}) %collective-permute-start.2) | collective-permute-done | bytes 40992 | tf_op jit(solution)/shard_map/ppermute | solution.py:596
  17.7 7.6 %all_cells.1 = (bf16[448,256]{1,0:T(8,128)(2,1)S(1)}, f32[8,512]{1,0:T(8,128)}) custom-call(s32[2]{0:T(128)S(1)} %pad_add_fusion.place_ref, bf16[8,8,640]{2,1,0:T(8,128)(2,1)S(1)} %pad_maximum_fusion.gathered_ref, bf16[256,512]{1,0:T(8,128)(2,1)S(1)} %prepare_weights.1.weights_ref, bf16[256,640]{1,0:T(8,128)(2,1)S(1)} %constant_dynamic-update-slice_fusion.joint_ref, ...), custom_call_target="tpu_custom_call" | custom-call | tf_op jit(solution)/shard_map/all_cells/pallas_call | solution.py:502
  25.3 0.0 collective-permute-start.3
  25.3 1.5 %collective-permute-done.3.other_ref = bf16[448,256]{1,0:T(8,128)(2,1)S(1)} collective-permute-done((bf16[448,256]{1,0:T(8,128)(2,1)S(1)}, bf16[448,256]{1,0:T(8,128)(2,1)S(1)}, u32[]{:S(2)}, u32[]{:S(2)}) %collective-permute-start.3) | collective-permute-done | bytes 229408 | tf_op jit(solution)/shard_map/ppermute | solution.py:606
  26.8 1.0 %finish_sums.1 = (f32[256,128]{1,0:T(8,128)}, f32[256,256]{1,0:T(8,128)}, f32[1,256]{1,0:T(1,128)}, f32[256,256]{1,0:T(8,128)}, f32[1,256]{1,0:T(1,128)}, /*index=5*/f32[16,256]{1,0:T(8,128)}, f32[8,256]{1,0:T(8,128)}) custom-call(bf16[448,256]{1,0:T(8,128)(2,1)S(1)} %get-tuple-element.45.own_ref, bf16[448,256]{1,0:T(8,128)(2,1)S(1)} %collective-permute-done.3.other_ref, ...), custom_call_target="tpu_custom_call" | custom-call | tf_op jit(solution)/shard_map/finish_sums/pallas_call | solution.py:608
  (4 shorter events, 0.0 us)
Async XLA Ops:
  2.2 5.1 %collective-permute-start = (bf16[1,8,640]{2,1,0:T(8,128)(2,1)}, bf16[1,8,640]{2,1,0:T(8,128)(2,1)S(1)}, u32[]{:S(2)}, u32[]{:S(2)}) collective-permute-start(bf16[1,8,640]{2,1,0:T(8,128)(2,1)} %bitcast.14), channel_id=1, source_target_pairs={{0,2},{2,0},{4,6},{6,4},{8,10},{10,8},{12,14},{14,12},{1,3},{3,1},... | collective-permute-start | bytes 30728 | tf_op jit(solution)/shard_map/ppermute | solution.py:580
  6.6 0.7 %copy-start = (bf16[8,640]{1,0:T(8,128)(2,1)S(1)}, bf16[8,640]{1,0:T(8,128)(2,1)}, u32[]{:S(2)}) copy-start(bf16[8,640]{1,0:T(8,128)(2,1)} %pack_inputs.1.packed_ref) | copy-start | bytes 30724
  7.3 4.9 %collective-permute-start.1 = (bf16[2,8,640]{2,1,0:T(8,128)(2,1)S(1)}, bf16[2,8,640]{2,1,0:T(8,128)(2,1)S(1)}, u32[]{:S(2)}, u32[]{:S(2)}) collective-permute-start(bf16[2,8,640]{2,1,0:T(8,128)(2,1)S(1)} %pad_maximum_fusion.2), channel_id=1, source_target_pairs={{0,4},{2,6},{4,0},{6,2},{8,12},{10,14},{12,8},{14,10},{1,5},{3,7},... | collective-permute-start | bytes 61448 | tf_op jit(solution)/shard_map/ppermute | solution.py:596
  12.2 5.4 %collective-permute-start.2 = (bf16[4,8,640]{2,1,0:T(8,128)(2,1)S(1)}, bf16[4,8,640]{2,1,0:T(8,128)(2,1)S(1)}, u32[]{:S(2)}, u32[]{:S(2)}) collective-permute-start(bf16[4,8,640]{2,1,0:T(8,128)(2,1)S(1)} %pad_maximum_fusion.1.gathered_ref), channel_id=1, source_target_pairs={{0,8},{2,10},{4,12},{6,14},{8,0},{10,2},{12,4},{14,6},{1,9},{3,11}... | collective-permute-start | bytes 122888 | tf_op jit(solution)/shard_map/ppermute | solution.py:596
  25.3 1.5 %collective-permute-start.3 = (bf16[448,256]{1,0:T(8,128)(2,1)S(1)}, bf16[448,256]{1,0:T(8,128)(2,1)S(1)}, u32[]{:S(2)}, u32[]{:S(2)}) collective-permute-start(bf16[448,256]{1,0:T(8,128)(2,1)S(1)} %get-tuple-element.45.own_ref), channel_id=1, source_target_pairs={{0,1},{1,0},{2,3},{3,2},{4,5},{5,4},{6,7},{7,6},{8,9},{9,8},{10,11... | collective-permute-start | bytes 688136 | tf_op jit(solution)/shard_map/ppermute | solution.py:606

commit v4 on v3

--- a/solution.py
+++ b/solution.py
@@ -17,6 +17,7 @@
 F32 = jnp.float32
 BF16 = jnp.bfloat16
 VMEM_BYTES = 40 * 1024 * 1024
+SMALL_ROWS = 32
 WHOLE_VMEM = 64 * 1024 * 1024 - 256 * 1024
 
 
@@ -169,9 +170,21 @@
 
 
 def pack_kernel(*refs):
-    sources, out_ref, buffers, (rows, arrived) = refs[:7], refs[7], refs[8:15], refs[15:]
-    fetch(sources, buffers, arrived)
-    adj_ref, x_ref, y_ref, z_ref, assign_ref, codes_ref, params_ref = buffers
+    sources, (out_ref, flat_ref), buffers, (rows, arrived) = refs[:14], refs[14:16], refs[16:28], refs[28:]
+    hidden = flat_ref.shape[1]
+    base = SMALL_ROWS + 2 * hidden
+    fetch(
+        sources,
+        [flat_ref.at[SMALL_ROWS : SMALL_ROWS + hidden], flat_ref.at[SMALL_ROWS + hidden : base]]
+        + list(buffers),
+        arrived,
+    )
+    wo_ref, buffers = buffers[0], buffers[1:]
+    out_dim = wo_ref.shape[1]
+    flat_ref[base:, 0:out_dim] = wo_ref[0 : hidden // 2]
+    flat_ref[base:, out_dim:] = wo_ref[hidden // 2 :]
+    adj_ref, x_ref, y_ref, z_ref, assign_ref, codes_ref, params_ref = buffers[:7]
+    table_ref, proj_ref, b1_ref, b2_ref = buffers[7:]
     cells = codes_ref.shape[1]
     pieces = [adj_ref[0:1], adj_ref[1:2]]
     for ref in (x_ref, y_ref, z_ref):
@@ -186,30 +199,36 @@
     rows[6:8] = jnp.zeros((2, 128), F32)
     out_ref[:, 0:cells] = params_ref[...]
     out_ref[:, cells:] = rows[...].astype(BF16)
+    embed = [table_ref[...].astype(F32), proj_ref[...].astype(F32)]
+    shifts = split(b1_ref[...], 3) + split(b2_ref[...], 3)
+    rest = jnp.zeros((SMALL_ROWS - 30, hidden), F32)
+    flat_ref[0:SMALL_ROWS] = jnp.concatenate(embed + shifts + [rest], axis=0).astype(BF16)
 
 
 def stage_kernel(packed_ref, out_ref):
     out_ref[...] = packed_ref[...]
 
 
-def weight_kernel(joint_ref, embed_ref, bias_ref, out_ref):
-    hidden = joint_ref.shape[0]
-    used = embed_ref.shape[0]
-    stack = embed_ref[...]
-    joined = jnp.dot(stack, joint_ref[:, 0:hidden], preferred_element_type=F32)
-    joined = jnp.concatenate([joined, bias_ref[0:1], jnp.zeros((7, hidden), F32)], axis=0)
-    shifts = split(0.5 * bias_ref[1:2], 3)
+def weight_kernel(flat_ref, out_ref):
+    hidden = flat_ref.shape[1]
+    first = slice(SMALL_ROWS, SMALL_ROWS + hidden)
+    small = flat_ref[0:SMALL_ROWS].astype(F32)
+    stack = small[0:24]
+    joined = dot(stack.astype(BF16), flat_ref[first])
+    bias = (small[24:25] + small[25:26]) + small[26:27]
+    joined = jnp.concatenate([joined, bias, jnp.zeros((7, hidden), F32)], axis=0)
+    shifts = [0.5 * small[at : at + 1] for at in (27, 28, 29)]
     rows = split(0.5 * joined, 3) + shifts + [jnp.zeros((29, hidden), F32)]
     out_ref[:, 0:128] = jnp.concatenate(rows, axis=0).T.astype(BF16)
-    second = joint_ref[:, hidden : 2 * hidden].astype(F32)
+    second = flat_ref[SMALL_ROWS + hidden : SMALL_ROWS + 2 * hidden].astype(F32)
     out_ref[:, 128 : 128 + hidden] = (0.5 * second).T.astype(BF16)
-    filled = [stack.astype(F32), jnp.zeros((8, hidden), F32)]
+    filled = [stack, jnp.zeros((8, hidden), F32)]
     rows = filled * 3 + [jnp.zeros((32, hidden), F32)]
     out_ref[:, 128 + hidden :] = jnp.concatenate(rows, axis=0).T.astype(BF16)
 
 
-SINE = (3.1415820121765137, -5.167142868041992, 2.5418989658355713, -0.5546361804008484)
-COSINE = (-4.934795379638672, 4.058451175689697, -1.3320938348770142, 0.22008062899112701)
+NEAR = (3.1051740646362305, -2.9883227348327637)
+FAR = (0.9884209632873535, -4.203672885894775)
 
 
 def dot(left, right):
@@ -251,13 +270,15 @@
     return jnp.broadcast_to(shift, (shift.shape[0], 128))
 
 
-def forward_kernel(gathered_ref, weights_ref, one_ref, slope_one_ref, two_ref, slope_two_ref, bias):
+def forward_kernel(
+    begin, gathered_ref, weights_ref, one_ref, slope_one_ref, two_ref, slope_two_ref, bias
+):
     count, hidden, cells = one_ref.shape
     bias[...] = bias_of(weights_ref)
     wide = jnp.concatenate([bias[...]] * (cells // 128), axis=1)
 
     def first(slot):
-        act, slope = activate(layer_one(weights_ref, feature_of(gathered_ref, slot)))
+        act, slope = activate(layer_one(weights_ref, feature_of(gathered_ref, begin + slot)))
         one_ref[slot] = act
         slope_one_ref[slot] = slope
 
@@ -276,18 +297,19 @@
 
 def cell_kernel(
     freq_size,
-    place_ref, gathered_ref, weights_ref, joint_ref,
-    one_ref, slope_one_ref, two_ref, slope_two_ref,
-    sums_ref, grad_params_ref,
-    across, where, lift, bias, totals, waves, deltas,
-    act_one, act_kept, slope_one, act_two, delta_two, spectra,
+    place_ref, gathered_ref, weights_ref, flat_ref, *refs
 ):
     chunks, _, width = gathered_ref.shape
     cells = width - 128
-    hidden = joint_ref.shape[0]
-    freqs = (joint_ref.shape[1] - 2 * hidden) // 2
-    w2_ref = joint_ref.at[:, hidden : 2 * hidden]
-    wo_ref = joint_ref.at[:, 2 * hidden :]
+    hidden = flat_ref.shape[1]
+    early = [refs[at : at + 4] for at in range(0, len(refs) - 14, 4)]
+    sums_ref, grad_params_ref, across, where, lift, bias, totals, waves = refs[-14:-6]
+    delta_two, spectra = refs[-6:-4]
+    early.append(refs[-4:])
+    freqs = lift.shape[0] // 2
+    base = SMALL_ROWS + 2 * hidden
+    half_rows = slice(base, base + hidden // 2)
+    w2_ref = flat_ref.at[SMALL_ROWS + hidden : base]
     targets = chunks * 16
     me = place_ref[0]
     freq_rank = place_ref[1]
@@ -317,13 +339,13 @@
             return jnp.broadcast_to(value[:, chunk : chunk + 1], (16, 128))
 
         where[0, here] = spread(point_y)
-        where[1, here] = spread(point_z * point_z)
-        where[2, here] = spread(wave)
-        where[3, here] = spread(kernel_gain * point_z)
+        where[1, here] = spread(wave * wave * (point_z * point_z))
+        where[2, here] = spread(kernel_gain * point_z * (wave * wave))
+        where[3, here] = spread(wave * wave)
         wide = spread(point_x)
         for at, side in enumerate(sides):
             offset = wide - side
-            across[here, at * 128 : (at + 1) * 128] = offset * offset
+            across[here, at * 128 : (at + 1) * 128] = offset * offset * where[3, here]
         select = jnp.where(spread(parts[11])[:, 0:freqs] == grid, 1.0, 0.0)
         part_a = select * spread(parts[0])[:, 0:freqs]
         part_b = select * spread(parts[1])[:, 0:freqs]
@@ -332,66 +354,69 @@
     lift[:, 0:targets] = jnp.concatenate(near, axis=0).T.astype(BF16)
     lift[:, targets:] = jnp.concatenate(far, axis=0).T.astype(BF16)
     bias[...] = bias_of(weights_ref)
-    totals[...] = jnp.zeros_like(totals)
-
-    top = hidden + 2 * freqs
-    ready = one_ref.shape[0]
-
-    def place(block):
-        slot = (block // ready) * ready + lax.bitwise_and(lax.bitwise_xor(me, block), ready - 1)
-        return slot, lax.bitwise_xor(slot, me)
+
+    middle = hidden + 32
+    top = middle + 2 * freqs
+    owners = [(part, at) for part in early for at in range(part[0].shape[0])]
+    ready = chunks - refs[-4].shape[0]
+
+    def layers(block):
+        part, at = owners[block]
+        return [ref.at[at] for ref in part]
+
+    def back_out(spectrum):
+        upper_rows = dot(flat_ref[half_rows, 0 : 2 * freqs], spectrum)
+        lower_rows = dot(flat_ref[half_rows, 2 * freqs : 4 * freqs], spectrum)
+        return jnp.concatenate([upper_rows, lower_rows], axis=0)
 
     def holograms(block, even):
-        chunk = place(block)[1]
+        chunk = lax.bitwise_xor(me, block)
         row = ((chunk * stride + freq_rank * cells) // SIDE).astype(F32)
         for at in range(0, targets, 16):
             here = slice(at, at + 16)
             offset = where[0, here] - row
-            rest = offset * offset + where[1, here]
+            rest = offset * offset * where[3, here] + where[1, here]
             for lane in range(0, cells, 128):
                 square = across[here, lane : lane + 128] + rest
-                inverse = lax.rsqrt(square)
-                turns = where[2, here] * (square * inverse)
+                turns = square * lax.rsqrt(square)
                 part = turns - jnp.round(turns)
                 power = part * part
-                sine = part * (((SINE[3] * power + SINE[2]) * power + SINE[1]) * power + SINE[0])
-                cosine = (COSINE[2] * power + COSINE[1]) * power + COSINE[0]
-                cosine = cosine * power + 1.0
-                amplitude = where[3, here] * (inverse * inverse)
-                twice = (amplitude + amplitude) * sine
-                waves[even, at : at + 16, lane : lane + 128] = (amplitude - twice * sine).astype(BF16)
+                sine = part * (NEAR[1] * power + NEAR[0])
+                cosine = (power + FAR[1]) * power + FAR[0]
+                sine_square = sine * sine
+                cosine_square = cosine * cosine
+                norm = square * (sine_square + cosine_square)
+                amplitude = where[2, here] * pl.reciprocal(norm, approx=True)
+                waves[even, at : at + 16, lane : lane + 128] = (
+                    amplitude * (cosine_square - sine_square)
+                ).astype(BF16)
                 waves[even, targets + at : targets + at + 16, lane : lane + 128] = (
-                    twice * cosine
+                    amplitude * ((sine + sine) * cosine)
                 ).astype(BF16)
                 yield
 
-    def kept(block, even):
-        if block < ready:
-            slot = place(block)[0]
-            refs = (one_ref, slope_one_ref, two_ref, slope_two_ref)
-            return [ref.at[slot] for ref in refs]
-        return act_kept.at[even], slope_one.at[even], act_two.at[even], None
-
     def lower(block, even):
-        slot, chunk = place(block)
-        total = totals.at[chunk // ready]
+        total = totals.at[lax.bitwise_xor(me, block) // 2]
 
         def outer(low, left, right):
-            total[low : low + left.shape[0]] += contract(left, right, 1, 1)
-
-        one, slope, two, _ = kept(block, even)
-        feature = feature_of(gathered_ref, slot)
+            rows = slice(low, low + left.shape[0])
+            product = contract(left, right, 1, 1)
+            total[rows] = total[rows] + product if block % 2 else product
+
+        one, slope, two, _ = layers(block)
+        feature = feature_of(gathered_ref, block)
         delta = delta_two[even]
         back = dot(w2_ref[...], delta)
         yield
         value = (back * slope[...]).astype(BF16)
-        deltas[chunk] = value
-        yield
-        outer(0, one[...], delta)
-        yield
-        outer(hidden, spectra[even], two[...])
-        yield
-        outer(top + 32, feature, delta)
+        if block == 0:
+            both = contract(weights_ref[:, 0:128], value, 0, 0)
+            grad_params_ref[...] = 0.5 * ((both[16:24] + both[48:56]) + both[80:88])
+        yield
+        outer(0, jnp.concatenate([one[...], feature], axis=0), delta)
+        yield
+        outer(middle, spectra[even], two[...])
+        yield
         outer(top, feature, value)
         yield
 
@@ -399,40 +424,39 @@
         spectrum = dot(lift[...], waves[even]).astype(BF16)
         spectra[even] = spectrum
         yield
-        if block < ready:
-            back = dot(wo_ref[...], spectrum)
-            yield
-            delta_two[even] = (back * kept(block, even)[3][...]).astype(BF16)
-            yield
-            return
-        act = act_one[even]
-        act_kept[even] = act
-        half = dot(second_ref[...], act)
+        back = back_out(spectrum)
+        yield
+        delta_two[even] = (back * layers(block)[3][...]).astype(BF16)
+        yield
+
+    def first(block):
+        one, slope_one, _, _ = layers(block)
+        half = layer_one(weights_ref, feature_of(gathered_ref, block))
+        yield
+        one[...], slope_one[...] = activate(half)
+        yield
+
+    def second(block):
+        one, _, two, slope_two = layers(block)
+        half = dot(second_ref[...], one[...])
         half = half + jnp.concatenate([bias[...]] * (cells // 128), axis=1)
         yield
-        back = dot(wo_ref[...], spectrum)
-        yield
-        act, slope = activate(half)
-        act_two[even] = act
-        yield
-        delta_two[even] = (back * slope).astype(BF16)
-        yield
-
-    def begin(block, even):
-        if block >= ready:
-            half = layer_one(weights_ref, feature_of(gathered_ref, place(block)[0]))
-            yield
-            act, slope = activate(half)
-            act_one[even] = act
-            slope_one[even] = slope
-            yield
-
-    stages = (begin, upper, lower)
+        two[...], slope_two[...] = activate(half)
+        yield
+
     for at in range(chunks + 2):
-        live = [lag for lag in (2, 1, 0) if 0 <= at - lag < chunks]
-        waiting = [stages[lag](at - lag, (at - lag) % 2) for lag in live]
-        spots = sum(5 if lag == 2 else ((5, 3), (2, 0))[1 - lag][at - lag < ready] for lag in live)
-        pieces = (targets // 16) * (cells // 128) if 0 in live else 0
+        waiting = []
+        if 0 <= at - 2 < chunks:
+            waiting.append((lower(at - 2, at % 2), 5))
+        if 0 <= at - 1 < chunks:
+            waiting.append((upper(at - 1, (at - 1) % 2), 3))
+        if ready <= at + ready - 1 < chunks:
+            waiting.append((second(at + ready - 1), 2))
+        if at + ready < chunks:
+            waiting.append((first(at + ready), 2))
+        spots = sum(count for _, count in waiting)
+        waiting = [stage for stage, _ in waiting]
+        pieces = (targets // 16) * (cells // 128) if at < chunks else 0
         extra = holograms(at, at % 2)
         done, drawn = 0, 0
         while waiting:
@@ -447,17 +471,22 @@
         if pieces:
             for _ in extra:
                 pass
-    both = contract(weights_ref[:, 0:128], deltas[me], 0, 0)
-    grad_params_ref[...] = 0.5 * ((both[16:24] + both[48:56]) + both[80:88])
-    sums_ref[...] = (totals[0] + totals[1]).astype(BF16)
+    pairs = chunks // 2
+    added = [totals.at[at] for at in range(pairs)]
+    for low in range(0, totals.shape[1], 16):
+        terms = [ref[low : low + 16] for ref in added]
+        while len(terms) > 1:
+            terms = [terms[at] + terms[at + 1] for at in range(0, len(terms), 2)]
+        sums_ref[low : low + 16] = terms[0].astype(BF16)
 
 
 def finish_kernel(
-    scale, own_ref, other_ref, weights_ref, joint_ref,
+    scale, own_ref, other_ref, weights_ref, flat_ref,
     out_ref, w2_ref, b2_ref, wone_ref, b1_ref, table_ref, proj_ref,
 ):
-    hidden = joint_ref.shape[0]
-    top = hidden + out_ref.shape[1]
+    hidden = flat_ref.shape[1]
+    middle = hidden + 32
+    top = middle + out_ref.shape[1]
     levels = table_ref.shape[0]
     used = levels + proj_ref.shape[0]
 
@@ -466,25 +495,24 @@
         return both * (scale * factor)
 
     w2_ref[...] = total(0, hidden, 0.5)
-    out_ref[...] = total(hidden, top, 1.0).T
+    out_ref[...] = total(middle, top, 1.0).T
     feature = total(top, top + 32, 0.25)
     b1_ref[...] = feature[used : used + 1]
-    b2_ref[...] = total(top + 32, top + 64, 0.5)[used : used + 1]
+    b2_ref[...] = total(hidden, middle, 0.5)[used : used + 1]
     rows = jnp.concatenate(split(feature, 3), axis=0).astype(BF16)
     embed = weights_ref[:, 128 + hidden : 128 + hidden + 96]
     wone_ref[...] = jnp.dot(embed, rows, preferred_element_type=F32)
-    back = contract(rows, joint_ref[:, 0:hidden], 1, 1)
+    back = contract(rows, flat_ref[SMALL_ROWS : SMALL_ROWS + hidden], 1, 1)
     back = (back[0:32] + back[32:64]) + back[64:96]
     table_ref[...] = back[0:levels]
     proj_ref[...] = back[levels:used]
 
 
-def run_forward(gathered, weights):
-    count, _, width = gathered.shape
+def run_forward(gathered, weights, begin, count):
     hidden = weights.shape[0]
-    block = (count, hidden, width - 128)
+    block = (count, hidden, gathered.shape[2] - 128)
     return pl.pallas_call(
-        forward_kernel,
+        functools.partial(forward_kernel, begin),
         out_shape=[jax.ShapeDtypeStruct(block, kind) for kind in (BF16, F32, BF16, F32)],
         scratch_shapes=[pltpu.VMEM((hidden, 128), F32)],
         compiler_params=pltpu.CompilerParams(vmem_limit_bytes=VMEM_BYTES),
@@ -492,39 +520,37 @@
     )(gathered, weights)
 
 
-def run_cells(place, gathered, weights, joint, early, freq_size):
+def run_cells(place, gathered, weights, flat, early, freq_size, out_dim):
     chunks, props, width = gathered.shape
     cells = width - 128
-    hidden = joint.shape[0]
-    out_dim = joint.shape[1] - 2 * hidden
+    hidden = flat.shape[1]
     targets = chunks * 16
+    rest = chunks - sum(part[0].shape[0] for part in early)
+    rows = hidden + out_dim + 64
     vmem = pl.BlockSpec(memory_space=pltpu.VMEM)
+    flattened = [array for part in early for array in part]
     return pl.pallas_call(
         functools.partial(cell_kernel, freq_size),
         out_shape=(
-            jax.ShapeDtypeStruct((hidden + out_dim + 64, hidden), BF16),
+            jax.ShapeDtypeStruct((rows, hidden), BF16),
             jax.ShapeDtypeStruct((props, cells), F32),
         ),
-        in_specs=[pl.BlockSpec(memory_space=pltpu.SMEM)] + [vmem] * 7,
+        in_specs=[pl.BlockSpec(memory_space=pltpu.SMEM)] + [vmem] * (3 + len(flattened)),
         out_specs=(vmem, vmem),
         scratch_shapes=[
             pltpu.VMEM((targets, cells), F32),
             pltpu.VMEM((4, targets, 128), F32),
             pltpu.VMEM((out_dim, 2 * targets), BF16),
             pltpu.VMEM((hidden, 128), F32),
-            pltpu.VMEM((2, hidden + out_dim + 64, hidden), F32),
+            pltpu.VMEM((chunks // 2, rows, hidden), F32),
             pltpu.VMEM((2, 2 * targets, cells), BF16),
-            pltpu.VMEM((chunks, hidden, cells), BF16),
-            pltpu.VMEM((2, hidden, cells), BF16),
-            pltpu.VMEM((2, hidden, cells), BF16),
-            pltpu.VMEM((2, hidden, cells), F32),
-            pltpu.VMEM((2, hidden, cells), BF16),
             pltpu.VMEM((2, hidden, cells), BF16),
             pltpu.VMEM((2, out_dim, cells), BF16),
-        ],
+        ]
+        + [pltpu.VMEM((rest, hidden, cells), kind) for kind in (BF16, F32, BF16, F32)],
         compiler_params=pltpu.CompilerParams(vmem_limit_bytes=VMEM_BYTES),
         name="all_cells",
-    )(place, gathered, weights, joint, *early)
+    )(place, gathered, weights, flat, *flattened)
 
 
 def small_body(
@@ -558,16 +584,20 @@
         return buffers, pltpu.SemaphoreType.DMA((len(arrays),))
 
     inputs = (
+        w_one, w_two, w_out,
         adjoint, target_x[None, :], target_y[None, :], target_z[None, :], assignment[None, :],
-        level_codes[None, :], cell_params,
+        level_codes[None, :], cell_params, level_table, w_proj, b_one[None, :], b_two[None, :],
     )
     whole = pltpu.CompilerParams(vmem_limit_bytes=WHOLE_VMEM)
     buffers, arrived = fetched(inputs)
-    packed = pl.pallas_call(
+    packed, flat = pl.pallas_call(
         pack_kernel,
-        out_shape=shape((props, cells + 128), BF16),
+        out_shape=(
+            shape((props, cells + 128), BF16),
+            shape((SMALL_ROWS + 2 * hidden + hidden // 2, hidden), BF16),
+        ),
         in_specs=[pl.BlockSpec(memory_space=pltpu.HBM)] * len(inputs),
-        scratch_shapes=buffers + [pltpu.VMEM((8, 128), F32), arrived],
+        scratch_shapes=buffers[2:] + [pltpu.VMEM((8, 128), F32), arrived],
         compiler_params=whole,
         name="pack_inputs",
     )(*inputs)
@@ -578,30 +608,27 @@
         name="stage_own",
     )(packed)
     moved = lax.ppermute(packed[None], "cells", [(at, at ^ 1) for at in range(chunks)])
-    embed = jnp.concatenate([level_table, w_proj], axis=0)
-    biases = jnp.concatenate([b_one[None, :], b_two[None, :]], axis=0)
-    gathered = jnp.concatenate([staged[None], moved], axis=0)
-    gathered, embed, biases, w_one, w_two, w_out = lax.optimization_barrier(
-        (gathered, embed, biases, w_one, w_two, w_out)
-    )
-    joint = jnp.concatenate([w_one, w_two, w_out], axis=1)
     weights = pl.pallas_call(
         weight_kernel,
         out_shape=shape((hidden, 256 + hidden), BF16),
         compiler_params=params,
         name="prepare_weights",
-    )(joint, embed, biases)
-    reach = 2
+    )(flat)
+    gathered = jnp.concatenate([staged[None], moved], axis=0)
+    gathered, weights = lax.optimization_barrier((gathered, weights))
+    reach, begin, early = 2, 0, []
     while reach < chunks:
         moved = lax.ppermute(gathered, "cells", [(at, at ^ reach) for at in range(chunks)])
-        if 2 * reach == chunks:
-            early = run_forward(gathered, weights)
+        early.append(run_forward(gathered, weights, begin, reach - begin))
+        begin = reach
         gathered = jnp.concatenate([gathered, moved], axis=0)
-        gathered, weights = lax.optimization_barrier((gathered, weights))
+        gathered, early = lax.optimization_barrier((gathered, early))
         reach *= 2
 
     place = jnp.stack([lax.axis_index("cells"), lax.axis_index("freq")]).astype(jnp.int32)
-    sums, grad_params = run_cells(place, gathered, weights, joint, early, freq_size)
+    sums, grad_params = run_cells(
+        place, gathered, weights, flat, early, freq_size, w_out.shape[1]
+    )
 
     other = lax.ppermute(sums, "freq", [(at, at ^ 1) for at in range(freq_size)])
     scale = 1.0 / math.sqrt(cells * chunks * freq_size)
@@ -618,7 +645,7 @@
         ),
         compiler_params=params,
         name="finish_sums",
-    )(sums, other, weights, joint)
+    )(sums, other, weights, flat)
     return (
         grad_out, grad_w2, grad_b2[0], grad_w1, grad_b1[0], grad_table, grad_proj, grad_params,
     )
@@ -639,7 +666,7 @@
             and chunks * cells * chunks * local <= 1 << 20
             and args[7].shape[0] == 16
             and args[8].shape[0] == 8
-            and hidden % 128 == 0
+            and hidden == 2 * args[13].shape[1]
             and mesh.shape["freq"] * cells % SIDE == 0
             and SIDE % cells == 0
             and args[13].shape[1] == 128

time: 28.2 us -> 26.7 us (0.947)
  local copies, waits for them, and re-layouts: 3.39 us -> 1.72 us
  other arithmetic: 1.52 us -> 0.1 us
  waiting for transfers between devices: 2.33 us -> 3.25 us
  starting transfers between devices: 7.56 us -> 8.03 us
  Pallas kernels: 12.3 us -> 12.7 us
    concatenate x2 -> x0, other arithmetic: 1.42 us -> none  [the longest x1 0.71 us: small_body(): embed = jnp.concatenate([level_table, w_proj], axis=0)]
    ppermute x2, waiting for transfers between devices: 0.85 us -> 1.77 us  [small_body(): lax.ppermute(gathered, 'cells', [(at, at ^ reach) for at in range(chunks)])]
    concatenate x1 -> x0, local copies, waits for them, and re-layouts: 0.86 us -> none  [small_body(): joint = jnp.concatenate([w_one, w_two, w_out], axis=1)]
    unnamed x4 -> x6, local copies, waits for them, and re-layouts: 2.53 us -> 1.72 us
    ppermute x2, starting transfers between devices: 4.55 us -> 5.02 us  [small_body(): lax.ppermute(gathered, 'cells', [(at, at ^ reach) for at in range(chunks)])]
    pallas_call x2 -> x3, Pallas kernels: 3.36 us -> 3.82 us  [the longest x2 1.96 us: run_forward(): pl.pallas_call(functools.partial(forward_kernel, begin), out_shape=[jax.S...]
  transfers between devices with their start and end apart: 4 -> 4, of which waited for: 2 -> 3; matrix products, arithmetic and copies ran while one was open for 15% -> 0% of each run, Pallas kernels for 8% -> 8%
where the time goes in v4:
time: 26.7 us; the launch traced here: 26.5 us
  Pallas kernels  12.7 us (48%)
  starting transfers between devices  8.03 us (30%)
  waiting for transfers between devices  3.25 us (12%)
  local copies, waits for them, and re-layouts  1.72 us (6%)
  between operations  0.71 us (3%)
    pallas_call x1, Pallas kernels, run_cells(): pl.pallas_call(functools.partial(cell_kernel, freq_size), out_shape=(jax....  7.58 us
    ppermute x2, starting transfers between devices, small_body(): lax.ppermute(gathered, 'cells', [(at, at ^ reach) for at in range(chunks)])  5.02 us
    ppermute x1, starting transfers between devices, small_body(): lax.ppermute(packed[None], 'cells', [(at, at ^ 1) for at in range(chunks)])  3 us
    pallas_call x2, Pallas kernels, run_forward(): pl.pallas_call(functools.partial(forward_kernel, begin), out_shape=[jax.S...  1.96 us
    pallas_call x1, Pallas kernels, small_body(): pl.pallas_call(pack_kernel, out_shape=(shape((props, cells + 128), BF16),...  1.86 us
    ppermute x2, waiting for transfers between devices, small_body(): lax.ppermute(gathered, 'cells', [(at, at ^ reach) for at in range(chunks)])  1.77 us
    unnamed x6, local copies, waits for them, and re-layouts  1.72 us
    ppermute x1, waiting for transfers between devices, small_body(): lax.ppermute(sums, 'freq', [(at, at ^ 1) for at in range(freq_size)])  1.49 us
  transfers between devices with their start and end apart: 4, of which 3 were waited for; matrix products, arithmetic and copies ran while one was open for 0% of the time, Pallas kernels for 8%

profile of v4, /device:TPU:0, one launch (start us, length us, event | category | flops | bytes accessed | tf_op | source)
XLA Modules:
  0.0 26.5 jit_solution(744993437713282676)
XLA Ops:
  0.6 1.9 %pack_inputs.1 = (bf16[8,640]{1,0:T(8,128)(2,1)}, bf16[672,256]{1,0:T(8,128)(2,1)}) custom-call(bf16[256,256]{1,0:T(8,128)(2,1)} %refs_0_.1, bf16[256,256]{1,0:T(8,128)(2,1)} %refs_1_.1, bf16[256,128]{1,0:T(8,128)(2,1)} %refs_2_.1, f32[2,16]{1,0:T(2,128)} %refs_3_.1, f32[1,16]{1,0:T(1,128)} %bitcast.18, f32[1,16]{1,0:T(1,128)} %bitcast.19, ...), custom_call_target="tpu_custom_call" | custom-call | tf_op jit(solution)/shard_map/pack_inputs/pallas_call | solution.py:593
  2.5 3.0 %collective-permute-start = (bf16[1,8,640]{2,1,0:T(8,128)(2,1)}, bf16[1,8,640]{2,1,0:T(8,128)(2,1)S(1)}, u32[]{:S(2)}, u32[]{:S(2)}) collective-permute-start(bf16[1,8,640]{2,1,0:T(8,128)(2,1)} %bitcast.14), channel_id=1, source_target_pairs={{0,2},{2,0},{4,6},{6,4},{8,10},{10,8},{12,14},{14,12},{1,3},{3,1},... | collective-permute-start | bytes 30728 | tf_op jit(solution)/shard_map/ppermute | solution.py:610
  5.5 0.0 copy-start.2
  5.5 0.7 %copy-done.2 = bf16[8,640]{1,0:T(8,128)(2,1)S(1)} copy-done((bf16[8,640]{1,0:T(8,128)(2,1)S(1)}, bf16[8,640]{1,0:T(8,128)(2,1)}, u32[]{:S(2)}) %copy-start.2) | copy-done | bytes 10264
  6.2 0.0 copy-start
  6.3 1.0 %copy-done = bf16[672,256]{1,0:T(8,128)(2,1)S(1)} copy-done((bf16[672,256]{1,0:T(8,128)(2,1)S(1)}, bf16[672,256]{1,0:T(8,128)(2,1)}, u32[]{:S(2)}) %copy-start) | copy-done | bytes 344088
  7.2 0.3 %prepare_weights.1.weights_ref = bf16[256,512]{1,0:T(8,128)(2,1)S(1)} custom-call(bf16[672,256]{1,0:T(8,128)(2,1)S(1)} %copy-done), custom_call_target="tpu_custom_call" | custom-call | tf_op jit(solution)/shard_map/prepare_weights/pallas_call | solution.py:611
  7.5 0.0 collective-permute-done
  7.5 2.0 %collective-permute-start.1 = (bf16[2,8,640]{2,1,0:T(8,128)(2,1)S(1)}, bf16[2,8,640]{2,1,0:T(8,128)(2,1)S(1)}, u32[]{:S(2)}, u32[]{:S(2)}) collective-permute-start(bf16[2,8,640]{2,1,0:T(8,128)(2,1)S(1)} %pad_maximum_fusion.2.gathered_ref), channel_id=1, source_target_pairs={{0,4},{2,6},{4,0},{6,2},{8,12},{10,14},{12,8},{14,10},{1,5},{3,7},... | collective-permute-start | bytes 61448 | tf_op jit(solution)/shard_map/ppermute | solution.py:621
  9.5 1.0 %early_forward.2 = (bf16[2,256,512]{2,1,0:T(8,128)(2,1)S(1)}, f32[2,256,512]{2,1,0:T(8,128)S(1)}, bf16[2,256,512]{2,1,0:T(8,128)(2,1)S(1)}, f32[2,256,512]{2,1,0:T(8,128)S(1)}) custom-call(bf16[2,8,640]{2,1,0:T(8,128)(2,1)S(1)} %pad_maximum_fusion.2.gathered_ref, bf16[256,512]{1,0:T(8,128)(2,1)S(1)} %prepare_weights.1.weights_ref), custom_call_target="tpu_custom_call" | custom-call | tf_op jit(solution)/shard_map/early_forward/pallas_call | solution.py:514
  10.5 0.0 copy-start.1
  10.5 0.8 %collective-permute-done.1 = bf16[2,8,640]{2,1,0:T(8,128)(2,1)S(1)} collective-permute-done((bf16[2,8,640]{2,1,0:T(8,128)(2,1)S(1)}, bf16[2,8,640]{2,1,0:T(8,128)(2,1)S(1)}, u32[]{:S(2)}, u32[]{:S(2)}) %collective-permute-start.1) | collective-permute-done | bytes 20512 | tf_op jit(solution)/shard_map/ppermute | solution.py:621
  11.4 3.0 %collective-permute-start.2 = (bf16[4,8,640]{2,1,0:T(8,128)(2,1)S(1)}, bf16[4,8,640]{2,1,0:T(8,128)(2,1)S(1)}, u32[]{:S(2)}, u32[]{:S(2)}) collective-permute-start(bf16[4,8,640]{2,1,0:T(8,128)(2,1)S(1)} %pad_maximum_fusion.1.gathered_ref), channel_id=1, source_target_pairs={{0,8},{2,10},{4,12},{6,14},{8,0},{10,2},{12,4},{14,6},{1,9},{3,11}... | collective-permute-start | bytes 122888 | tf_op jit(solution)/shard_map/ppermute | solution.py:621
  14.4 0.1 pad_add_fusion.place_ref
  14.5 1.0 %early_forward.3 = (bf16[2,256,512]{2,1,0:T(8,128)(2,1)S(1)}, f32[2,256,512]{2,1,0:T(8,128)S(1)}, bf16[2,256,512]{2,1,0:T(8,128)(2,1)S(1)}, f32[2,256,512]{2,1,0:T(8,128)S(1)}) custom-call(bf16[4,8,640]{2,1,0:T(8,128)(2,1)S(1)} %pad_maximum_fusion.1.gathered_ref, bf16[256,512]{1,0:T(8,128)(2,1)S(1)} %prepare_weights.1.weights_ref), custom_call_target="tpu_custom_call" | custom-call | tf_op jit(solution)/shard_map/early_forward/pallas_call | solution.py:514
  15.5 0.9 %collective-permute-done.2 = bf16[4,8,640]{2,1,0:T(8,128)(2,1)S(1)} collective-permute-done((bf16[4,8,640]{2,1,0:T(8,128)(2,1)S(1)}, bf16[4,8,640]{2,1,0:T(8,128)(2,1)S(1)}, u32[]{:S(2)}, u32[]{:S(2)}) %collective-permute-start.2) | collective-permute-done | bytes 40992 | tf_op jit(solution)/shard_map/ppermute | solution.py:621
  16.4 0.0 copy-done.1
  16.4 7.6 %all_cells.1 = (bf16[448,256]{1,0:T(8,128)(2,1)S(1)}, f32[8,512]{1,0:T(8,128)}) custom-call(s32[2]{0:T(128)S(1)} %pad_add_fusion.place_ref, bf16[8,8,640]{2,1,0:T(8,128)(2,1)S(1)} %pad_maximum_fusion.gathered_ref, bf16[256,512]{1,0:T(8,128)(2,1)S(1)} %prepare_weights.1.weights_ref, bf16[672,256]{1,0:T(8,128)(2,1)S(1)} %copy-done.1, ...), custom_call_target="tpu_custom_call" | custom-call | tf_op jit(solution)/shard_map/all_cells/pallas_call | solution.py:532
  24.0 0.0 collective-permute-start.3
  24.0 1.5 %collective-permute-done.3.other_ref = bf16[448,256]{1,0:T(8,128)(2,1)S(1)} collective-permute-done((bf16[448,256]{1,0:T(8,128)(2,1)S(1)}, bf16[448,256]{1,0:T(8,128)(2,1)S(1)}, u32[]{:S(2)}, u32[]{:S(2)}) %collective-permute-start.3) | collective-permute-done | bytes 229408 | tf_op jit(solution)/shard_map/ppermute | solution.py:633
  25.5 1.0 %finish_sums.1 = (f32[256,128]{1,0:T(8,128)}, f32[256,256]{1,0:T(8,128)}, f32[1,256]{1,0:T(1,128)}, f32[256,256]{1,0:T(8,128)}, f32[1,256]{1,0:T(1,128)}, /*index=5*/f32[16,256]{1,0:T(8,128)}, f32[8,256]{1,0:T(8,128)}) custom-call(bf16[448,256]{1,0:T(8,128)(2,1)S(1)} %get-tuple-element.69.own_ref, bf16[448,256]{1,0:T(8,128)(2,1)S(1)} %collective-permute-done.3.other_ref, ...), custom_call_target="tpu_custom_call" | custom-call | tf_op jit(solution)/shard_map/finish_sums/pallas_call | solution.py:635
  (4 shorter events, 0.0 us)
Async XLA Ops:
  2.5 5.0 %collective-permute-start = (bf16[1,8,640]{2,1,0:T(8,128)(2,1)}, bf16[1,8,640]{2,1,0:T(8,128)(2,1)S(1)}, u32[]{:S(2)}, u32[]{:S(2)}) collective-permute-start(bf16[1,8,640]{2,1,0:T(8,128)(2,1)} %bitcast.14), channel_id=1, source_target_pairs={{0,2},{2,0},{4,6},{6,4},{8,10},{10,8},{12,14},{14,12},{1,3},{3,1},... | collective-permute-start | bytes 30728 | tf_op jit(solution)/shard_map/ppermute | solution.py:610
  5.5 0.7 %copy-start.2 = (bf16[8,640]{1,0:T(8,128)(2,1)S(1)}, bf16[8,640]{1,0:T(8,128)(2,1)}, u32[]{:S(2)}) copy-start(bf16[8,640]{1,0:T(8,128)(2,1)} %get-tuple-element.43.packed_ref) | copy-start | bytes 30724
  6.2 1.0 %copy-start = (bf16[672,256]{1,0:T(8,128)(2,1)S(1)}, bf16[672,256]{1,0:T(8,128)(2,1)}, u32[]{:S(2)}) copy-start(bf16[672,256]{1,0:T(8,128)(2,1)} %get-tuple-element.44.flat_ref) | copy-start | bytes 1032196
  7.5 3.8 %collective-permute-start.1 = (bf16[2,8,640]{2,1,0:T(8,128)(2,1)S(1)}, bf16[2,8,640]{2,1,0:T(8,128)(2,1)S(1)}, u32[]{:S(2)}, u32[]{:S(2)}) collective-permute-start(bf16[2,8,640]{2,1,0:T(8,128)(2,1)S(1)} %pad_maximum_fusion.2.gathered_ref), channel_id=1, source_target_pairs={{0,4},{2,6},{4,0},{6,2},{8,12},{10,14},{12,8},{14,10},{1,5},{3,7},... | collective-permute-start | bytes 61448 | tf_op jit(solution)/shard_map/ppermute | solution.py:621
  10.5 5.9 %copy-start.1 = (bf16[672,256]{1,0:T(8,128)(2,1)S(1)}, bf16[672,256]{1,0:T(8,128)(2,1)}, u32[]{:S(2)}) copy-start(bf16[672,256]{1,0:T(8,128)(2,1)} %get-tuple-element.44.flat_ref) | copy-start | bytes 1032196
  11.4 5.0 %collective-permute-start.2 = (bf16[4,8,640]{2,1,0:T(8,128)(2,1)S(1)}, bf16[4,8,640]{2,1,0:T(8,128)(2,1)S(1)}, u32[]{:S(2)}, u32[]{:S(2)}) collective-permute-start(bf16[4,8,640]{2,1,0:T(8,128)(2,1)S(1)} %pad_maximum_fusion.1.gathered_ref), channel_id=1, source_target_pairs={{0,8},{2,10},{4,12},{6,14},{8,0},{10,2},{12,4},{14,6},{1,9},{3,11}... | collective-permute-start | bytes 122888 | tf_op jit(solution)/shard_map/ppermute | solution.py:621
  24.0 1.5 %collective-permute-start.3 = (bf16[448,256]{1,0:T(8,128)(2,1)S(1)}, bf16[448,256]{1,0:T(8,128)(2,1)S(1)}, u32[]{:S(2)}, u32[]{:S(2)}) collective-permute-start(bf16[448,256]{1,0:T(8,128)(2,1)S(1)} %get-tuple-element.69.own_ref), channel_id=1, source_target_pairs={{0,1},{1,0},{2,3},{3,2},{4,5},{5,4},{6,7},{7,6},{8,9},{9,8},{10,11... | collective-permute-start | bytes 688136 | tf_op jit(solution)/shard_map/ppermute | solution.py:633

commit v5 on v4

--- a/solution.py
+++ b/solution.py
@@ -18,6 +18,7 @@
 BF16 = jnp.bfloat16
 VMEM_BYTES = 40 * 1024 * 1024
 SMALL_ROWS = 32
+EARLY_BLOCKS = 1
 WHOLE_VMEM = 64 * 1024 * 1024 - 256 * 1024
 
 
@@ -295,6 +296,88 @@
     second(count - 1)
 
 
+def lay_targets(tiles, first_col, freqs, where, across, near, far):
+    count = len(tiles)
+    fill = [jnp.zeros((8 - count % 8, 128), F32)] if count % 8 else []
+    low = jnp.concatenate([tile[4:5] for tile in tiles] + fill, axis=0).T
+    high = jnp.concatenate([tile[5:6] for tile in tiles] + fill, axis=0).T
+    parts = [low[at * 16 : (at + 1) * 16] for at in range(8)]
+    parts += [high[at * 16 : (at + 1) * 16] for at in range(4)]
+    point_x = (parts[2] + parts[3]) + parts[4]
+    point_y = (parts[5] + parts[6]) + parts[7]
+    point_z = (parts[8] + parts[9]) + parts[10]
+    wave = (wave_low + (wave_high - wave_low) * parts[11] / (freqs - 1)) * (0.5 / math.pi)
+    cells = across.shape[1]
+    sides = [
+        first_col + lane + lax.broadcasted_iota(jnp.int32, (1, 128), 1)
+        for lane in range(0, cells, 128)
+    ]
+    sides = [lax.rem(side, SIDE).astype(F32) for side in sides]
+    grid = lax.broadcasted_iota(jnp.int32, (16, freqs), 1).astype(F32)
+    for chunk in range(count):
+        here = slice(chunk * 16, chunk * 16 + 16)
+
+        def spread(value):
+            return jnp.broadcast_to(value[:, chunk : chunk + 1], (16, 128))
+
+        square = spread(wave * wave)
+        where[0, here] = spread(point_y)
+        where[1, here] = spread(wave * wave * (point_z * point_z))
+        where[2, here] = spread(kernel_gain * point_z * (wave * wave))
+        where[3, here] = square
+        wide = spread(point_x)
+        for at, side in enumerate(sides):
+            offset = wide - side
+            across[here, at * 128 : (at + 1) * 128] = offset * offset * square
+        select = jnp.where(spread(parts[11])[:, 0:freqs] == grid, 1.0, 0.0)
+        part_a = select * spread(parts[0])[:, 0:freqs]
+        part_b = select * spread(parts[1])[:, 0:freqs]
+        near[here] = jnp.concatenate([part_a, part_b], axis=1)
+        far[here] = jnp.concatenate([part_b, -part_a], axis=1)
+
+
+def hologram_pieces(row, where, across, waves):
+    for at in range(0, across.shape[0], 16):
+        here = slice(at, at + 16)
+        offset = where[0, here] - row
+        rest = offset * offset * where[3, here] + where[1, here]
+        for lane in range(0, across.shape[1], 128):
+            lanes = slice(lane, lane + 128)
+            square = across[here, lanes] + rest
+            turns = square * lax.rsqrt(square)
+            part = turns - jnp.round(turns)
+            power = part * part
+            sine = part * (NEAR[1] * power + NEAR[0])
+            cosine = (power + FAR[1]) * power + FAR[0]
+            sine_square = sine * sine
+            cosine_square = cosine * cosine
+            norm = square * (sine_square + cosine_square)
+            amplitude = where[2, here] * pl.reciprocal(norm, approx=True)
+            waves[0, here, lanes] = (
+                amplitude * (cosine_square - sine_square)
+            ).astype(BF16)
+            waves[1, here, lanes] = (
+                amplitude * ((sine + sine) * cosine)
+            ).astype(BF16)
+            yield
+
+
+def early_kernel(freq_size, freqs, place_ref, gathered_ref, where, across, near, far, waves):
+    count, _, width = gathered_ref.shape
+    cells = width - 128
+    me, freq_rank = place_ref[0], place_ref[1]
+    local = lax.bitwise_and(me, count - 1)
+    tiles = [
+        gathered_ref[lax.bitwise_xor(local, at), :, cells:].astype(F32) for at in range(count)
+    ]
+    lay_targets(tiles, freq_rank * cells, freqs, where, across, near, far)
+    for block in range(waves.shape[0]):
+        chunk = lax.bitwise_xor(me, block)
+        row = ((chunk * freq_size + freq_rank) * cells // SIDE).astype(F32)
+        for _ in hologram_pieces(row, where, across, waves.at[block]):
+            pass
+
+
 def cell_kernel(
     freq_size,
     place_ref, gathered_ref, weights_ref, flat_ref, *refs
@@ -302,8 +385,9 @@
     chunks, _, width = gathered_ref.shape
     cells = width - 128
     hidden = flat_ref.shape[1]
-    early = [refs[at : at + 4] for at in range(0, len(refs) - 14, 4)]
-    sums_ref, grad_params_ref, across, where, lift, bias, totals, waves = refs[-14:-6]
+    early = [refs[at : at + 4] for at in range(5, len(refs) - 16, 4)]
+    early_where, early_across, early_near, early_far, early_waves = refs[0:5]
+    sums_ref, grad_params_ref, across, where, near, far, lift, bias, totals, waves = refs[-16:-6]
     delta_two, spectra = refs[-6:-4]
     early.append(refs[-4:])
     freqs = lift.shape[0] // 2
@@ -316,49 +400,26 @@
     stride = freq_size * cells
     second_ref = weights_ref.at[:, 128 : 128 + hidden]
 
-    rows = [gathered_ref[chunk ^ me, :, cells:].astype(F32) for chunk in range(chunks)]
-    low = jnp.concatenate([row[4:5] for row in rows], axis=0).T
-    high = jnp.concatenate([row[5:6] for row in rows], axis=0).T
-    parts = [low[at * 16 : (at + 1) * 16] for at in range(8)]
-    parts += [high[at * 16 : (at + 1) * 16] for at in range(4)]
-    point_x = (parts[2] + parts[3]) + parts[4]
-    point_y = (parts[5] + parts[6]) + parts[7]
-    point_z = (parts[8] + parts[9]) + parts[10]
-    wave = (wave_low + (wave_high - wave_low) * parts[11] / (freqs - 1)) * (0.5 / math.pi)
-    sides = [
-        freq_rank * cells + lane + lax.broadcasted_iota(jnp.int32, (1, 128), 1)
-        for lane in range(0, cells, 128)
+    ready = chunks - refs[-4].shape[0]
+    upper_first = lax.bitwise_and(me, ready) != 0
+
+    def in_order(own, new):
+        low = lax.select(upper_first, new, own)
+        return jnp.concatenate([low, lax.select(upper_first, own, new)], axis=0)
+
+    local = lax.bitwise_and(me, ready - 1)
+    tiles = [
+        gathered_ref[ready + lax.bitwise_xor(local, at), :, cells:].astype(F32)
+        for at in range(ready)
     ]
-    sides = [lax.rem(side, SIDE).astype(F32) for side in sides]
-    grid = lax.broadcasted_iota(jnp.int32, (16, freqs), 1).astype(F32)
-    near, far = [], []
-    for chunk in range(chunks):
-        here = slice(chunk * 16, chunk * 16 + 16)
-
-        def spread(value):
-            return jnp.broadcast_to(value[:, chunk : chunk + 1], (16, 128))
-
-        where[0, here] = spread(point_y)
-        where[1, here] = spread(wave * wave * (point_z * point_z))
-        where[2, here] = spread(kernel_gain * point_z * (wave * wave))
-        where[3, here] = spread(wave * wave)
-        wide = spread(point_x)
-        for at, side in enumerate(sides):
-            offset = wide - side
-            across[here, at * 128 : (at + 1) * 128] = offset * offset * where[3, here]
-        select = jnp.where(spread(parts[11])[:, 0:freqs] == grid, 1.0, 0.0)
-        part_a = select * spread(parts[0])[:, 0:freqs]
-        part_b = select * spread(parts[1])[:, 0:freqs]
-        near.append(jnp.concatenate([part_a, part_b], axis=1))
-        far.append(jnp.concatenate([part_b, -part_a], axis=1))
-    lift[:, 0:targets] = jnp.concatenate(near, axis=0).T.astype(BF16)
-    lift[:, targets:] = jnp.concatenate(far, axis=0).T.astype(BF16)
+    lay_targets(tiles, freq_rank * cells, freqs, where, across, near, far)
+    lift[:, 0:targets] = in_order(early_near[...], near[...]).T.astype(BF16)
+    lift[:, targets:] = in_order(early_far[...], far[...]).T.astype(BF16)
     bias[...] = bias_of(weights_ref)
 
     middle = hidden + 32
     top = middle + 2 * freqs
     owners = [(part, at) for part in early for at in range(part[0].shape[0])]
-    ready = chunks - refs[-4].shape[0]
 
     def layers(block):
         part, at = owners[block]
@@ -370,30 +431,15 @@
         return jnp.concatenate([upper_rows, lower_rows], axis=0)
 
     def holograms(block, even):
-        chunk = lax.bitwise_xor(me, block)
-        row = ((chunk * stride + freq_rank * cells) // SIDE).astype(F32)
-        for at in range(0, targets, 16):
-            here = slice(at, at + 16)
-            offset = where[0, here] - row
-            rest = offset * offset * where[3, here] + where[1, here]
-            for lane in range(0, cells, 128):
-                square = across[here, lane : lane + 128] + rest
-                turns = square * lax.rsqrt(square)
-                part = turns - jnp.round(turns)
-                power = part * part
-                sine = part * (NEAR[1] * power + NEAR[0])
-                cosine = (power + FAR[1]) * power + FAR[0]
-                sine_square = sine * sine
-                cosine_square = cosine * cosine
-                norm = square * (sine_square + cosine_square)
-                amplitude = where[2, here] * pl.reciprocal(norm, approx=True)
-                waves[even, at : at + 16, lane : lane + 128] = (
-                    amplitude * (cosine_square - sine_square)
-                ).astype(BF16)
-                waves[even, targets + at : targets + at + 16, lane : lane + 128] = (
-                    amplitude * ((sine + sine) * cosine)
-                ).astype(BF16)
-                yield
+        row = ((lax.bitwise_xor(me, block) * stride + freq_rank * cells) // SIDE).astype(F32)
+        if block >= EARLY_BLOCKS:
+            yield from hologram_pieces(row, early_where, early_across, waves.at[even, 0])
+        yield from hologram_pieces(row, where, across, waves.at[even, 1])
+
+    def kernels_of(block, even):
+        own = early_waves.at[block] if block < EARLY_BLOCKS else waves.at[even, 0]
+        new = waves.at[even, 1]
+        return jnp.concatenate([in_order(own[at], new[at]) for at in range(2)], axis=0)
 
     def lower(block, even):
         total = totals.at[lax.bitwise_xor(me, block) // 2]
@@ -421,7 +467,7 @@
         yield
 
     def upper(block, even):
-        spectrum = dot(lift[...], waves[even]).astype(BF16)
+        spectrum = dot(lift[...], kernels_of(block, even)).astype(BF16)
         spectra[even] = spectrum
         yield
         back = back_out(spectrum)
@@ -456,8 +502,10 @@
             waiting.append((first(at + ready), 2))
         spots = sum(count for _, count in waiting)
         waiting = [stage for stage, _ in waiting]
-        pieces = (targets // 16) * (cells // 128) if at < chunks else 0
-        extra = holograms(at, at % 2)
+        pieces, extra = 0, None
+        if at < chunks:
+            pieces = (targets // (32 if at < EARLY_BLOCKS else 16)) * (cells // 128)
+            extra = holograms(at, at % 2)
         done, drawn = 0, 0
         while waiting:
             for stage in list(waiting):
@@ -520,7 +568,27 @@
     )(gathered, weights)
 
 
-def run_cells(place, gathered, weights, flat, early, freq_size, out_dim):
+def run_early(place, gathered, freq_size, out_dim):
+    count, _, width = gathered.shape
+    cells = width - 128
+    known = count * 16
+    vmem = pl.BlockSpec(memory_space=pltpu.VMEM)
+    return pl.pallas_call(
+        functools.partial(early_kernel, freq_size, out_dim // 2),
+        out_shape=[
+            jax.ShapeDtypeStruct((4, known, 128), F32),
+            jax.ShapeDtypeStruct((known, cells), F32),
+            jax.ShapeDtypeStruct((known, out_dim), F32),
+            jax.ShapeDtypeStruct((known, out_dim), F32),
+            jax.ShapeDtypeStruct((EARLY_BLOCKS, 2, known, cells), BF16),
+        ],
+        in_specs=[pl.BlockSpec(memory_space=pltpu.SMEM), vmem],
+        compiler_params=pltpu.CompilerParams(vmem_limit_bytes=VMEM_BYTES),
+        name="early_holograms",
+    )(place, gathered)
+
+
+def run_cells(place, gathered, weights, flat, waves, early, freq_size, out_dim):
     chunks, props, width = gathered.shape
     cells = width - 128
     hidden = flat.shape[1]
@@ -528,7 +596,7 @@
     rest = chunks - sum(part[0].shape[0] for part in early)
     rows = hidden + out_dim + 64
     vmem = pl.BlockSpec(memory_space=pltpu.VMEM)
-    flattened = [array for part in early for array in part]
+    flattened = list(waves) + [array for part in early for array in part]
     return pl.pallas_call(
         functools.partial(cell_kernel, freq_size),
         out_shape=(
@@ -538,12 +606,14 @@
         in_specs=[pl.BlockSpec(memory_space=pltpu.SMEM)] + [vmem] * (3 + len(flattened)),
         out_specs=(vmem, vmem),
         scratch_shapes=[
-            pltpu.VMEM((targets, cells), F32),
-            pltpu.VMEM((4, targets, 128), F32),
+            pltpu.VMEM((targets // 2, cells), F32),
+            pltpu.VMEM((4, targets // 2, 128), F32),
+            pltpu.VMEM((targets // 2, out_dim), F32),
+            pltpu.VMEM((targets // 2, out_dim), F32),
             pltpu.VMEM((out_dim, 2 * targets), BF16),
             pltpu.VMEM((hidden, 128), F32),
             pltpu.VMEM((chunks // 2, rows, hidden), F32),
-            pltpu.VMEM((2, 2 * targets, cells), BF16),
+            pltpu.VMEM((2, 2, 2, targets // 2, cells), BF16),
             pltpu.VMEM((2, hidden, cells), BF16),
             pltpu.VMEM((2, out_dim, cells), BF16),
         ]
@@ -616,18 +686,21 @@
     )(flat)
     gathered = jnp.concatenate([staged[None], moved], axis=0)
     gathered, weights = lax.optimization_barrier((gathered, weights))
+    place = jnp.stack([lax.axis_index("cells"), lax.axis_index("freq")]).astype(jnp.int32)
+    out_dim = w_out.shape[1]
     reach, begin, early = 2, 0, []
     while reach < chunks:
         moved = lax.ppermute(gathered, "cells", [(at, at ^ reach) for at in range(chunks)])
         early.append(run_forward(gathered, weights, begin, reach - begin))
+        if 2 * reach == chunks:
+            waves = run_early(place, gathered, freq_size, out_dim)
         begin = reach
         gathered = jnp.concatenate([gathered, moved], axis=0)
         gathered, early = lax.optimization_barrier((gathered, early))
         reach *= 2
 
-    place = jnp.stack([lax.axis_index("cells"), lax.axis_index("freq")]).astype(jnp.int32)
     sums, grad_params = run_cells(
-        place, gathered, weights, flat, early, freq_size, w_out.shape[1]
+        place, gathered, weights, flat, waves, early, freq_size, out_dim
     )
 
     other = lax.ppermute(sums, "freq", [(at, at ^ 1) for at in range(freq_size)])

time: 26.7 us -> 26.5 us (level)
  waiting for transfers between devices: 3.25 us -> 2.34 us
  Pallas kernels: 12.7 us -> 13.3 us
    pallas_call x0 -> x1, Pallas kernels: none -> 0.93 us  [run_early(): pl.pallas_call(functools.partial(early_kernel, freq_size, out_dim // 2),...]
    ppermute x2, waiting for transfers between devices: 1.77 us -> 0.85 us  [small_body(): lax.ppermute(gathered, 'cells', [(at, at ^ reach) for at in range(chunks)])]
  transfers between devices with their start and end apart: 4 -> 4, of which waited for: 3 -> 2; matrix products, arithmetic and copies ran while one was open for 0% -> 0% of each run, Pallas kernels for 8% -> 12%
where the time goes in v5:
time: 26.5 us; the launch traced here: 26.3 us
  Pallas kernels  13.3 us (50%)
  starting transfers between devices  8.03 us (30%)
  waiting for transfers between devices  2.34 us (9%)
  local copies, waits for them, and re-layouts  1.72 us (6%)
  between operations  0.73 us (3%)
    pallas_call x1, Pallas kernels, run_cells(): pl.pallas_call(functools.partial(cell_kernel, freq_size), out_shape=(jax....  7.32 us
    ppermute x2, starting transfers between devices, small_body(): lax.ppermute(gathered, 'cells', [(at, at ^ reach) for at in range(chunks)])  5.02 us
    ppermute x1, starting transfers between devices, small_body(): lax.ppermute(packed[None], 'cells', [(at, at ^ 1) for at in range(chunks)])  3 us
    pallas_call x2, Pallas kernels, run_forward(): pl.pallas_call(functools.partial(forward_kernel, begin), out_shape=[jax.S...  1.96 us
    pallas_call x1, Pallas kernels, small_body(): pl.pallas_call(pack_kernel, out_shape=(shape((props, cells + 128), BF16),...  1.86 us
    unnamed x6, local copies, waits for them, and re-layouts  1.72 us
    ppermute x1, waiting for transfers between devices, small_body(): lax.ppermute(sums, 'freq', [(at, at ^ 1) for at in range(freq_size)])  1.49 us
    pallas_call x1, Pallas kernels, small_body(): pl.pallas_call(functools.partial(finish_kernel, scale), out_shape=(shape(...  0.99 us
  transfers between devices with their start and end apart: 4, of which 2 were waited for; matrix products, arithmetic and copies ran while one was open for 0% of the time, Pallas kernels for 12%

profile of v5, /device:TPU:0, one launch (start us, length us, event | category | flops | bytes accessed | tf_op | source)
XLA Modules:
  0.0 26.3 jit_solution(1369984790545104187)
XLA Ops:
  0.6 1.9 %pack_inputs.1 = (bf16[8,640]{1,0:T(8,128)(2,1)}, bf16[672,256]{1,0:T(8,128)(2,1)}) custom-call(bf16[256,256]{1,0:T(8,128)(2,1)} %refs_0_.1, bf16[256,256]{1,0:T(8,128)(2,1)} %refs_1_.1, bf16[256,128]{1,0:T(8,128)(2,1)} %refs_2_.1, f32[2,16]{1,0:T(2,128)} %refs_3_.1, f32[1,16]{1,0:T(1,128)} %bitcast.18, f32[1,16]{1,0:T(1,128)} %bitcast.19, ...), custom_call_target="tpu_custom_call" | custom-call | tf_op jit(solution)/shard_map/pack_inputs/pallas_call | solution.py:663
  2.5 3.0 %collective-permute-start = (bf16[1,8,640]{2,1,0:T(8,128)(2,1)}, bf16[1,8,640]{2,1,0:T(8,128)(2,1)S(1)}, u32[]{:S(2)}, u32[]{:S(2)}) collective-permute-start(bf16[1,8,640]{2,1,0:T(8,128)(2,1)} %bitcast.14), channel_id=1, source_target_pairs={{0,2},{2,0},{4,6},{6,4},{8,10},{10,8},{12,14},{14,12},{1,3},{3,1},... | collective-permute-start | bytes 30728 | tf_op jit(solution)/shard_map/ppermute | solution.py:680
  5.5 0.0 copy-start.2
  5.5 0.7 %copy-done.2 = bf16[8,640]{1,0:T(8,128)(2,1)S(1)} copy-done((bf16[8,640]{1,0:T(8,128)(2,1)S(1)}, bf16[8,640]{1,0:T(8,128)(2,1)}, u32[]{:S(2)}) %copy-start.2) | copy-done | bytes 10264
  6.2 0.0 copy-start
  6.2 1.0 %copy-done = bf16[672,256]{1,0:T(8,128)(2,1)S(1)} copy-done((bf16[672,256]{1,0:T(8,128)(2,1)S(1)}, bf16[672,256]{1,0:T(8,128)(2,1)}, u32[]{:S(2)}) %copy-start) | copy-done | bytes 344088
  7.2 0.3 %prepare_weights.1.weights_ref = bf16[256,512]{1,0:T(8,128)(2,1)S(1)} custom-call(bf16[672,256]{1,0:T(8,128)(2,1)S(1)} %copy-done), custom_call_target="tpu_custom_call" | custom-call | tf_op jit(solution)/shard_map/prepare_weights/pallas_call | solution.py:681
  7.5 0.0 collective-permute-done
  7.5 2.0 %collective-permute-start.1 = (bf16[2,8,640]{2,1,0:T(8,128)(2,1)S(1)}, bf16[2,8,640]{2,1,0:T(8,128)(2,1)S(1)}, u32[]{:S(2)}, u32[]{:S(2)}) collective-permute-start(bf16[2,8,640]{2,1,0:T(8,128)(2,1)S(1)} %pad_maximum_fusion.2.gathered_ref), channel_id=1, source_target_pairs={{0,4},{2,6},{4,0},{6,2},{8,12},{10,14},{12,8},{14,10},{1,5},{3,7},... | collective-permute-start | bytes 61448 | tf_op jit(solution)/shard_map/ppermute | solution.py:693
  9.5 1.0 %early_forward.2 = (bf16[2,256,512]{2,1,0:T(8,128)(2,1)S(1)}, f32[2,256,512]{2,1,0:T(8,128)S(1)}, bf16[2,256,512]{2,1,0:T(8,128)(2,1)S(1)}, f32[2,256,512]{2,1,0:T(8,128)S(1)}) custom-call(bf16[2,8,640]{2,1,0:T(8,128)(2,1)S(1)} %pad_maximum_fusion.2.gathered_ref, bf16[256,512]{1,0:T(8,128)(2,1)S(1)} %prepare_weights.1.weights_ref), custom_call_target="tpu_custom_call" | custom-call | tf_op jit(solution)/shard_map/early_forward/pallas_call | solution.py:562
  10.5 0.0 copy-start.1
  10.5 0.8 %collective-permute-done.1 = bf16[2,8,640]{2,1,0:T(8,128)(2,1)S(1)} collective-permute-done((bf16[2,8,640]{2,1,0:T(8,128)(2,1)S(1)}, bf16[2,8,640]{2,1,0:T(8,128)(2,1)S(1)}, u32[]{:S(2)}, u32[]{:S(2)}) %collective-permute-start.1) | collective-permute-done | bytes 20512 | tf_op jit(solution)/shard_map/ppermute | solution.py:693
  11.4 3.0 %collective-permute-start.2 = (bf16[4,8,640]{2,1,0:T(8,128)(2,1)S(1)}, bf16[4,8,640]{2,1,0:T(8,128)(2,1)S(1)}, u32[]{:S(2)}, u32[]{:S(2)}) collective-permute-start(bf16[4,8,640]{2,1,0:T(8,128)(2,1)S(1)} %pad_maximum_fusion.1.gathered_ref), channel_id=1, source_target_pairs={{0,8},{2,10},{4,12},{6,14},{8,0},{10,2},{12,4},{14,6},{1,9},{3,11}... | collective-permute-start | bytes 122888 | tf_op jit(solution)/shard_map/ppermute | solution.py:693
  14.4 0.1 pad_add_fusion.place_ref
  14.5 1.0 %early_forward.3 = (bf16[2,256,512]{2,1,0:T(8,128)(2,1)S(1)}, f32[2,256,512]{2,1,0:T(8,128)S(1)}, bf16[2,256,512]{2,1,0:T(8,128)(2,1)S(1)}, f32[2,256,512]{2,1,0:T(8,128)S(1)}) custom-call(bf16[4,8,640]{2,1,0:T(8,128)(2,1)S(1)} %pad_maximum_fusion.1.gathered_ref, bf16[256,512]{1,0:T(8,128)(2,1)S(1)} %prepare_weights.1.weights_ref), custom_call_target="tpu_custom_call" | custom-call | tf_op jit(solution)/shard_map/early_forward/pallas_call | solution.py:562
  15.5 0.9 %early_holograms.1 = (f32[4,64,128]{2,1,0:T(8,128)S(1)}, f32[64,512]{1,0:T(8,128)S(1)}, f32[64,128]{1,0:T(8,128)S(1)}, f32[64,128]{1,0:T(8,128)S(1)}, bf16[1,2,64,512]{3,2,1,0:T(8,128)(2,1)S(1)}) custom-call(s32[2]{0:T(128)S(1)} %pad_add_fusion.place_ref, bf16[4,8,640]{2,1,0:T(8,128)(2,1)S(1)} %pad_maximum_fusion.1.gathered_ref), custom_call_target="tpu_custom_call" | custom-call | tf_op jit(solution)/shard_map/early_holograms/pallas_call | solution.py:576
  16.4 0.0 collective-permute-done.2
  16.5 0.0 copy-done.1
  16.5 7.3 %all_cells.1 = (bf16[448,256]{1,0:T(8,128)(2,1)S(1)}, f32[8,512]{1,0:T(8,128)}) custom-call(s32[2]{0:T(128)S(1)} %pad_add_fusion.place_ref, bf16[8,8,640]{2,1,0:T(8,128)(2,1)S(1)} %pad_maximum_fusion.gathered_ref, bf16[256,512]{1,0:T(8,128)(2,1)S(1)} %prepare_weights.1.weights_ref, bf16[672,256]{1,0:T(8,128)(2,1)S(1)} %copy-done.1, ...), custom_call_target="tpu_custom_call" | custom-call | tf_op jit(solution)/shard_map/all_cells/pallas_call | solution.py:600
  23.8 0.0 collective-permute-start.3
  23.8 1.5 %collective-permute-done.3.other_ref = bf16[448,256]{1,0:T(8,128)(2,1)S(1)} collective-permute-done((bf16[448,256]{1,0:T(8,128)(2,1)S(1)}, bf16[448,256]{1,0:T(8,128)(2,1)S(1)}, u32[]{:S(2)}, u32[]{:S(2)}) %collective-permute-start.3) | collective-permute-done | bytes 229408 | tf_op jit(solution)/shard_map/ppermute | solution.py:706
  25.3 1.0 %finish_sums.1 = (f32[256,128]{1,0:T(8,128)}, f32[256,256]{1,0:T(8,128)}, f32[1,256]{1,0:T(1,128)}, f32[256,256]{1,0:T(8,128)}, f32[1,256]{1,0:T(1,128)}, /*index=5*/f32[16,256]{1,0:T(8,128)}, f32[8,256]{1,0:T(8,128)}) custom-call(bf16[448,256]{1,0:T(8,128)(2,1)S(1)} %get-tuple-element.79.own_ref, bf16[448,256]{1,0:T(8,128)(2,1)S(1)} %collective-permute-done.3.other_ref, ...), custom_call_target="tpu_custom_call" | custom-call | tf_op jit(solution)/shard_map/finish_sums/pallas_call | solution.py:708
  (4 shorter events, 0.0 us)
Async XLA Ops:
  2.5 5.0 %collective-permute-start = (bf16[1,8,640]{2,1,0:T(8,128)(2,1)}, bf16[1,8,640]{2,1,0:T(8,128)(2,1)S(1)}, u32[]{:S(2)}, u32[]{:S(2)}) collective-permute-start(bf16[1,8,640]{2,1,0:T(8,128)(2,1)} %bitcast.14), channel_id=1, source_target_pairs={{0,2},{2,0},{4,6},{6,4},{8,10},{10,8},{12,14},{14,12},{1,3},{3,1},... | collective-permute-start | bytes 30728 | tf_op jit(solution)/shard_map/ppermute | solution.py:680
  5.5 0.7 %copy-start.2 = (bf16[8,640]{1,0:T(8,128)(2,1)S(1)}, bf16[8,640]{1,0:T(8,128)(2,1)}, u32[]{:S(2)}) copy-start(bf16[8,640]{1,0:T(8,128)(2,1)} %get-tuple-element.48.packed_ref) | copy-start | bytes 30724
  6.2 1.0 %copy-start = (bf16[672,256]{1,0:T(8,128)(2,1)S(1)}, bf16[672,256]{1,0:T(8,128)(2,1)}, u32[]{:S(2)}) copy-start(bf16[672,256]{1,0:T(8,128)(2,1)} %get-tuple-element.49.flat_ref) | copy-start | bytes 1032196
  7.5 3.8 %collective-permute-start.1 = (bf16[2,8,640]{2,1,0:T(8,128)(2,1)S(1)}, bf16[2,8,640]{2,1,0:T(8,128)(2,1)S(1)}, u32[]{:S(2)}, u32[]{:S(2)}) collective-permute-start(bf16[2,8,640]{2,1,0:T(8,128)(2,1)S(1)} %pad_maximum_fusion.2.gathered_ref), channel_id=1, source_target_pairs={{0,4},{2,6},{4,0},{6,2},{8,12},{10,14},{12,8},{14,10},{1,5},{3,7},... | collective-permute-start | bytes 61448 | tf_op jit(solution)/shard_map/ppermute | solution.py:693
  10.5 5.9 %copy-start.1 = (bf16[672,256]{1,0:T(8,128)(2,1)S(1)}, bf16[672,256]{1,0:T(8,128)(2,1)}, u32[]{:S(2)}) copy-start(bf16[672,256]{1,0:T(8,128)(2,1)} %get-tuple-element.49.flat_ref) | copy-start | bytes 1032196
  11.4 5.0 %collective-permute-start.2 = (bf16[4,8,640]{2,1,0:T(8,128)(2,1)S(1)}, bf16[4,8,640]{2,1,0:T(8,128)(2,1)S(1)}, u32[]{:S(2)}, u32[]{:S(2)}) collective-permute-start(bf16[4,8,640]{2,1,0:T(8,128)(2,1)S(1)} %pad_maximum_fusion.1.gathered_ref), channel_id=1, source_target_pairs={{0,8},{2,10},{4,12},{6,14},{8,0},{10,2},{12,4},{14,6},{1,9},{3,11}... | collective-permute-start | bytes 122888 | tf_op jit(solution)/shard_map/ppermute | solution.py:693
  23.8 1.5 %collective-permute-start.3 = (bf16[448,256]{1,0:T(8,128)(2,1)S(1)}, bf16[448,256]{1,0:T(8,128)(2,1)S(1)}, u32[]{:S(2)}, u32[]{:S(2)}) collective-permute-start(bf16[448,256]{1,0:T(8,128)(2,1)S(1)} %get-tuple-element.79.own_ref), channel_id=1, source_target_pairs={{0,1},{1,0},{2,3},{3,2},{4,5},{5,4},{6,7},{7,6},{8,9},{9,8},{10,11... | collective-permute-start | bytes 688136 | tf_op jit(solution)/shard_map/ppermute | solution.py:706

commit v6 on v5

--- a/solution.py
+++ b/solution.py
@@ -453,6 +453,7 @@
         feature = feature_of(gathered_ref, block)
         delta = delta_two[even]
         back = dot(w2_ref[...], delta)
+        outer(middle, spectra[even], two[...])
         yield
         value = (back * slope[...]).astype(BF16)
         if block == 0:
@@ -461,8 +462,6 @@
         yield
         outer(0, jnp.concatenate([one[...], feature], axis=0), delta)
         yield
-        outer(middle, spectra[even], two[...])
-        yield
         outer(top, feature, value)
         yield
 
@@ -492,14 +491,14 @@
 
     for at in range(chunks + 2):
         waiting = []
-        if 0 <= at - 2 < chunks:
-            waiting.append((lower(at - 2, at % 2), 5))
         if 0 <= at - 1 < chunks:
             waiting.append((upper(at - 1, (at - 1) % 2), 3))
         if ready <= at + ready - 1 < chunks:
             waiting.append((second(at + ready - 1), 2))
         if at + ready < chunks:
             waiting.append((first(at + ready), 2))
+        if 0 <= at - 2 < chunks:
+            waiting.append((lower(at - 2, at % 2), 4))
         spots = sum(count for _, count in waiting)
         waiting = [stage for stage, _ in waiting]
         pieces, extra = 0, None

time: 26.5 us -> 26 us (0.981)
  Pallas kernels: 13.3 us -> 12.9 us
    pallas_call x1, Pallas kernels: 7.32 us -> 6.86 us  [run_cells(): pl.pallas_call(functools.partial(cell_kernel, freq_size), out_shape=(jax....]
where the time goes in v6:
time: 26 us; the launch traced here: 25.8 us
  Pallas kernels  12.9 us (50%)
  starting transfers between devices  8.03 us (31%)
  waiting for transfers between devices  2.34 us (9%)
  local copies, waits for them, and re-layouts  1.72 us (7%)
  between operations  0.73 us (3%)
    pallas_call x1, Pallas kernels, run_cells(): pl.pallas_call(functools.partial(cell_kernel, freq_size), out_shape=(jax....  6.86 us
    ppermute x2, starting transfers between devices, small_body(): lax.ppermute(gathered, 'cells', [(at, at ^ reach) for at in range(chunks)])  5.02 us
    ppermute x1, starting transfers between devices, small_body(): lax.ppermute(packed[None], 'cells', [(at, at ^ 1) for at in range(chunks)])  3 us
    pallas_call x2, Pallas kernels, run_forward(): pl.pallas_call(functools.partial(forward_kernel, begin), out_shape=[jax.S...  1.96 us
    pallas_call x1, Pallas kernels, small_body(): pl.pallas_call(pack_kernel, out_shape=(shape((props, cells + 128), BF16),...  1.86 us
    unnamed x6, local copies, waits for them, and re-layouts  1.72 us
    ppermute x1, waiting for transfers between devices, small_body(): lax.ppermute(sums, 'freq', [(at, at ^ 1) for at in range(freq_size)])  1.49 us
    pallas_call x1, Pallas kernels, small_body(): pl.pallas_call(functools.partial(finish_kernel, scale), out_shape=(shape(...  0.99 us
  transfers between devices with their start and end apart: 4, of which 2 were waited for; matrix products, arithmetic and copies ran while one was open for 0% of the time, Pallas kernels for 12%

profile of v6, /device:TPU:0, one launch (start us, length us, event | category | flops | bytes accessed | tf_op | source)
XLA Modules:
  0.0 25.8 jit_solution(17544263827928924157)
XLA Ops:
  0.6 1.9 %pack_inputs.1 = (bf16[8,640]{1,0:T(8,128)(2,1)}, bf16[672,256]{1,0:T(8,128)(2,1)}) custom-call(bf16[256,256]{1,0:T(8,128)(2,1)} %refs_0_.1, bf16[256,256]{1,0:T(8,128)(2,1)} %refs_1_.1, bf16[256,128]{1,0:T(8,128)(2,1)} %refs_2_.1, f32[2,16]{1,0:T(2,128)} %refs_3_.1, f32[1,16]{1,0:T(1,128)} %bitcast.18, f32[1,16]{1,0:T(1,128)} %bitcast.19, ...), custom_call_target="tpu_custom_call" | custom-call | tf_op jit(solution)/shard_map/pack_inputs/pallas_call | solution.py:662
  2.5 3.0 %collective-permute-start = (bf16[1,8,640]{2,1,0:T(8,128)(2,1)}, bf16[1,8,640]{2,1,0:T(8,128)(2,1)S(1)}, u32[]{:S(2)}, u32[]{:S(2)}) collective-permute-start(bf16[1,8,640]{2,1,0:T(8,128)(2,1)} %bitcast.14), channel_id=1, source_target_pairs={{0,2},{2,0},{4,6},{6,4},{8,10},{10,8},{12,14},{14,12},{1,3},{3,1},... | collective-permute-start | bytes 30728 | tf_op jit(solution)/shard_map/ppermute | solution.py:679
  5.5 0.0 copy-start.2
  5.5 0.7 %copy-done.2 = bf16[8,640]{1,0:T(8,128)(2,1)S(1)} copy-done((bf16[8,640]{1,0:T(8,128)(2,1)S(1)}, bf16[8,640]{1,0:T(8,128)(2,1)}, u32[]{:S(2)}) %copy-start.2) | copy-done | bytes 10264
  6.2 0.0 copy-start
  6.2 1.0 %copy-done = bf16[672,256]{1,0:T(8,128)(2,1)S(1)} copy-done((bf16[672,256]{1,0:T(8,128)(2,1)S(1)}, bf16[672,256]{1,0:T(8,128)(2,1)}, u32[]{:S(2)}) %copy-start) | copy-done | bytes 344088
  7.2 0.3 %prepare_weights.1.weights_ref = bf16[256,512]{1,0:T(8,128)(2,1)S(1)} custom-call(bf16[672,256]{1,0:T(8,128)(2,1)S(1)} %copy-done), custom_call_target="tpu_custom_call" | custom-call | tf_op jit(solution)/shard_map/prepare_weights/pallas_call | solution.py:680
  7.5 0.0 collective-permute-done
  7.5 2.0 %collective-permute-start.1 = (bf16[2,8,640]{2,1,0:T(8,128)(2,1)S(1)}, bf16[2,8,640]{2,1,0:T(8,128)(2,1)S(1)}, u32[]{:S(2)}, u32[]{:S(2)}) collective-permute-start(bf16[2,8,640]{2,1,0:T(8,128)(2,1)S(1)} %pad_maximum_fusion.2.gathered_ref), channel_id=1, source_target_pairs={{0,4},{2,6},{4,0},{6,2},{8,12},{10,14},{12,8},{14,10},{1,5},{3,7},... | collective-permute-start | bytes 61448 | tf_op jit(solution)/shard_map/ppermute | solution.py:692
  9.5 1.0 %early_forward.2 = (bf16[2,256,512]{2,1,0:T(8,128)(2,1)S(1)}, f32[2,256,512]{2,1,0:T(8,128)S(1)}, bf16[2,256,512]{2,1,0:T(8,128)(2,1)S(1)}, f32[2,256,512]{2,1,0:T(8,128)S(1)}) custom-call(bf16[2,8,640]{2,1,0:T(8,128)(2,1)S(1)} %pad_maximum_fusion.2.gathered_ref, bf16[256,512]{1,0:T(8,128)(2,1)S(1)} %prepare_weights.1.weights_ref), custom_call_target="tpu_custom_call" | custom-call | tf_op jit(solution)/shard_map/early_forward/pallas_call | solution.py:561
  10.5 0.0 copy-start.1
  10.5 0.8 %collective-permute-done.1 = bf16[2,8,640]{2,1,0:T(8,128)(2,1)S(1)} collective-permute-done((bf16[2,8,640]{2,1,0:T(8,128)(2,1)S(1)}, bf16[2,8,640]{2,1,0:T(8,128)(2,1)S(1)}, u32[]{:S(2)}, u32[]{:S(2)}) %collective-permute-start.1) | collective-permute-done | bytes 20512 | tf_op jit(solution)/shard_map/ppermute | solution.py:692
  11.4 3.0 %collective-permute-start.2 = (bf16[4,8,640]{2,1,0:T(8,128)(2,1)S(1)}, bf16[4,8,640]{2,1,0:T(8,128)(2,1)S(1)}, u32[]{:S(2)}, u32[]{:S(2)}) collective-permute-start(bf16[4,8,640]{2,1,0:T(8,128)(2,1)S(1)} %pad_maximum_fusion.1.gathered_ref), channel_id=1, source_target_pairs={{0,8},{2,10},{4,12},{6,14},{8,0},{10,2},{12,4},{14,6},{1,9},{3,11}... | collective-permute-start | bytes 122888 | tf_op jit(solution)/shard_map/ppermute | solution.py:692
  14.4 0.1 pad_add_fusion.place_ref
  14.5 1.0 %early_forward.3 = (bf16[2,256,512]{2,1,0:T(8,128)(2,1)S(1)}, f32[2,256,512]{2,1,0:T(8,128)S(1)}, bf16[2,256,512]{2,1,0:T(8,128)(2,1)S(1)}, f32[2,256,512]{2,1,0:T(8,128)S(1)}) custom-call(bf16[4,8,640]{2,1,0:T(8,128)(2,1)S(1)} %pad_maximum_fusion.1.gathered_ref, bf16[256,512]{1,0:T(8,128)(2,1)S(1)} %prepare_weights.1.weights_ref), custom_call_target="tpu_custom_call" | custom-call | tf_op jit(solution)/shard_map/early_forward/pallas_call | solution.py:561
  15.5 0.9 %early_holograms.1 = (f32[4,64,128]{2,1,0:T(8,128)S(1)}, f32[64,512]{1,0:T(8,128)S(1)}, f32[64,128]{1,0:T(8,128)S(1)}, f32[64,128]{1,0:T(8,128)S(1)}, bf16[1,2,64,512]{3,2,1,0:T(8,128)(2,1)S(1)}) custom-call(s32[2]{0:T(128)S(1)} %pad_add_fusion.place_ref, bf16[4,8,640]{2,1,0:T(8,128)(2,1)S(1)} %pad_maximum_fusion.1.gathered_ref), custom_call_target="tpu_custom_call" | custom-call | tf_op jit(solution)/shard_map/early_holograms/pallas_call | solution.py:575
  16.4 0.0 collective-permute-done.2
  16.5 0.0 copy-done.1
  16.5 6.9 %all_cells.1 = (bf16[448,256]{1,0:T(8,128)(2,1)S(1)}, f32[8,512]{1,0:T(8,128)}) custom-call(s32[2]{0:T(128)S(1)} %pad_add_fusion.place_ref, bf16[8,8,640]{2,1,0:T(8,128)(2,1)S(1)} %pad_maximum_fusion.gathered_ref, bf16[256,512]{1,0:T(8,128)(2,1)S(1)} %prepare_weights.1.weights_ref, bf16[672,256]{1,0:T(8,128)(2,1)S(1)} %copy-done.1, ...), custom_call_target="tpu_custom_call" | custom-call | tf_op jit(solution)/shard_map/all_cells/pallas_call | solution.py:599
  23.3 0.0 collective-permute-start.3
  23.3 1.5 %collective-permute-done.3.other_ref = bf16[448,256]{1,0:T(8,128)(2,1)S(1)} collective-permute-done((bf16[448,256]{1,0:T(8,128)(2,1)S(1)}, bf16[448,256]{1,0:T(8,128)(2,1)S(1)}, u32[]{:S(2)}, u32[]{:S(2)}) %collective-permute-start.3) | collective-permute-done | bytes 229408 | tf_op jit(solution)/shard_map/ppermute | solution.py:705
  24.8 1.0 %finish_sums.1 = (f32[256,128]{1,0:T(8,128)}, f32[256,256]{1,0:T(8,128)}, f32[1,256]{1,0:T(1,128)}, f32[256,256]{1,0:T(8,128)}, f32[1,256]{1,0:T(1,128)}, /*index=5*/f32[16,256]{1,0:T(8,128)}, f32[8,256]{1,0:T(8,128)}) custom-call(bf16[448,256]{1,0:T(8,128)(2,1)S(1)} %get-tuple-element.79.own_ref, bf16[448,256]{1,0:T(8,128)(2,1)S(1)} %collective-permute-done.3.other_ref, ...), custom_call_target="tpu_custom_call" | custom-call | tf_op jit(solution)/shard_map/finish_sums/pallas_call | solution.py:707
  (4 shorter events, 0.0 us)
Async XLA Ops:
  2.5 5.0 %collective-permute-start = (bf16[1,8,640]{2,1,0:T(8,128)(2,1)}, bf16[1,8,640]{2,1,0:T(8,128)(2,1)S(1)}, u32[]{:S(2)}, u32[]{:S(2)}) collective-permute-start(bf16[1,8,640]{2,1,0:T(8,128)(2,1)} %bitcast.14), channel_id=1, source_target_pairs={{0,2},{2,0},{4,6},{6,4},{8,10},{10,8},{12,14},{14,12},{1,3},{3,1},... | collective-permute-start | bytes 30728 | tf_op jit(solution)/shard_map/ppermute | solution.py:679
  5.5 0.7 %copy-start.2 = (bf16[8,640]{1,0:T(8,128)(2,1)S(1)}, bf16[8,640]{1,0:T(8,128)(2,1)}, u32[]{:S(2)}) copy-start(bf16[8,640]{1,0:T(8,128)(2,1)} %get-tuple-element.48.packed_ref) | copy-start | bytes 30724
  6.2 1.0 %copy-start = (bf16[672,256]{1,0:T(8,128)(2,1)S(1)}, bf16[672,256]{1,0:T(8,128)(2,1)}, u32[]{:S(2)}) copy-start(bf16[672,256]{1,0:T(8,128)(2,1)} %get-tuple-element.49.flat_ref) | copy-start | bytes 1032196
  7.5 3.8 %collective-permute-start.1 = (bf16[2,8,640]{2,1,0:T(8,128)(2,1)S(1)}, bf16[2,8,640]{2,1,0:T(8,128)(2,1)S(1)}, u32[]{:S(2)}, u32[]{:S(2)}) collective-permute-start(bf16[2,8,640]{2,1,0:T(8,128)(2,1)S(1)} %pad_maximum_fusion.2.gathered_ref), channel_id=1, source_target_pairs={{0,4},{2,6},{4,0},{6,2},{8,12},{10,14},{12,8},{14,10},{1,5},{3,7},... | collective-permute-start | bytes 61448 | tf_op jit(solution)/shard_map/ppermute | solution.py:692
  10.5 5.9 %copy-start.1 = (bf16[672,256]{1,0:T(8,128)(2,1)S(1)}, bf16[672,256]{1,0:T(8,128)(2,1)}, u32[]{:S(2)}) copy-start(bf16[672,256]{1,0:T(8,128)(2,1)} %get-tuple-element.49.flat_ref) | copy-start | bytes 1032196
  11.4 5.0 %collective-permute-start.2 = (bf16[4,8,640]{2,1,0:T(8,128)(2,1)S(1)}, bf16[4,8,640]{2,1,0:T(8,128)(2,1)S(1)}, u32[]{:S(2)}, u32[]{:S(2)}) collective-permute-start(bf16[4,8,640]{2,1,0:T(8,128)(2,1)S(1)} %pad_maximum_fusion.1.gathered_ref), channel_id=1, source_target_pairs={{0,8},{2,10},{4,12},{6,14},{8,0},{10,2},{12,4},{14,6},{1,9},{3,11}... | collective-permute-start | bytes 122888 | tf_op jit(solution)/shard_map/ppermute | solution.py:692
  23.3 1.5 %collective-permute-start.3 = (bf16[448,256]{1,0:T(8,128)(2,1)S(1)}, bf16[448,256]{1,0:T(8,128)(2,1)S(1)}, u32[]{:S(2)}, u32[]{:S(2)}) collective-permute-start(bf16[448,256]{1,0:T(8,128)(2,1)S(1)} %get-tuple-element.79.own_ref), channel_id=1, source_target_pairs={{0,1},{1,0},{2,3},{3,2},{4,5},{5,4},{6,7},{7,6},{8,9},{9,8},{10,11... | collective-permute-start | bytes 688136 | tf_op jit(solution)/shard_map/ppermute | solution.py:705

commit v7 on v6

--- a/solution.py
+++ b/solution.py
@@ -289,11 +289,10 @@
         two_ref[slot] = act
         slope_two_ref[slot] = slope
 
-    first(0)
-    for slot in range(1, count):
-        second(slot - 1)
+    for slot in range(count):
         first(slot)
-    second(count - 1)
+    for slot in range(count):
+        second(slot)
 
 
 def lay_targets(tiles, first_col, freqs, where, across, near, far):

time: 26 us -> 26 us (level)
  Pallas kernels: 12.9 us -> 12.5 us
  waiting for transfers between devices: 2.34 us -> 2.73 us
    pallas_call x2, Pallas kernels: 1.96 us -> 1.55 us  [run_forward(): pl.pallas_call(functools.partial(forward_kernel, begin), out_shape=[jax.S...]
    ppermute x2, waiting for transfers between devices: 0.85 us -> 1.24 us  [small_body(): lax.ppermute(gathered, 'cells', [(at, at ^ reach) for at in range(chunks)])]
  transfers between devices with their start and end apart: 4 -> 4, of which waited for: 2 -> 3; matrix products, arithmetic and copies ran while one was open for 0% -> 0% of each run, Pallas kernels for 12% -> 11%
where the time goes in v7:
time: 26 us; the launch traced here: 25.8 us
  Pallas kernels  12.5 us (48%)
  starting transfers between devices  8.03 us (31%)
  waiting for transfers between devices  2.73 us (10%)
  local copies, waits for them, and re-layouts  1.72 us (7%)
  between operations  0.72 us (3%)
    pallas_call x1, Pallas kernels, run_cells(): pl.pallas_call(functools.partial(cell_kernel, freq_size), out_shape=(jax....  6.85 us
    ppermute x2, starting transfers between devices, small_body(): lax.ppermute(gathered, 'cells', [(at, at ^ reach) for at in range(chunks)])  5.02 us
    ppermute x1, starting transfers between devices, small_body(): lax.ppermute(packed[None], 'cells', [(at, at ^ 1) for at in range(chunks)])  3 us
    pallas_call x1, Pallas kernels, small_body(): pl.pallas_call(pack_kernel, out_shape=(shape((props, cells + 128), BF16),...  1.86 us
    unnamed x6, local copies, waits for them, and re-layouts  1.72 us
    pallas_call x2, Pallas kernels, run_forward(): pl.pallas_call(functools.partial(forward_kernel, begin), out_shape=[jax.S...  1.55 us
    ppermute x1, waiting for transfers between devices, small_body(): lax.ppermute(sums, 'freq', [(at, at ^ 1) for at in range(freq_size)])  1.49 us
    ppermute x2, waiting for transfers between devices, small_body(): lax.ppermute(gathered, 'cells', [(at, at ^ reach) for at in range(chunks)])  1.24 us
  transfers between devices with their start and end apart: 4, of which 3 were waited for; matrix products, arithmetic and copies ran while one was open for 0% of the time, Pallas kernels for 11%

profile of v7, /device:TPU:0, one launch (start us, length us, event | category | flops | bytes accessed | tf_op | source)
XLA Modules:
  0.0 25.8 jit_solution(2906521271662733588)
XLA Ops:
  0.6 1.9 %pack_inputs.1 = (bf16[8,640]{1,0:T(8,128)(2,1)}, bf16[672,256]{1,0:T(8,128)(2,1)}) custom-call(bf16[256,256]{1,0:T(8,128)(2,1)} %refs_0_.1, bf16[256,256]{1,0:T(8,128)(2,1)} %refs_1_.1, bf16[256,128]{1,0:T(8,128)(2,1)} %refs_2_.1, f32[2,16]{1,0:T(2,128)} %refs_3_.1, f32[1,16]{1,0:T(1,128)} %bitcast.18, f32[1,16]{1,0:T(1,128)} %bitcast.19, ...), custom_call_target="tpu_custom_call" | custom-call | tf_op jit(solution)/shard_map/pack_inputs/pallas_call | solution.py:661
  2.5 3.0 %collective-permute-start = (bf16[1,8,640]{2,1,0:T(8,128)(2,1)}, bf16[1,8,640]{2,1,0:T(8,128)(2,1)S(1)}, u32[]{:S(2)}, u32[]{:S(2)}) collective-permute-start(bf16[1,8,640]{2,1,0:T(8,128)(2,1)} %bitcast.14), channel_id=1, source_target_pairs={{0,2},{2,0},{4,6},{6,4},{8,10},{10,8},{12,14},{14,12},{1,3},{3,1},... | collective-permute-start | bytes 30728 | tf_op jit(solution)/shard_map/ppermute | solution.py:678
  5.5 0.0 copy-start.2
  5.5 0.7 %copy-done.2 = bf16[8,640]{1,0:T(8,128)(2,1)S(1)} copy-done((bf16[8,640]{1,0:T(8,128)(2,1)S(1)}, bf16[8,640]{1,0:T(8,128)(2,1)}, u32[]{:S(2)}) %copy-start.2) | copy-done | bytes 10264
  6.2 0.0 copy-start
  6.2 1.0 %copy-done = bf16[672,256]{1,0:T(8,128)(2,1)S(1)} copy-done((bf16[672,256]{1,0:T(8,128)(2,1)S(1)}, bf16[672,256]{1,0:T(8,128)(2,1)}, u32[]{:S(2)}) %copy-start) | copy-done | bytes 344088
  7.2 0.3 %prepare_weights.1.weights_ref = bf16[256,512]{1,0:T(8,128)(2,1)S(1)} custom-call(bf16[672,256]{1,0:T(8,128)(2,1)S(1)} %copy-done), custom_call_target="tpu_custom_call" | custom-call | tf_op jit(solution)/shard_map/prepare_weights/pallas_call | solution.py:679
  7.5 0.0 collective-permute-done
  7.5 2.0 %collective-permute-start.1 = (bf16[2,8,640]{2,1,0:T(8,128)(2,1)S(1)}, bf16[2,8,640]{2,1,0:T(8,128)(2,1)S(1)}, u32[]{:S(2)}, u32[]{:S(2)}) collective-permute-start(bf16[2,8,640]{2,1,0:T(8,128)(2,1)S(1)} %pad_maximum_fusion.2.gathered_ref), channel_id=1, source_target_pairs={{0,4},{2,6},{4,0},{6,2},{8,12},{10,14},{12,8},{14,10},{1,5},{3,7},... | collective-permute-start | bytes 61448 | tf_op jit(solution)/shard_map/ppermute | solution.py:691
  9.5 0.8 %early_forward.2 = (bf16[2,256,512]{2,1,0:T(8,128)(2,1)S(1)}, f32[2,256,512]{2,1,0:T(8,128)S(1)}, bf16[2,256,512]{2,1,0:T(8,128)(2,1)S(1)}, f32[2,256,512]{2,1,0:T(8,128)S(1)}) custom-call(bf16[2,8,640]{2,1,0:T(8,128)(2,1)S(1)} %pad_maximum_fusion.2.gathered_ref, bf16[256,512]{1,0:T(8,128)(2,1)S(1)} %prepare_weights.1.weights_ref), custom_call_target="tpu_custom_call" | custom-call | tf_op jit(solution)/shard_map/early_forward/pallas_call | solution.py:560
  10.3 0.0 copy-start.1
  10.3 1.1 %collective-permute-done.1 = bf16[2,8,640]{2,1,0:T(8,128)(2,1)S(1)} collective-permute-done((bf16[2,8,640]{2,1,0:T(8,128)(2,1)S(1)}, bf16[2,8,640]{2,1,0:T(8,128)(2,1)S(1)}, u32[]{:S(2)}, u32[]{:S(2)}) %collective-permute-start.1) | collective-permute-done | bytes 20512 | tf_op jit(solution)/shard_map/ppermute | solution.py:691
  11.4 3.0 %collective-permute-start.2 = (bf16[4,8,640]{2,1,0:T(8,128)(2,1)S(1)}, bf16[4,8,640]{2,1,0:T(8,128)(2,1)S(1)}, u32[]{:S(2)}, u32[]{:S(2)}) collective-permute-start(bf16[4,8,640]{2,1,0:T(8,128)(2,1)S(1)} %pad_maximum_fusion.1.gathered_ref), channel_id=1, source_target_pairs={{0,8},{2,10},{4,12},{6,14},{8,0},{10,2},{12,4},{14,6},{1,9},{3,11}... | collective-permute-start | bytes 122888 | tf_op jit(solution)/shard_map/ppermute | solution.py:691
  14.4 0.1 pad_add_fusion.place_ref
  14.5 0.8 %early_forward.3 = (bf16[2,256,512]{2,1,0:T(8,128)(2,1)S(1)}, f32[2,256,512]{2,1,0:T(8,128)S(1)}, bf16[2,256,512]{2,1,0:T(8,128)(2,1)S(1)}, f32[2,256,512]{2,1,0:T(8,128)S(1)}) custom-call(bf16[4,8,640]{2,1,0:T(8,128)(2,1)S(1)} %pad_maximum_fusion.1.gathered_ref, bf16[256,512]{1,0:T(8,128)(2,1)S(1)} %prepare_weights.1.weights_ref), custom_call_target="tpu_custom_call" | custom-call | tf_op jit(solution)/shard_map/early_forward/pallas_call | solution.py:560
  15.3 0.9 %early_holograms.1 = (f32[4,64,128]{2,1,0:T(8,128)S(1)}, f32[64,512]{1,0:T(8,128)S(1)}, f32[64,128]{1,0:T(8,128)S(1)}, f32[64,128]{1,0:T(8,128)S(1)}, bf16[1,2,64,512]{3,2,1,0:T(8,128)(2,1)S(1)}) custom-call(s32[2]{0:T(128)S(1)} %pad_add_fusion.place_ref, bf16[4,8,640]{2,1,0:T(8,128)(2,1)S(1)} %pad_maximum_fusion.1.gathered_ref), custom_call_target="tpu_custom_call" | custom-call | tf_op jit(solution)/shard_map/early_holograms/pallas_call | solution.py:574
  16.2 0.2 collective-permute-done.2
  16.4 0.0 copy-done.1
  16.4 6.9 %all_cells.1 = (bf16[448,256]{1,0:T(8,128)(2,1)S(1)}, f32[8,512]{1,0:T(8,128)}) custom-call(s32[2]{0:T(128)S(1)} %pad_add_fusion.place_ref, bf16[8,8,640]{2,1,0:T(8,128)(2,1)S(1)} %pad_maximum_fusion.gathered_ref, bf16[256,512]{1,0:T(8,128)(2,1)S(1)} %prepare_weights.1.weights_ref, bf16[672,256]{1,0:T(8,128)(2,1)S(1)} %copy-done.1, ...), custom_call_target="tpu_custom_call" | custom-call | tf_op jit(solution)/shard_map/all_cells/pallas_call | solution.py:598
  23.3 0.0 collective-permute-start.3
  23.3 1.5 %collective-permute-done.3.other_ref = bf16[448,256]{1,0:T(8,128)(2,1)S(1)} collective-permute-done((bf16[448,256]{1,0:T(8,128)(2,1)S(1)}, bf16[448,256]{1,0:T(8,128)(2,1)S(1)}, u32[]{:S(2)}, u32[]{:S(2)}) %collective-permute-start.3) | collective-permute-done | bytes 229408 | tf_op jit(solution)/shard_map/ppermute | solution.py:704
  24.8 1.0 %finish_sums.1 = (f32[256,128]{1,0:T(8,128)}, f32[256,256]{1,0:T(8,128)}, f32[1,256]{1,0:T(1,128)}, f32[256,256]{1,0:T(8,128)}, f32[1,256]{1,0:T(1,128)}, /*index=5*/f32[16,256]{1,0:T(8,128)}, f32[8,256]{1,0:T(8,128)}) custom-call(bf16[448,256]{1,0:T(8,128)(2,1)S(1)} %get-tuple-element.79.own_ref, bf16[448,256]{1,0:T(8,128)(2,1)S(1)} %collective-permute-done.3.other_ref, ...), custom_call_target="tpu_custom_call" | custom-call | tf_op jit(solution)/shard_map/finish_sums/pallas_call | solution.py:706
  (4 shorter events, 0.0 us)
Async XLA Ops:
  2.5 5.0 %collective-permute-start = (bf16[1,8,640]{2,1,0:T(8,128)(2,1)}, bf16[1,8,640]{2,1,0:T(8,128)(2,1)S(1)}, u32[]{:S(2)}, u32[]{:S(2)}) collective-permute-start(bf16[1,8,640]{2,1,0:T(8,128)(2,1)} %bitcast.14), channel_id=1, source_target_pairs={{0,2},{2,0},{4,6},{6,4},{8,10},{10,8},{12,14},{14,12},{1,3},{3,1},... | collective-permute-start | bytes 30728 | tf_op jit(solution)/shard_map/ppermute | solution.py:678
  5.5 0.7 %copy-start.2 = (bf16[8,640]{1,0:T(8,128)(2,1)S(1)}, bf16[8,640]{1,0:T(8,128)(2,1)}, u32[]{:S(2)}) copy-start(bf16[8,640]{1,0:T(8,128)(2,1)} %get-tuple-element.48.packed_ref) | copy-start | bytes 30724
  6.2 1.0 %copy-start = (bf16[672,256]{1,0:T(8,128)(2,1)S(1)}, bf16[672,256]{1,0:T(8,128)(2,1)}, u32[]{:S(2)}) copy-start(bf16[672,256]{1,0:T(8,128)(2,1)} %get-tuple-element.49.flat_ref) | copy-start | bytes 1032196
  7.5 3.8 %collective-permute-start.1 = (bf16[2,8,640]{2,1,0:T(8,128)(2,1)S(1)}, bf16[2,8,640]{2,1,0:T(8,128)(2,1)S(1)}, u32[]{:S(2)}, u32[]{:S(2)}) collective-permute-start(bf16[2,8,640]{2,1,0:T(8,128)(2,1)S(1)} %pad_maximum_fusion.2.gathered_ref), channel_id=1, source_target_pairs={{0,4},{2,6},{4,0},{6,2},{8,12},{10,14},{12,8},{14,10},{1,5},{3,7},... | collective-permute-start | bytes 61448 | tf_op jit(solution)/shard_map/ppermute | solution.py:691
  10.3 6.1 %copy-start.1 = (bf16[672,256]{1,0:T(8,128)(2,1)S(1)}, bf16[672,256]{1,0:T(8,128)(2,1)}, u32[]{:S(2)}) copy-start(bf16[672,256]{1,0:T(8,128)(2,1)} %get-tuple-element.49.flat_ref) | copy-start | bytes 1032196
  11.4 5.0 %collective-permute-start.2 = (bf16[4,8,640]{2,1,0:T(8,128)(2,1)S(1)}, bf16[4,8,640]{2,1,0:T(8,128)(2,1)S(1)}, u32[]{:S(2)}, u32[]{:S(2)}) collective-permute-start(bf16[4,8,640]{2,1,0:T(8,128)(2,1)S(1)} %pad_maximum_fusion.1.gathered_ref), channel_id=1, source_target_pairs={{0,8},{2,10},{4,12},{6,14},{8,0},{10,2},{12,4},{14,6},{1,9},{3,11}... | collective-permute-start | bytes 122888 | tf_op jit(solution)/shard_map/ppermute | solution.py:691
  23.3 1.5 %collective-permute-start.3 = (bf16[448,256]{1,0:T(8,128)(2,1)S(1)}, bf16[448,256]{1,0:T(8,128)(2,1)S(1)}, u32[]{:S(2)}, u32[]{:S(2)}) collective-permute-start(bf16[448,256]{1,0:T(8,128)(2,1)S(1)} %get-tuple-element.79.own_ref), channel_id=1, source_target_pairs={{0,1},{1,0},{2,3},{3,2},{4,5},{5,4},{6,7},{7,6},{8,9},{9,8},{10,11... | collective-permute-start | bytes 688136 | tf_op jit(solution)/shard_map/ppermute | solution.py:704
